TPU v7x, 32 devices: a whole 2x2x4 slice. The times are simulated.
32 devices in a mesh: dp: 8 (over z, x), sp: 4 (over y, core).
Axes of the slice: x: 2, y: 2, z: 4, core: 2. Of those that a mesh axis runs over, the one named last changes fastest.
Arguments:
- samples_hi: bfloat16 [8, 90, 180, 768], P('dp', None, 'sp'), may hold values from -6 to 6
- samples_lo: bfloat16 [32, 23, 45, 768], P(('dp', 'sp')), may hold values from -6 to 6
- cotan_hi: bfloat16 [8, 90, 180, 768], P('dp', None, 'sp'), may hold values from -6 to 6
- cotan_lo: bfloat16 [32, 23, 45, 768], P(('dp', 'sp')), may hold values from -6 to 6
- live_slots: int32 [32], P(('dp', 'sp')), may hold values 0 or 1
- spectral_w: float32 [3072, 96], P(('dp', 'sp')), may hold values from -0.4375 to 0.4375
- vectors: float32 [13, 768], P(None, ('dp', 'sp')), may hold values from 0.5 to 1.5
- weight_in: float32 [768, 3072], P(None, ('dp', 'sp')), may hold values from -0.21875 to 0.21875
- weight_out: float32 [3072, 768], P(('dp', 'sp')), may hold values from -0.109375 to 0.109375
- moment_spec: float32 [3072, 96], P(('dp', 'sp')), may hold values from -768 to 768
- moment_in: float32 [768, 3072], P(None, ('dp', 'sp')), may hold values from -768 to 768
- moment_out: float32 [3072, 768], P(('dp', 'sp')), may hold values from -768 to 768
- adam_first: float32 [13, 768], P(None, ('dp', 'sp')), may hold values from -128 to 128
- adam_second: float32 [13, 768], P(None, ('dp', 'sp')), may hold values from 16.272 to 65.088
Outputs:
- block_hi: bfloat16 [8, 90, 180, 768], P('dp', None, 'sp')
- block_lo: bfloat16 [32, 23, 45, 768], P(('dp', 'sp'))
- grad_hi: float32 [8, 90, 180, 768], P('dp', None, 'sp')
- grad_lo: float32 [32, 23, 45, 768], P(('dp', 'sp'))
- new_spectral: float32 [3072, 96], P(('dp', 'sp'))
- new_weight_in: float32 [768, 3072], P(None, ('dp', 'sp'))
- new_weight_out: float32 [3072, 768], P(('dp', 'sp'))
- new_moment_spec: float32 [3072, 96], P(('dp', 'sp'))
- new_moment_in: float32 [768, 3072], P(None, ('dp', 'sp'))
- new_moment_out: float32 [3072, 768], P(('dp', 'sp'))
- new_vectors: float32 [13, 768], P(None, ('dp', 'sp'))
- new_adam_first: float32 [13, 768], P(None, ('dp', 'sp'))
- new_adam_second: float32 [13, 768], P(None, ('dp', 'sp'))
All inputs are finite; a program needn't handle non-finite values. No bound on the sum of `live_slots` on one device may be relied on, other than what follows from the above.
Results may differ from a plain program's by a relative error of at most 0.02.
Values may be sent and summed in bfloat16 or wider, within the bound.
A program may use at most 576 MiB of HBM per device.

v0:
```python
import math

import jax
import jax.numpy as jnp
from jax import lax
from jax.sharding import PartitionSpec as P

D = 768
FF = 3072
NB = 8
BS = 96
H = 90
W = 180
HL = 23
WL = 45
STEP = 10
NEWTON_STEPS = 5


highest = lax.Precision.HIGHEST
epsilon = 1e-06
shrink_level = 0.01
shrink_sharp = 10.0
momentum = 0.95
newton_a = 3.4445
newton_b = -4.775
newton_c = 2.0315
muon_rate = 0.5
adam_rate = 0.3
decay = 0.01
beta_one = 0.9
beta_two = 0.999


def dft_pair(length):
    index = jnp.arange(length, dtype=jnp.int32)
    phase = index[:, None] * index[None, :] % length
    angle = phase.astype(jnp.float32) * (2.0 * math.pi / length)
    factor = 1.0 / math.sqrt(length)
    return (
        (jnp.cos(angle) * factor).astype(jnp.bfloat16),
        (jnp.sin(angle) * factor).astype(jnp.bfloat16),
    )


def contract(form, left, right):
    return jnp.einsum(form, left, right, preferred_element_type=jnp.float32)


def to_freq(cos_rows, sin_rows, values):
    return (
        contract("kw,nhwd->knhd", cos_rows, values),
        -contract("kw,nhwd->knhd", sin_rows, values),
    )


def to_space(cos_cols, sin_cols, real_part, imag_part):
    return contract("kw,knhd->nhwd", cos_cols, real_part) - contract(
        "kw,knhd->nhwd", sin_cols, imag_part
    )


def norm_forward(values, gain, shift):
    center = values - jnp.mean(values, axis=-1, keepdims=True)
    scale = lax.rsqrt(jnp.mean(center * center, axis=-1, keepdims=True) + epsilon)
    normed = center * scale
    return (normed * gain + shift, normed, scale)


def norm_backward(grad_out, normed, scale, gain):
    axes_all = tuple(range(grad_out.ndim - 1))
    grad_gain = jnp.sum(grad_out * normed, axis=axes_all)
    grad_shift = jnp.sum(grad_out, axis=axes_all)
    grad_normed = grad_out * gain
    grad_in = scale * (
        grad_normed
        - jnp.mean(grad_normed, axis=-1, keepdims=True)
        - normed * jnp.mean(grad_normed * normed, axis=-1, keepdims=True)
    )
    return (grad_in, grad_gain, grad_shift)


def gelu_grad(pre_values, grad_out):
    return jax.vjp(jax.nn.gelu, pre_values)[1](grad_out)[0]


def shrink(values):
    return values - shrink_level * jnp.tanh(shrink_sharp * values)


def shrink_grad(values, grad_out):
    bend_tanh = jnp.tanh(shrink_sharp * values)
    return grad_out * (1.0 - shrink_level * shrink_sharp * (1.0 - bend_tanh * bend_tanh))


def block_product(real_in, imag_in, weight_re, weight_im):
    real_out = contract("nbi,bij->nbj", real_in, weight_re) - contract(
        "nbi,bij->nbj", imag_in, weight_im
    )
    imag_out = contract("nbi,bij->nbj", real_in, weight_im) + contract(
        "nbi,bij->nbj", imag_in, weight_re
    )
    return (real_out, imag_out)


def block_back(real_in, imag_in, weight_re, weight_im, grad_re, grad_im):
    input_re = contract("nbj,bij->nbi", grad_re, weight_re) + contract(
        "nbj,bij->nbi", grad_im, weight_im
    )
    input_im = contract("nbj,bij->nbi", grad_im, weight_re) - contract(
        "nbj,bij->nbi", grad_re, weight_im
    )
    weight_g_re = contract("nbi,nbj->bij", real_in, grad_re) + contract(
        "nbi,nbj->bij", imag_in, grad_im
    )
    weight_g_im = contract("nbi,nbj->bij", real_in, grad_im) - contract(
        "nbi,nbj->bij", imag_in, grad_re
    )
    return (input_re, input_im, weight_g_re, weight_g_im)


def column_sum(values):
    return jnp.sum(values.astype(jnp.float32), axis=0)


def filter_forward(area_re, area_im, cos_h, sin_h, weights, biases):
    block_count = weights.shape[2]
    four_re = contract("mh,knhd->knmd", cos_h, area_re) + contract("mh,knhd->knmd", sin_h, area_im)
    four_im = contract("mh,knhd->knmd", cos_h, area_im) - contract("mh,knhd->knmd", sin_h, area_re)
    shape = four_re.shape
    four_re = four_re.astype(jnp.bfloat16).reshape(-1, block_count, BS)
    four_im = four_im.astype(jnp.bfloat16).reshape(-1, block_count, BS)
    first_re, first_im = block_product(four_re, four_im, weights[0, 0], weights[0, 1])
    first_re = first_re + biases[0]
    first_im = first_im + biases[1]
    act_re = jax.nn.gelu(first_re).astype(jnp.bfloat16)
    act_im = jax.nn.gelu(first_im).astype(jnp.bfloat16)
    second_re, second_im = block_product(act_re, act_im, weights[1, 0], weights[1, 1])
    second_re = second_re + biases[2]
    second_im = second_im + biases[3]
    shrunk_re = shrink(second_re).astype(jnp.bfloat16).reshape(shape)
    shrunk_im = shrink(second_im).astype(jnp.bfloat16).reshape(shape)
    back_re = contract("mh,knmd->knhd", cos_h, shrunk_re) - contract(
        "mh,knmd->knhd", sin_h, shrunk_im
    )
    back_im = contract("mh,knmd->knhd", cos_h, shrunk_im) + contract(
        "mh,knmd->knhd", sin_h, shrunk_re
    )
    saved = (four_re, four_im, first_re, first_im, act_re, act_im, second_re, second_im)
    return (back_re.astype(jnp.bfloat16), back_im.astype(jnp.bfloat16), saved)


def filter_backward(grad_re, grad_im, saved, cos_h, sin_h, weights):
    four_re, four_im, first_re, first_im, act_re, act_im, second_re, second_im = saved
    shrunk_g_re = contract("mh,knhd->knmd", cos_h, grad_re) + contract(
        "mh,knhd->knmd", sin_h, grad_im
    )
    shrunk_g_im = contract("mh,knhd->knmd", cos_h, grad_im) - contract(
        "mh,knhd->knmd", sin_h, grad_re
    )
    shape = shrunk_g_re.shape
    second_g_re = shrink_grad(second_re, shrunk_g_re.reshape(second_re.shape)).astype(jnp.bfloat16)
    second_g_im = shrink_grad(second_im, shrunk_g_im.reshape(second_im.shape)).astype(jnp.bfloat16)
    act_g_re, act_g_im, layer_two_re, layer_two_im = block_back(
        act_re, act_im, weights[1, 0], weights[1, 1], second_g_re, second_g_im
    )
    first_g_re = gelu_grad(first_re, act_g_re).astype(jnp.bfloat16)
    first_g_im = gelu_grad(first_im, act_g_im).astype(jnp.bfloat16)
    four_g_re, four_g_im, layer_one_re, layer_one_im = block_back(
        four_re, four_im, weights[0, 0], weights[0, 1], first_g_re, first_g_im
    )
    four_g_re = four_g_re.astype(jnp.bfloat16).reshape(shape)
    four_g_im = four_g_im.astype(jnp.bfloat16).reshape(shape)
    area_g_re = contract("mh,knmd->knhd", cos_h, four_g_re) - contract(
        "mh,knmd->knhd", sin_h, four_g_im
    )
    area_g_im = contract("mh,knmd->knhd", sin_h, four_g_re) + contract(
        "mh,knmd->knhd", cos_h, four_g_im
    )
    grad_weights = jnp.stack(
        [jnp.stack([layer_one_re, layer_one_im]), jnp.stack([layer_two_re, layer_two_im])]
    )
    grad_biases = jnp.stack(
        [
            column_sum(first_g_re),
            column_sum(first_g_im),
            column_sum(second_g_re),
            column_sum(second_g_im),
        ]
    )
    return (
        area_g_re.astype(jnp.bfloat16),
        area_g_im.astype(jnp.bfloat16),
        grad_weights,
        grad_biases,
    )


def body(
    samples_hi,
    samples_lo,
    cotan_hi,
    cotan_lo,
    live_slots,
    spectral_w,
    vectors,
    weight_in,
    weight_out,
    moment_spec,
    moment_in,
    moment_out,
    adam_first,
    adam_second,
):
    spectral_full, vectors_full = (
        lax.all_gather(spectral_w, ("dp", "sp"), axis=0, tiled=True),
        lax.all_gather(vectors, ("dp", "sp"), axis=1, tiled=True),
    )
    weights = spectral_full.astype(jnp.bfloat16).reshape(2, 2, NB, BS, BS)
    gain_one = vectors_full[0]
    shift_one = vectors_full[1]
    gain_two = vectors_full[2]
    shift_two = vectors_full[3]
    bias_out = vectors_full[4]
    bias_hidden = vectors_full[5:9].reshape(FF)
    spec_bias = vectors_full[9:13].reshape(4, NB, BS)
    cos_w, sin_w = dft_pair(W)
    cos_h, sin_h = dft_pair(H)
    cos_wl, sin_wl = dft_pair(WL)
    cos_hl, sin_hl = dft_pair(HL)
    own_width = samples_hi.shape[2]
    own_start = lax.axis_index("sp") * own_width
    cos_rows = lax.dynamic_slice_in_dim(cos_w, own_start, own_width, 0)
    sin_rows = lax.dynamic_slice_in_dim(sin_w, own_start, own_width, 0)
    cos_cols = lax.dynamic_slice_in_dim(cos_w, own_start, own_width, 1)
    sin_cols = lax.dynamic_slice_in_dim(sin_w, own_start, own_width, 1)

    def fold_freq(piece):
        part_re, part_im = to_freq(cos_rows, sin_rows, piece)
        return (part_re, part_im)

    def fold_space(pieces):
        return to_space(cos_cols, sin_cols, pieces[0], pieces[1])

    input_hi = samples_hi.astype(jnp.float32)
    norm_hi, normed_hi, scale_hi = norm_forward(input_hi, gain_one, shift_one)
    low_hi = norm_hi.astype(jnp.bfloat16)
    area_re_hi, area_im_hi = fold_freq(lax.all_gather(low_hi, "sp", axis=2, tiled=True))
    back_re_hi, back_im_hi, saved_hi = filter_forward(
        area_re_hi.astype(jnp.bfloat16),
        area_im_hi.astype(jnp.bfloat16),
        cos_h,
        sin_h,
        weights,
        spec_bias,
    )
    filtered_hi = fold_space(
        (
            lax.all_gather(back_re_hi, "sp", axis=0, tiled=True),
            lax.all_gather(back_im_hi, "sp", axis=0, tiled=True),
        )
    )
    mixed_hi = filtered_hi + norm_hi + input_hi
    input_lo = samples_lo.astype(jnp.float32)
    norm_lo, normed_lo, scale_lo = norm_forward(input_lo, gain_one, shift_one)
    low_lo = norm_lo.astype(jnp.bfloat16)
    area_re_lo, area_im_lo = to_freq(cos_wl, sin_wl, low_lo)
    back_re_lo, back_im_lo, saved_lo = filter_forward(
        area_re_lo.astype(jnp.bfloat16),
        area_im_lo.astype(jnp.bfloat16),
        cos_hl,
        sin_hl,
        weights,
        spec_bias,
    )
    mixed_lo = to_space(cos_wl, sin_wl, back_re_lo, back_im_lo) + norm_lo + input_lo
    weight_in_full, weight_out_full = (
        lax.all_gather(weight_in.astype(jnp.bfloat16), ("dp", "sp"), axis=1, tiled=True),
        lax.all_gather(weight_out.astype(jnp.bfloat16), ("dp", "sp"), axis=0, tiled=True),
    )
    rows_hi = input_hi.size // D
    mixed_rows = jnp.concatenate([mixed_hi.reshape(-1, D), mixed_lo.reshape(-1, D)], axis=0)
    norm_rows, normed_rows, scale_rows = norm_forward(mixed_rows, gain_two, shift_two)
    low_rows = norm_rows.astype(jnp.bfloat16)
    hidden = jnp.dot(low_rows, weight_in_full, preferred_element_type=jnp.float32) + bias_hidden
    active = jax.nn.gelu(hidden).astype(jnp.bfloat16)
    output_rows = (
        mixed_rows
        + (jnp.dot(active, weight_out_full, preferred_element_type=jnp.float32) + bias_out)
    ).astype(jnp.bfloat16)
    block_hi = output_rows[:rows_hi].reshape(samples_hi.shape)
    block_lo = output_rows[rows_hi:].reshape(samples_lo.shape)
    live_mask = live_slots.astype(jnp.bfloat16)[:, None, None, None]
    cotan_rows = jnp.concatenate(
        [cotan_hi.reshape(-1, D), (cotan_lo * live_mask).reshape(-1, D)], axis=0
    )
    grad_weight_out = contract("nf,nd->fd", active, cotan_rows)
    grad_bias_out = column_sum(cotan_rows)
    grad_active = contract("nd,fd->nf", cotan_rows, weight_out_full)
    grad_hidden = gelu_grad(hidden, grad_active).astype(jnp.bfloat16)
    grad_bias_hidden = column_sum(grad_hidden)
    grad_weight_in = contract("nd,nf->df", low_rows, grad_hidden)
    grad_norm_rows = contract("nf,df->nd", grad_hidden, weight_in_full)
    grad_rows_ln, grad_gain_two, grad_shift_two = norm_backward(
        grad_norm_rows, normed_rows, scale_rows, gain_two
    )
    grad_mixed = cotan_rows.astype(jnp.float32) + grad_rows_ln
    grad_mixed_hi = grad_mixed[:rows_hi].reshape(input_hi.shape)
    grad_mixed_lo = grad_mixed[rows_hi:].reshape(input_lo.shape)
    grad_back_re_hi, grad_back_im_hi = fold_freq(
        lax.all_gather(grad_mixed_hi.astype(jnp.bfloat16), "sp", axis=2, tiled=True)
    )
    grad_area_re_hi, grad_area_im_hi, grad_weights_hi, grad_biases_hi = filter_backward(
        grad_back_re_hi.astype(jnp.bfloat16),
        grad_back_im_hi.astype(jnp.bfloat16),
        saved_hi,
        cos_h,
        sin_h,
        weights,
    )
    grad_low_hi = fold_space(
        (
            lax.all_gather(grad_area_re_hi, "sp", axis=0, tiled=True),
            lax.all_gather(grad_area_im_hi, "sp", axis=0, tiled=True),
        )
    )
    grad_in_hi, grad_gain_hi, grad_shift_hi = norm_backward(
        grad_low_hi + grad_mixed_hi, normed_hi, scale_hi, gain_one
    )
    grad_hi = grad_mixed_hi + grad_in_hi
    grad_back_re_lo, grad_back_im_lo = to_freq(cos_wl, sin_wl, grad_mixed_lo.astype(jnp.bfloat16))
    grad_area_re_lo, grad_area_im_lo, grad_weights_lo, grad_biases_lo = filter_backward(
        grad_back_re_lo.astype(jnp.bfloat16),
        grad_back_im_lo.astype(jnp.bfloat16),
        saved_lo,
        cos_hl,
        sin_hl,
        weights,
    )
    grad_low_lo = to_space(cos_wl, sin_wl, grad_area_re_lo, grad_area_im_lo)
    grad_in_lo, grad_gain_lo, grad_shift_lo = norm_backward(
        grad_low_lo + grad_mixed_lo, normed_lo, scale_lo, gain_one
    )
    grad_lo = grad_mixed_lo + grad_in_lo
    grad_spec_rows = (grad_weights_hi + grad_weights_lo).reshape(-1, BS)
    grad_vectors = jnp.concatenate(
        [
            jnp.stack(
                [
                    grad_gain_hi + grad_gain_lo,
                    grad_shift_hi + grad_shift_lo,
                    grad_gain_two,
                    grad_shift_two,
                    grad_bias_out,
                ]
            ),
            grad_bias_hidden.reshape(4, D),
            (grad_biases_hi + grad_biases_lo).reshape(4, D),
        ],
        axis=0,
    )
    red_spec, red_vectors = (
        lax.psum_scatter(grad_spec_rows, ("dp", "sp"), scatter_dimension=0, tiled=True),
        lax.psum_scatter(grad_vectors, ("dp", "sp"), scatter_dimension=1, tiled=True),
    )
    red_in, red_out = (
        lax.psum_scatter(grad_weight_in, ("dp", "sp"), scatter_dimension=1, tiled=True),
        lax.psum_scatter(grad_weight_out, ("dp", "sp"), scatter_dimension=0, tiled=True),
    )
    new_moment_spec = momentum * moment_spec + red_spec
    new_moment_in = momentum * moment_in + red_in
    new_moment_out = momentum * moment_out + red_out
    left_iter = red_in + momentum * new_moment_in
    right_iter = red_out + momentum * new_moment_out
    block_iter = red_spec + momentum * new_moment_spec
    flat_rank = lax.axis_index(("dp", "sp"))
    local_rows = moment_spec.shape[0]
    matrix_id = flat_rank * local_rows // BS
    selector = (jnp.arange(4 * NB, dtype=jnp.int32) == matrix_id).astype(jnp.float32)
    for newton_turn in range(NEWTON_STEPS):
        gram_left = jnp.dot(left_iter, left_iter.T, precision=highest)
        gram_right = jnp.dot(right_iter.T, right_iter, precision=highest)
        gram_block = (
            selector[:, None, None] * jnp.dot(block_iter.T, block_iter, precision=highest)[None]
        )
        gram_left, gram_right, gram_block = lax.psum(
            (gram_left, gram_right, gram_block), ("dp", "sp")
        )
        gram_one = jnp.einsum("m,mij->ij", selector, gram_block, precision=highest)
        if newton_turn == 0:
            size_left = 1.0 / (jnp.sqrt(jnp.trace(gram_left)) + 1e-07)
            size_right = 1.0 / (jnp.sqrt(jnp.trace(gram_right)) + 1e-07)
            size_block = 1.0 / (jnp.sqrt(jnp.trace(gram_one)) + 1e-07)
            left_iter = left_iter * size_left
            right_iter = right_iter * size_right
            block_iter = block_iter * size_block
            gram_left = gram_left * (size_left * size_left)
            gram_right = gram_right * (size_right * size_right)
            gram_one = gram_one * (size_block * size_block)
        once_left = jnp.dot(gram_left, left_iter, precision=highest)
        left_iter = (
            newton_a * left_iter
            + newton_b * once_left
            + newton_c * jnp.dot(gram_left, once_left, precision=highest)
        )
        once_right = jnp.dot(right_iter, gram_right, precision=highest)
        right_iter = (
            newton_a * right_iter
            + newton_b * once_right
            + newton_c * jnp.dot(once_right, gram_right, precision=highest)
        )
        once_block = jnp.dot(block_iter, gram_one, precision=highest)
        block_iter = (
            newton_a * block_iter
            + newton_b * once_block
            + newton_c * jnp.dot(once_block, gram_one, precision=highest)
        )
    keep_share = 1.0 - muon_rate * decay
    new_weight_in = weight_in * keep_share - muon_rate * left_iter
    new_weight_out = weight_out * keep_share - muon_rate * math.sqrt(max(1.0, FF / D)) * right_iter
    new_spectral = spectral_w * keep_share - muon_rate * block_iter
    new_adam_first = beta_one * adam_first + (1.0 - beta_one) * red_vectors
    new_adam_second = beta_two * adam_second + (1.0 - beta_two) * red_vectors * red_vectors
    first_hat = new_adam_first / (1.0 - beta_one**STEP)
    second_hat = new_adam_second / (1.0 - beta_two**STEP)
    new_vectors = vectors * (1.0 - adam_rate * decay) - adam_rate * first_hat / (
        jnp.sqrt(second_hat) + 1e-08
    )
    return (
        block_hi,
        block_lo,
        grad_hi,
        grad_lo,
        new_spectral,
        new_weight_in,
        new_weight_out,
        new_moment_spec,
        new_moment_in,
        new_moment_out,
        new_vectors,
        new_adam_first,
        new_adam_second,
    )


def solution(mesh):
    placed = (
        P("dp", None, "sp", None),
        P(("dp", "sp"), None, None, None),
        P("dp", None, "sp", None),
        P(("dp", "sp"), None, None, None),
        P(("dp", "sp")),
        P(("dp", "sp"), None),
        P(None, ("dp", "sp")),
        P(None, ("dp", "sp")),
        P(("dp", "sp"), None),
        P(("dp", "sp"), None),
        P(None, ("dp", "sp")),
        P(("dp", "sp"), None),
        P(None, ("dp", "sp")),
        P(None, ("dp", "sp")),
    )
    return jax.shard_map(
        body,
        mesh=mesh,
        in_specs=placed,
        out_specs=(
            P("dp", None, "sp", None),
            P(("dp", "sp"), None, None, None),
            P("dp", None, "sp", None),
            P(("dp", "sp"), None, None, None),
            P(("dp", "sp"), None),
            P(None, ("dp", "sp")),
            P(("dp", "sp"), None),
            P(("dp", "sp"), None),
            P(None, ("dp", "sp")),
            P(("dp", "sp"), None),
            P(None, ("dp", "sp")),
            P(None, ("dp", "sp")),
            P(None, ("dp", "sp")),
        ),
        check_vma=False,
    )
```

profile of v0, /device:TPU:0, one launch (start us, length us, event | category | flops | bytes accessed | tf_op | source)
XLA Modules:
  0.0 3055.7 jit_solution(18202026773124337435)
XLA Ops:
  14.6 43.9 %all-gather = f32[32,24,13]{1,2,0:T(8,128)S(1)} all-gather(f32[1,24,13]{1,2,0:T(8,128)S(1)} %bitcast.672), channel_id=1, replica_groups=mesh['dp'=8,'sp'=4] {'dp','sp'}, dimensions={0}, use_global_device_ids=true | all-gather | bytes 41184 | tf_op jit(solution)/shard_map/all_gather | solution.py:217
  70.8 39.4 %all_gather.32 = bf16[3072,96]{1,0:T(8,128)(2,1)S(1)} all-gather(bf16[96,96]{1,0:T(8,128)(2,1)S(1)} %convert), channel_id=1, replica_groups=mesh['dp'=8,'sp'=4] {'dp','sp'}, dimensions={0}, use_global_device_ids=true | all-gather | bytes 608256 | tf_op jit(solution)/shard_map/all_gather | solution.py:216
  112.9 121.0 %all-gather.10.cloned.1.call-done = bf16[1,90,180,768]{3,1,0,2:T(8,128)(2,1)} async-done(((bf16[1,90,45,768]{3,1,0,2:T(8,128)(2,1)}), bf16[1,90,180,768]{3,1,0,2:T(8,128)(2,1)}) %all-gather.10.cloned.1.call-update) | async-done | bytes 24883216 | tf_op jit(solution)/shard_map/all_gather | solution.py:248
  233.9 26.0 fusion.80
  270.8 26.5 negate_convert_fusion.1
  318.2 13.7 reshape.495
  343.2 13.6 fusion.103
  356.7 13.7 reshape.497
  397.6 15.4 fusion.71
  425.6 15.4 fusion.70
  454.5 19.5 reshape.576
  487.2 14.7 fusion.69
  501.9 19.5 reshape.575
  668.5 41.0 %all-gather.14.cloned.1.call-done = bf16[180,1,90,768]{3,2,1,0:T(8,128)(2,1)} async-done(((bf16[45,1,90,768]{3,2,1,0:T(8,128)(2,1)}), bf16[180,1,90,768]{3,2,1,0:T(8,128)(2,1)}) %all-gather.14.cloned.1.call-update) | async-done | bytes 24883216 | tf_op jit(solution)/shard_map/all_gather | solution.py:260
  709.5 23.1 fusion.15
  732.6 140.9 %all-gather.12.cloned.1.call-done = bf16[180,1,90,768]{3,2,1,0:T(8,128)(2,1)} async-done(((bf16[45,1,90,768]{3,2,1,0:T(8,128)(2,1)}), bf16[180,1,90,768]{3,2,1,0:T(8,128)(2,1)}) %all-gather.12.cloned.1.call-update) | async-done | bytes 24883216 | tf_op jit(solution)/shard_map/all_gather | solution.py:259
  873.5 31.1 %convert_add_fusion = f32[1,90,45,768]{3,2,1,0:T(8,128)} fusion(bf16[1,90,45,768]{3,2,1,0:T(8,128)(2,1)} %param.14, f32[90,768,45]{1,2,0:T(8,128)} %fusion.15, bf16[180,1,90,768]{3,2,1,0:T(8,128)(2,1)} %all-gather.12.cloned.1.call-done, f32[768]{0:T(1024)S(1)} %copy-done.115, f32[768]{0:T(1024)S(1)} %copy-done.105, f32[90,45]{1,0:T(8,128)S(1)} %copy-done.92, ...), kind=kOutput, calls=%fused_computation.35 | convolution fusion | flops 1144627200 | bytes 56140804 | tf_op jit(solution)/shard_map/kw,knhd->nhwd/dot_general | solution.py:47
  904.6 13.9 reshape.502
  940.5 51.3 %multiply_convert_fusion = (bf16[5085,3072]{1,0:T(8,128)(2,1)}, f32[5085,3072]{1,0:T(8,128)}) fusion(f32[3072]{0:T(1024)S(1)} %add.733, bf16[768,3072]{0,1:T(8,128)(2,1)} %all-gather.16.cloned.1.call-done, f32[768]{0:T(1024)S(1)} %copy-done.129, f32[768]{0:T(1024)S(1)} %copy-done.123, f32[5085]{0:T(1024)S(1)} %add_rsqrt_fusion.1, ...), kind=kOutput, calls=%fused_computation.10 | convolution fusion | flops 24173690880 | bytes 114125544 | tf_op jit(solution)/shard_map/dot_general | solution.py:285
  991.8 14.5 all-gather.18.cloned.1.call-done
  1006.3 72.3 %convert_reduce_fusion = (f32[3072]{0:T(1024)}, bf16[5085,3072]{1,0:T(8,128)(2,1)}) fusion(f32[5085,3072]{1,0:T(8,128)} %get-tuple-element.161, f32[3072]{0:T(1024)S(1)} %add.733, bf16[3072,768]{1,0:T(8,128)(2,1)} %all-gather.18.cloned.1.call-done, bf16[1035,768]{1,0:T(8,128)(2,1)} %reshape.514, bf16[4050,768]{1,0:T(8,128)(2,1)} %reshape.513), kind=kOutput, calls=%fused_computation.9 | convolution fusion | flops 24368967680 | bytes 106280448 | tf_op jit(solution)/shard_map/nd,fd->nf/dot_general | solution.py:47
  1078.6 42.7 %multiply_reduce_fusion = (f32[768]{0:T(1024)}, f32[5085]{0:T(1024)S(1)}, f32[5085]{0:T(1024)S(1)}, f32[768]{0:T(1024)}, f32[5085,768]{1,0:T(8,128)}) fusion(f32[5085]{0:T(1024)S(1)} %add_rsqrt_fusion.1, f32[5085]{0:T(1024)S(1)} %broadcast_multiply_fusion.11, f32[1035,768]{1,0:T(8,128)S(1)} %reshape.510, f32[4050,768]{1,0:T(8,128)} %reshape.502, ...), kind=kOutput, calls=%fused_computation.51 | convolution fusion | flops 24033079296 | bytes 67293648 | tf_op jit(solution)/shard_map/nf,df->nd/dot_general | solution.py:47
  1121.3 23.5 convert_reduce_fusion.2
  1154.7 14.3 reshape.515
  1215.8 32.7 %fusion.544 = f32[3072,768]{1,0:T(8,128)} fusion(bf16[5085,3072]{1,0:T(8,128)(2,1)} %get-tuple-element.160, bf16[1035,768]{1,0:T(8,128)(2,1)} %reshape.514, bf16[4050,768]{1,0:T(8,128)(2,1)} %reshape.513), kind=kOutput, calls=%fused_computation.661 | convolution fusion | flops 24009662464 | bytes 48489984 | tf_op jit(solution)/shard_map/nf,nd->fd/dot_general | solution.py:47
  1291.5 39.4 %fusion.546 = f32[768,3072]{0,1:T(8,128)} fusion(bf16[5085,3072]{1,0:T(8,128)(2,1)} %get-tuple-element.166, f32[768]{0:T(1024)S(1)} %copy-done.130, f32[768]{0:T(1024)S(1)} %copy-done.123, f32[5085]{0:T(1024)S(1)} %add_rsqrt_fusion.1, f32[5085]{0:T(1024)S(1)} %broadcast_multiply_fusion.11, f32[1035,768]{1,0:T(8,128)S(1)} %reshape.510, ...), kind=kOutput, calls=%fused_computation.663 | convolution fusion | flops 24017471488 | bytes 56347368 | tf_op jit(solution)/shard_map/nd,nf->df/dot_general | solution.py:47
  1346.6 25.9 fusion.83
  1384.1 26.9 negate_convert_fusion
  1434.2 17.3 reshape.517
  1451.5 16.3 copy.616
  1497.6 17.7 reshape.518
  1515.3 16.7 copy.622
  1577.5 18.7 convert_reduce_fusion.5
  1602.6 18.5 convert_reduce_fusion.6
  1652.0 85.9 %reduce-scatter.5.cloned.1.call-done = f32[96,96]{1,0:T(8,128)} async-done(((f32[3072,96]{1,0:T(8,128)}), f32[96,96]{1,0:T(8,128)}) %reduce-scatter.5.cloned.1.call-update) | async-done | bytes 36880 | tf_op jit(solution)/shard_map/reduce_scatter | solution.py:363
  1741.4 158.5 %all-reduce.20.cloned.1.call-done = (f32[32,96,96]{2,1,0:T(8,128)}, f32[768,768]{1,0:T(8,128)}, f32[768,768]{1,0:T(8,128)}) async-done(((f32[32,96,96]{2,1,0:T(8,128)}, f32[768,768]{1,0:T(8,128)}, f32[768,768]{1,0:T(8,128)}), (f32[32,96,96]{2,1,0:T(8,128)}, f32[768,768]{1,0:T(8,128)}, f32[768,768]{1,0:T(8,128)})) %all-reduce.20.cloned.1.call-update) | async-done | bytes 5898256 | tf_op jit(solution)/shard_map/psum | solution.py:386
  1928.1 156.7 %all-reduce.18.cloned.1.call-done = (f32[32,96,96]{2,1,0:T(8,128)}, f32[768,768]{1,0:T(8,128)}, f32[768,768]{1,0:T(8,128)}) async-done(((f32[32,96,96]{2,1,0:T(8,128)}, f32[768,768]{1,0:T(8,128)}, f32[768,768]{1,0:T(8,128)}), (f32[32,96,96]{2,1,0:T(8,128)}, f32[768,768]{1,0:T(8,128)}, f32[768,768]{1,0:T(8,128)})) %all-reduce.18.cloned.1.call-update) | async-done | bytes 5898256 | tf_op jit(solution)/shard_map/psum | solution.py:386
  2106.3 156.7 %all-reduce.16.cloned.1.call-done = (f32[32,96,96]{2,1,0:T(8,128)}, f32[768,768]{1,0:T(8,128)}, f32[768,768]{1,0:T(8,128)}) async-done(((f32[32,96,96]{2,1,0:T(8,128)}, f32[768,768]{1,0:T(8,128)}, f32[768,768]{1,0:T(8,128)}), (f32[32,96,96]{2,1,0:T(8,128)}, f32[768,768]{1,0:T(8,128)}, f32[768,768]{1,0:T(8,128)})) %all-reduce.16.cloned.1.call-update) | async-done | bytes 5898256 | tf_op jit(solution)/shard_map/psum | solution.py:386
  2305.9 19.5 reshape.577
  2338.6 103.3 %all-reduce.14.cloned.1.call-done = (f32[32,96,96]{2,1,0:T(8,128)}, f32[768,768]{1,0:T(8,128)}, f32[768,768]{1,0:T(8,128)}) async-done(((f32[32,96,96]{2,1,0:T(8,128)}, f32[768,768]{1,0:T(8,128)}, f32[768,768]{1,0:T(8,128)}), (f32[32,96,96]{2,1,0:T(8,128)}, f32[768,768]{1,0:T(8,128)}, f32[768,768]{1,0:T(8,128)})) %all-reduce.14.cloned.1.call-update) | async-done | bytes 5898256 | tf_op jit(solution)/shard_map/psum | solution.py:386
  2484.3 19.5 reshape.578
  2544.9 38.1 %add_convert_fusion = bf16[5085,768]{1,0:T(8,128)(2,1)} fusion(bf16[5085,3072]{1,0:T(8,128)(2,1)} %get-tuple-element.160, bf16[3072,768]{1,0:T(8,128)(2,1)} %all-gather.18.cloned.1.call-done, f32[768]{0:T(1024)S(1)} %copy-done.128, f32[1035,768]{1,0:T(8,128)S(1)} %copy-done.10, f32[4050,768]{1,0:T(8,128)} %reshape.502), kind=kOutput, calls=%fused_computation.53 | convolution fusion | flops 24009662464 | bytes 59395584 | tf_op jit(solution)/shard_map/dot_general | solution.py:289
  2668.9 115.4 %all-gather.24.cloned.1.call-done = bf16[180,1,90,768]{3,2,1,0:T(8,128)(2,1)} async-done(((bf16[45,1,90,768]{3,2,1,0:T(8,128)(2,1)}), bf16[180,1,90,768]{3,2,1,0:T(8,128)(2,1)}) %all-gather.24.cloned.1.call-update) | async-done | bytes 24883216 | tf_op jit(solution)/shard_map/all_gather | solution.py:324
  2784.3 23.0 fusion.7
  2807.3 140.9 %all-gather.22.cloned.1.call-done = bf16[180,1,90,768]{3,2,1,0:T(8,128)(2,1)} async-done(((bf16[45,1,90,768]{3,2,1,0:T(8,128)(2,1)}), bf16[180,1,90,768]{3,2,1,0:T(8,128)(2,1)}) %all-gather.22.cloned.1.call-update) | async-done | bytes 24883216 | tf_op jit(solution)/shard_map/all_gather | solution.py:323
  2948.3 30.7 %fusion.44 = (f32[768]{0:T(1024)S(1)}, f32[90,45]{1,0:T(8,128)S(1)}, f32[90,45]{1,0:T(8,128)S(1)}, f32[768]{0:T(1024)S(1)}, f32[1,90,45,768]{3,2,1,0:T(8,128)}) fusion(bf16[1,90,45,768]{3,2,1,0:T(8,128)(2,1)} %param.14, f32[90,45]{1,0:T(8,128)S(1)} %copy-done.93, f32[90,45]{1,0:T(8,128)S(1)} %copy-done.82, f32[768]{0:T(1024)S(1)} %copy-done.106, ...), kind=kOutput, calls=%fused_computation.65 | convolution fusion | flops 1157059072 | bytes 68616848 | tf_op jit(solution)/shard_map/kw,knhd->nhwd/dot_general | solution.py:47
  2979.2 39.9 %all-reduce = f32[13,768]{1,0:T(8,128)S(1)} all-reduce(f32[13,768]{1,0:T(8,128)S(1)} %concatenate.13), channel_id=5, replica_groups=mesh['dp'=8,'sp'=4] {'dp','sp'}, use_global_device_ids=true, to_apply=%region_49.50.clone | all-reduce | flops 9984 | bytes 79872
  3031.1 17.2 copy.669
  (585 shorter events, 850.3 us)
Async XLA Ops:
  7.2 226.7 %all-gather.10.cloned.1.call-start = ((), (), s32[]{:S(2)}) async-start(), calls=%async_computation.3 | async-start | bytes 33177600 | tf_op jit(solution)/shard_map/all_gather | solution.py:248
  12.0 52.4 %copy-start.80 = (f32[90,45]{1,0:T(8,128)}, f32[90,45]{1,0:T(8,128)S(1)}, u32[]{:S(2)}) copy-start(f32[90,45]{1,0:T(8,128)S(1)} %broadcast_multiply_fusion.8) | copy-start | bytes 48604
  14.5 49.9 %copy-start.91 = (f32[90,45]{1,0:T(8,128)}, f32[90,45]{1,0:T(8,128)S(1)}, u32[]{:S(2)}) copy-start(f32[90,45]{1,0:T(8,128)S(1)} %add_rsqrt_fusion) | copy-start | bytes 48604
  69.7 639.8 %all-gather.14.cloned.1.call-start = ((), (), s32[]{:S(2)}) async-start(), calls=%async_computation.5 | async-start | bytes 33177600 | tf_op jit(solution)/shard_map/all_gather | solution.py:260
  112.0 148.0 %copy-start.101 = (bf16[180,180]{1,0:T(8,128)(2,1)}, bf16[180,180]{1,0:T(8,128)(2,1)S(1)}, u32[]{:S(2)}) copy-start(bf16[180,180]{1,0:T(8,128)(2,1)S(1)} %multiply_convert_fusion.8) | copy-start | bytes 194404
  112.7 158.0 %copy-start.96 = (bf16[180,180]{1,0:T(8,128)(2,1)}, bf16[180,180]{1,0:T(8,128)(2,1)S(1)}, u32[]{:S(2)}) copy-start(bf16[180,180]{1,0:T(8,128)(2,1)S(1)} %multiply_convert_fusion.7) | copy-start | bytes 194404
  112.9 284.7 %copy-start.45 = (bf16[1,1,8,96,96]{3,2,1,0,4:T(8,128)(2,1)}, bf16[1,1,8,96,96]{3,2,1,0,4:T(8,128)(2,1)S(1)}, u32[]{:S(2)}) copy-start(bf16[1,1,8,96,96]{3,2,1,0,4:T(8,128)(2,1)S(1)} %get-tuple-element.142) | copy-start | bytes 442372
  112.9 312.7 %copy-start.42 = (bf16[1,1,8,96,96]{3,2,1,0,4:T(8,128)(2,1)}, bf16[1,1,8,96,96]{3,2,1,0,4:T(8,128)(2,1)S(1)}, u32[]{:S(2)}) copy-start(bf16[1,1,8,96,96]{3,2,1,0,4:T(8,128)(2,1)S(1)} %get-tuple-element.143) | copy-start | bytes 442372
  112.9 328.0 %copy-start.25 = (bf16[1,1,8,96,96]{3,2,1,0,4:T(8,128)(2,1)}, bf16[1,1,8,96,96]{3,2,1,0,4:T(8,128)(2,1)S(1)}, u32[]{:S(2)}) copy-start(bf16[1,1,8,96,96]{3,2,1,0,4:T(8,128)(2,1)S(1)} %get-tuple-element.141) | copy-start | bytes 442372
  112.9 374.3 %copy-start.64 = (bf16[1,1,8,96,96]{3,2,1,0,4:T(8,128)(2,1)}, bf16[1,1,8,96,96]{3,2,1,0,4:T(8,128)(2,1)S(1)}, u32[]{:S(2)}) copy-start(bf16[1,1,8,96,96]{3,2,1,0,4:T(8,128)(2,1)S(1)} %get-tuple-element.140) | copy-start | bytes 442372
  370.4 20.8 slice-start
  547.5 326.1 %all-gather.12.cloned.1.call-start = ((), (), s32[]{:S(2)}) async-start(), calls=%async_computation.4 | async-start | bytes 33177600 | tf_op jit(solution)/shard_map/all_gather | solution.py:259
  562.8 377.7 %all-gather.16.cloned.1.call-start = ((), (), s32[]{:S(2)}) async-start(), calls=%async_computation.6 | async-start | bytes 4866048 | tf_op jit(solution)/shard_map/all_gather | solution.py:278
  564.4 441.9 %all-gather.18.cloned.1.call-start = ((), (), s32[]{:S(2)}) async-start(), calls=%async_computation.7 | async-start | bytes 4866048 | tf_op jit(solution)/shard_map/all_gather | solution.py:279
  565.2 781.5 %all-gather.20.cloned.1.call-start = ((), (), s32[]{:S(2)}) async-start(), calls=%async_computation.8 | async-start | bytes 33177600 | tf_op jit(solution)/shard_map/all_gather | solution.py:311
  566.4 84.8 %copy-start.99 = (f32[23,45]{1,0:T(8,128)}, f32[23,45]{1,0:T(8,128)S(1)}, u32[]{:S(2)}) copy-start(f32[23,45]{1,0:T(8,128)S(1)} %broadcast_multiply_fusion.14) | copy-start | bytes 12424
  567.2 84.1 %copy-start.107 = (f32[23,45]{1,0:T(8,128)}, f32[23,45]{1,0:T(8,128)S(1)}, u32[]{:S(2)}) copy-start(f32[23,45]{1,0:T(8,128)S(1)} %add_rsqrt_fusion.2) | copy-start | bytes 12424
  658.1 633.4 %copy-start.9 = (f32[1035,768]{1,0:T(8,128)}, f32[1035,768]{1,0:T(8,128)S(1)}, u32[]{:S(2)}) copy-start(f32[1035,768]{1,0:T(8,128)S(1)} %reshape.510) | copy-start | bytes 9538564
  658.1 51.4 %copy-start.97 = (bf16[180,180]{1,0:T(8,128)(2,1)S(1)}, bf16[180,180]{1,0:T(8,128)(2,1)}, u32[]{:S(2)}) copy-start(bf16[180,180]{1,0:T(8,128)(2,1)} %copy-done.96) | copy-start | bytes 194404
  668.5 205.1 %copy-start.81 = (f32[90,45]{1,0:T(8,128)S(1)}, f32[90,45]{1,0:T(8,128)}, u32[]{:S(2)}) copy-start(f32[90,45]{1,0:T(8,128)} %copy-done.80) | copy-start | bytes 48604
  668.5 205.1 %copy-start.92 = (f32[90,45]{1,0:T(8,128)S(1)}, f32[90,45]{1,0:T(8,128)}, u32[]{:S(2)}) copy-start(f32[90,45]{1,0:T(8,128)} %copy-done.91) | copy-start | bytes 48604
  668.5 205.1 %copy-start.102 = (bf16[180,180]{1,0:T(8,128)(2,1)S(1)}, bf16[180,180]{1,0:T(8,128)(2,1)}, u32[]{:S(2)}) copy-start(bf16[180,180]{1,0:T(8,128)(2,1)} %copy-done.101) | copy-start | bytes 194404
  1078.6 42.7 %copy-start.63 = (bf16[1035,768]{1,0:T(8,128)(2,1)S(1)}, bf16[1035,768]{1,0:T(8,128)(2,1)}, u32[]{:S(2)}) copy-start(bf16[1035,768]{1,0:T(8,128)(2,1)} %reshape.514) | copy-start | bytes 4769284
  1185.3 455.4 %reduce-scatter.9.cloned.1.call-start = ((), (), s32[]{:S(2)}) async-start(), calls=%async_computation.13 | async-start | bytes 9732096 | tf_op jit(solution)/shard_map/reduce_scatter | solution.py:368
  1248.6 393.1 %reduce-scatter.7.cloned.1.call-start = ((), (), s32[]{:S(2)}) async-start(), calls=%async_computation.12 | async-start | bytes 9732096 | tf_op jit(solution)/shard_map/reduce_scatter | solution.py:367
  1331.0 406.9 %reduce-scatter.5.cloned.1.call-start = ((), (), s32[]{:S(2)}) async-start(), calls=%async_computation.11 | async-start | bytes 1622016 | tf_op jit(solution)/shard_map/reduce_scatter | solution.py:363
  1451.5 35.8 %slice-start.2 = ((s8[6635520]{0:T(1024)(128)(4,1)}), s8[2441216]{0:T(1024)(128)(4,1)S(1)}, s32[]{:S(2)}) async-start(s8[6635520]{0:T(1024)(128)(4,1)} %bitcast.652), calls=%async_computation.21 | async-start | bytes 4882432
  1467.8 19.5 slice-start.3
  1515.3 36.9 %slice-start.4 = ((s8[6291456]{0:T(1024)(128)(4,1)}), s8[2097152]{0:T(1024)(128)(4,1)S(1)}, s32[]{:S(2)}) async-start(s8[6291456]{0:T(1024)(128)(4,1)} %bitcast.654), calls=%async_computation.23 | async-start | bytes 4194304
  1532.0 20.2 slice-start.5
  1640.5 97.4 %copy-start.116 = (f32[96,96]{1,0:T(8,128)S(1)}, f32[96,96]{1,0:T(8,128)}, u32[]{:S(2)}) copy-start(f32[96,96]{1,0:T(8,128)} %param.23) | copy-start | bytes 110596
  1640.5 259.4 %all-reduce.20.cloned.1.call-start = ((), (), s32[]{:S(2)}) async-start(), calls=%async_computation.18 | async-start | bytes 12582912 | tf_op jit(solution)/shard_map/psum | solution.py:386
  1641.7 272.4 %copy-start.69 = (f32[96,768]{1,0:T(8,128)}, f32[96,768]{1,0:T(8,128)S(1)}, u32[]{:S(2)}) copy-start(f32[96,768]{1,0:T(8,128)S(1)} %multiply_add_fusion.1) | copy-start | bytes 884740
  1642.8 278.8 %copy-start.70 = (f32[768,96]{0,1:T(8,128)}, f32[768,96]{0,1:T(8,128)S(1)}, u32[]{:S(2)}) copy-start(f32[768,96]{0,1:T(8,128)S(1)} %multiply_add_fusion.3) | copy-start | bytes 884740
  1738.7 172.0 %copy-start.94 = (f32[96,96]{1,0:T(8,128)}, f32[96,96]{1,0:T(8,128)S(1)}, u32[]{:S(2)}) copy-start(f32[96,96]{1,0:T(8,128)S(1)} %multiply_add_fusion.5) | copy-start | bytes 110596
  1741.2 169.3 %copy-start.95 = (f32[96,96]{1,0:T(8,128)S(1)}, f32[96,96]{1,0:T(8,128)}, u32[]{:S(2)}) copy-start(f32[96,96]{1,0:T(8,128)} %reduce-scatter.5.cloned.1.call-done) | copy-start | bytes 110596
  1741.2 171.3 %copy-start.71 = (f32[96,768]{1,0:T(8,128)S(1)}, f32[96,768]{1,0:T(8,128)}, u32[]{:S(2)}) copy-start(f32[96,768]{1,0:T(8,128)} %reduce-scatter.9.cloned.1.call-done) | copy-start | bytes 884740
  1741.2 343.6 %all-reduce.18.cloned.1.call-start = ((), (), s32[]{:S(2)}) async-start(), calls=%async_computation.17 | async-start | bytes 12582912 | tf_op jit(solution)/shard_map/psum | solution.py:386
  1924.1 163.7 %copy-start.86 = (f32[96,96]{1,0:T(8,128)S(1)}, f32[96,96]{1,0:T(8,128)}, u32[]{:S(2)}) copy-start(f32[96,96]{1,0:T(8,128)} %copy-done.85) | copy-start | bytes 110596
  1928.0 335.0 %all-reduce.16.cloned.1.call-start = ((), (), s32[]{:S(2)}) async-start(), calls=%async_computation.16 | async-start | bytes 12582912 | tf_op jit(solution)/shard_map/psum | solution.py:386
  2106.3 335.6 %all-reduce.14.cloned.1.call-start = ((), (), s32[]{:S(2)}) async-start(), calls=%async_computation.15 | async-start | bytes 12582912 | tf_op jit(solution)/shard_map/psum | solution.py:386
  2284.8 368.9 %all-reduce.12.cloned.1.call-start = ((), (), s32[]{:S(2)}) async-start(), calls=%async_computation.14 | async-start | bytes 12582912 | tf_op jit(solution)/shard_map/psum | solution.py:386
  2463.4 320.9 %all-gather.24.cloned.1.call-start = ((), (), s32[]{:S(2)}) async-start(), calls=%async_computation.10 | async-start | bytes 33177600 | tf_op jit(solution)/shard_map/all_gather | solution.py:324
  2530.0 418.3 %all-gather.22.cloned.1.call-start = ((), (), s32[]{:S(2)}) async-start(), calls=%async_computation.9 | async-start | bytes 33177600 | tf_op jit(solution)/shard_map/all_gather | solution.py:323
  2662.0 122.3 %copy-start.98 = (bf16[180,180]{1,0:T(8,128)(2,1)S(1)}, bf16[180,180]{1,0:T(8,128)(2,1)}, u32[]{:S(2)}) copy-start(bf16[180,180]{1,0:T(8,128)(2,1)} %copy-done.96) | copy-start | bytes 194404
  2668.9 279.4 %copy-start.82 = (f32[90,45]{1,0:T(8,128)S(1)}, f32[90,45]{1,0:T(8,128)}, u32[]{:S(2)}) copy-start(f32[90,45]{1,0:T(8,128)} %copy-done.80) | copy-start | bytes 48604
  2668.9 279.4 %copy-start.93 = (f32[90,45]{1,0:T(8,128)S(1)}, f32[90,45]{1,0:T(8,128)}, u32[]{:S(2)}) copy-start(f32[90,45]{1,0:T(8,128)} %copy-done.91) | copy-start | bytes 48604
  2668.9 279.4 %copy-start.103 = (bf16[180,180]{1,0:T(8,128)(2,1)S(1)}, bf16[180,180]{1,0:T(8,128)(2,1)}, u32[]{:S(2)}) copy-start(bf16[180,180]{1,0:T(8,128)(2,1)} %copy-done.101) | copy-start | bytes 194404
  (115 other events, 675.6 us)
Sparse Core Ops, SparseCore 0:
  69.8 164.0 all-gather.9
  547.6 161.8 all-gather.13
  711.1 162.4 all-gather.11
  876.9 63.5 all-gather.15
  943.8 62.4 all-gather.17
  1185.4 161.2 all-gather.19
  1352.5 135.3 reduce-scatter.8
  1495.4 134.7 reduce-scatter.6
  1640.7 97.1 reduce-scatter.4
  1744.4 155.5 all-reduce.19
  1928.2 156.5 all-reduce.17
  2106.4 156.6 all-reduce.15
  2284.9 156.8 all-reduce.13
  2463.5 156.7 all-reduce.11
  2621.8 162.4 all-gather.23
  2785.8 162.4 all-gather.21
where the time goes:
time: 3070 us; the launch traced here: 3060 us
  waiting for transfers between devices  1250 us (41%)
  matrix products  1070 us (35%)
  local copies, waits for them, and re-layouts  460 us (15%)
  other arithmetic  132 us (4%)
  blocking collectives  123 us (4%)
    dot_general x100, matrix products, contract(): return jnp.einsum(form, left, right, preferred_element_type=jnp.float32)  876 us
    psum x5, waiting for transfers between devices, body(): lax.psum((gram_left, gram_right, gram_block), ('dp', 'sp'))  575 us
    another operation x12, local copies, waits for them, and re-layouts  150 us
    all_gather x1, waiting for transfers between devices, body(): lax.all_gather(back_re_hi, 'sp', axis=0, tiled=True)  141 us
    all_gather x1, waiting for transfers between devices, body(): lax.all_gather(grad_area_re_hi, 'sp', axis=0, tiled=True)  141 us
    all_gather x1, waiting for transfers between devices, body(): lax.all_gather(low_hi, 'sp', axis=2, tiled=True)  121 us
    all_gather x1, waiting for transfers between devices, body(): lax.all_gather(grad_area_im_hi, 'sp', axis=0, tiled=True)  115 us
    reduce_scatter x1, waiting for transfers between devices, body(): lax.psum_scatter(grad_spec_rows, ('dp', 'sp'), scatter_dimension=0, tiled...  85.9 us
  transfers between devices with their start and end apart: 16, of which 13 were waited for; matrix products, arithmetic and copies ran while one was open for 32% of the time, Pallas kernels for 0%

commit v1 on v0

v1 whole, which is shorter than its diff:
```python
import functools
import math

import jax
import jax.numpy as jnp
import numpy as np
from jax import lax
from jax.experimental import pallas as pl
from jax.experimental.pallas import tpu as pltpu
from jax.sharding import PartitionSpec as P

D = 768
FF = 3072
NB = 8
BS = 96
H = 90
W = 180
HL = 23
WL = 45
STEP = 10
NEWTON_STEPS = 5

F32 = jnp.float32
BF = jnp.bfloat16
highest = lax.Precision.HIGHEST
epsilon = 1e-06
shrink_level = 0.01
shrink_sharp = 10.0
momentum = 0.95
newton_a = 3.4445
newton_b = -4.775
newton_c = 2.0315
muon_rate = 0.5
adam_rate = 0.3
decay = 0.01
beta_one = 0.9
beta_two = 0.999

K0 = math.sqrt(2.0 / math.pi)
K1 = K0 * 0.044715

SPLIT = 4
GD = D // SPLIT
PAIR = 2 * GD
HALF = H // 2
OWN = W // SPLIT
PW = 48
PM = 96
KF = W // 2 + 1
KP = 96
KG = 7
GROUPS = KF // KG
ROWS = KG * PM
LM = 24
LK = 24
LROWS = LK * LM
HB = 5
LB = 8
FC = 512
NC = FF // FC
VMEM_LIMIT = 60 * 2**20


def wave(length, rows, cols):
    phase = np.outer(rows, cols) % length
    angle = phase * (2.0 * math.pi / length)
    factor = 1.0 / math.sqrt(length)
    return np.cos(angle) * factor, np.sin(angle) * factor


def tables():
    wide = np.zeros((SPLIT, 2 * KP, SPLIT * PW))
    for s in range(SPLIT):
        for j in range(SPLIT):
            cols = (s ^ j) * OWN + np.arange(OWN)
            c, d = wave(W, np.arange(KF), cols)
            wide[s, :KF, j * PW : j * PW + OWN] = c
            wide[s, KP : KP + KF, j * PW : j * PW + OWN] = -d
    tall = np.zeros((2 * PM, 2 * PM))
    for part in range(2):
        c, d = wave(H, np.arange(H), part * HALF + np.arange(HALF))
        re, im = part * PW, PM + part * PW
        tall[:H, re : re + HALF] = c
        tall[:H, im : im + HALF] = d
        tall[PM : PM + H, re : re + HALF] = -d
        tall[PM : PM + H, im : im + HALF] = c
    wide_lo = np.zeros((2 * LK, PW))
    c, d = wave(WL, np.arange(WL // 2 + 1), np.arange(WL))
    wide_lo[: WL // 2 + 1, :WL] = c
    wide_lo[LK : LK + WL // 2 + 1, :WL] = -d
    tall_lo = np.zeros((2 * LM, 2 * LM))
    c, d = wave(HL, np.arange(HL), np.arange(HL))
    tall_lo[:HL, :HL] = c
    tall_lo[:HL, LM : LM + HL] = d
    tall_lo[LM : LM + HL, :HL] = -d
    tall_lo[LM : LM + HL, LM : LM + HL] = c
    return wide, tall, wide_lo, tall_lo


def dot(left, right):
    return jnp.dot(left, right, preferred_element_type=F32)


def dot_nt(left, right):
    return lax.dot_general(left, right, (((1,), (1,)), ((), ())), preferred_element_type=F32)


def dot_tn(left, right):
    return lax.dot_general(left, right, (((0,), (0,)), ((), ())), preferred_element_type=F32)


def normed(values):
    center = values - jnp.mean(values, axis=-1, keepdims=True)
    scale = lax.rsqrt(jnp.mean(center * center, axis=-1, keepdims=True) + epsilon)
    return center * scale, scale


def norm_back(grad, norm, scale, gain):
    pushed = grad * gain
    return scale * (
        pushed
        - jnp.mean(pushed, axis=-1, keepdims=True)
        - norm * jnp.mean(pushed * norm, axis=-1, keepdims=True)
    )


def pad_rows(values):
    return jnp.concatenate(
        [values, jnp.zeros((PW - values.shape[0], values.shape[1]), values.dtype)], axis=0
    )


def lanes(*pieces):
    return jnp.concatenate(pieces, axis=1)


def unpack_pair(fs):
    pieces = [fs[g].astype(F32) for g in range(SPLIT)]
    return (
        lanes(*[p[:, :GD] for p in pieces]),
        lanes(*[p[:, GD:] for p in pieces]),
    )


def pack_pair(row_a, row_b, fs):
    for g in range(SPLIT):
        cut = slice(g * GD, (g + 1) * GD)
        fs[g] = lanes(row_a[:, cut], row_b[:, cut]).astype(BF)


VM = pl.BlockSpec(memory_space=pltpu.VMEM)
SM = pl.BlockSpec(memory_space=pltpu.SMEM)
ANY = pl.BlockSpec(memory_space=pl.ANY)


def params():
    return pltpu.CompilerParams(vmem_limit_bytes=VMEM_LIMIT)


def shape(dims, kind):
    return jax.ShapeDtypeStruct(dims, kind)


PACKED = (HALF, PW, PAIR)
PACKED_BLOCK = pl.BlockSpec((HB, PW, PAIR), lambda i: (i, 0, 0))
WIDE_BLOCK = pl.BlockSpec((2, HB, OWN, D), lambda i: (0, i, 0, 0))


def pack_kernel(own_ref, x_ref, vec_ref, o0, o1, o2, o3, fs):
    own = own_ref[0]
    gain, shift = vec_ref[0:1, :], vec_ref[1:2, :]

    def one(i, _):
        rows = []
        for part in range(2):
            norm, _unused = normed(x_ref[part, i].astype(F32))
            rows.append(pad_rows(norm * gain + shift))
        pack_pair(rows[0], rows[1], fs)
        for j, out in enumerate((o0, o1, o2, o3)):
            out[i] = fs[own ^ j]
        return 0

    lax.fori_loop(0, HB, one, 0)


def norm_packed(own, samples, vectors):
    return pl.pallas_call(
        pack_kernel,
        grid=(HALF // HB,),
        in_specs=[SM, WIDE_BLOCK, VM],
        out_specs=[PACKED_BLOCK] * SPLIT,
        out_shape=[shape(PACKED, BF)] * SPLIT,
        scratch_shapes=[pltpu.VMEM((SPLIT, PW, PAIR), BF)],
        compiler_params=params(),
        name="norm_pack",
    )(own, samples, vectors)


def exchange(slabs):
    moved = [slabs[0]]
    for j in range(1, SPLIT):
        moved.append(lax.ppermute(slabs[j], "sp", [(i, i ^ j) for i in range(SPLIT)]))
    return moved


def to_freq_wide(slabs, table, space):
    def one(i, _):
        rows = jnp.concatenate([slab[i] for slab in slabs], axis=0)
        area = dot(table[...], rows)
        for c in range(3):
            space[c, pl.ds(i, 2 * KP, stride=PW), :] = area[:, c * 128 : (c + 1) * 128]
        return 0

    lax.fori_loop(0, HALF, one, 0)


def to_freq_tall(k, table, space):
    re = lanes(*[space[c, pl.ds(pl.multiple_of(k * PW, PW), PW), :] for c in range(3)])
    im = lanes(*[space[c, pl.ds(pl.multiple_of((KP + k) * PW, PW), PW), :] for c in range(3)])
    rows = jnp.concatenate([re[:, :GD], re[:, GD:], im[:, :GD], im[:, GD:]], axis=0)
    return dot(table[...], rows.astype(BF))


def to_space_tall(k, table, four, space):
    back = dot(table[...], four)
    for part in range(2):
        base = part * PM
        packed = lanes(back[base : base + PW], back[base + PW : base + PM])
        at = pl.ds(pl.multiple_of((part * KP + k) * PW, PW), PW)
        for c in range(3):
            space[c, at, :] = packed[:, c * 128 : (c + 1) * 128]


def to_space_wide(table, space, outs):
    def one(i, _):
        rows = lanes(*[space[c, pl.ds(i, 2 * KP, stride=PW), :] for c in range(3)])
        field = dot(table[...], rows.astype(BF)).astype(BF)
        for j, out in enumerate(outs):
            out[i] = field[j * PW : (j + 1) * PW]
        return 0

    lax.fori_loop(0, HALF, one, 0)


def clear(ref):
    def one(i, _):
        for c in range(ref.shape[0]):
            ref[c, pl.ds(pl.multiple_of(i * 192, 192), 192), :] = jnp.zeros((192, 128), F32)
        return 0

    lax.fori_loop(0, ref.shape[1] // 192, one, 0)


def keep_minus(row, width, first, last):
    at = row + lax.broadcasted_iota(jnp.int32, (width, 1), 0)
    return jnp.where((at >= first) & (at < last), 1.0, 0.0).astype(F32)


def mlp_forward(fre, fim, wu, wv, w1, bias, us, vs, actp, actm, put, base, first, last, chunk):
    rows = us.shape[0]
    us[...] = dot(fre, wu)
    vs[...] = dot(fim, wv)
    b0, b1 = bias[0:1, :], bias[1:2, :]

    def act(i, _):
        at = pl.ds(pl.multiple_of(i * chunk, chunk), chunk)
        u = us[at, :] + b0
        v = vs[at, :]
        for ref, value in ((actp, u + v), (actm, u - v)):
            t = jnp.tanh(value * (K0 + K1 * (value * value)))
            ref[at, :] = (value * (0.5 + 0.5 * t)).astype(BF)
        return 0

    lax.fori_loop(0, rows // chunk, act, 0)
    us[...] = dot(actp[...], w1)
    vs[...] = dot(actm[...], w1)

    def shrunk(i, _):
        at = pl.ds(pl.multiple_of(i * chunk, chunk), chunk)
        p = us[at, :] + b1
        m = vs[at, :] + b1
        p = p - shrink_level * jnp.tanh(shrink_sharp * p)
        m = (m - shrink_level * jnp.tanh(shrink_sharp * m)) * keep_minus(
            base + i * chunk, chunk, first, last
        )
        put(at, (p[:, :GD] + m[:, :GD]).astype(BF), (p[:, GD:] - m[:, GD:]).astype(BF))
        return 0

    lax.fori_loop(0, rows // chunk, shrunk, 0)


def mlp_backward(
    fre, fim, gs, wu, wv, w1, bias, us, vs, actp, actm, dp, dm, gsp, gsm, sums, put,
    gwu, gwv, gw1, ge, base, first, last, chunk,
):
    rows = us.shape[0]
    us[...] = dot(fre, wu)
    vs[...] = dot(fim, wv)
    b0, b1 = bias[0:1, :], bias[1:2, :]
    sign = jnp.where(lax.broadcasted_iota(jnp.int32, (1, PAIR), 1) < GD, 1.0, -1.0).astype(F32)

    def act(i, _):
        at = pl.ds(pl.multiple_of(i * chunk, chunk), chunk)
        u = us[at, :] + b0
        v = vs[at, :]
        for ref, slope, value in ((actp, dp, u + v), (actm, dm, u - v)):
            square = value * value
            hp = 0.5 + 0.5 * jnp.tanh(value * (K0 + K1 * square))
            on = value * hp
            ref[at, :] = on.astype(BF)
            slope[at, :] = hp + on * (1.0 - hp) * (2.0 * K0 + 6.0 * K1 * square)
        return 0

    lax.fori_loop(0, rows // chunk, act, 0)
    us[...] = dot(actp[...], w1)
    vs[...] = dot(actm[...], w1)

    def second(i, total):
        at = pl.ds(pl.multiple_of(i * chunk, chunk), chunk)
        grad = gs[at, :]
        tp = jnp.tanh(shrink_sharp * (us[at, :] + b1))
        tm = jnp.tanh(shrink_sharp * (vs[at, :] + b1))
        flat = 1.0 - shrink_level * shrink_sharp
        bend = shrink_level * shrink_sharp
        p = grad * (flat + bend * (tp * tp))
        m = (grad * (sign * keep_minus(base + i * chunk, chunk, first, last))) * (
            flat + bend * (tm * tm)
        )
        gsp[at, :] = p.astype(BF)
        gsm[at, :] = m.astype(BF)
        return total + jnp.sum(p + m, axis=0, keepdims=True)

    ge[1:2, :] += lax.fori_loop(0, rows // chunk, second, jnp.zeros((1, PAIR), F32))
    us[...] = dot_nt(gsp[...], w1)
    vs[...] = dot_nt(gsm[...], w1)
    gw1[...] += dot_tn(actp[...], gsp[...]) + dot_tn(actm[...], gsm[...])

    def first_grad(i, total):
        at = pl.ds(pl.multiple_of(i * chunk, chunk), chunk)
        p = us[at, :] * dp[at, :]
        m = vs[at, :] * dm[at, :]
        both = p + m
        gsp[at, :] = both.astype(BF)
        gsm[at, :] = (p - m).astype(BF)
        return total + jnp.sum(both, axis=0, keepdims=True)

    ge[0:1, :] += lax.fori_loop(0, rows // chunk, first_grad, jnp.zeros((1, PAIR), F32))
    gwu[...] += dot_tn(fre, gsp[...])
    gwv[...] += dot_tn(fim, gsm[...])
    put(dot_nt(gsp[...], wu).astype(BF), dot_nt(gsm[...], wv).astype(BF))


def block_grads(gwu, gwv, gw1):
    cells = {}
    for b in range(2):
        r = slice(b * BS, (b + 1) * BS)
        i = slice(GD + b * BS, GD + (b + 1) * BS)
        cells[0, 0, b] = gwu[r, r] + gwv[r, i]
        cells[0, 1, b] = gwu[r, i] - gwv[r, r]
        cells[1, 0, b] = gw1[r, r] + gw1[i, i]
        cells[1, 1, b] = gw1[r, i] - gw1[i, r]
    return cells


def filter_kernel(
    x0, x1, x2, x3, tw, twt, th, tht, wu, wv, w1, bias,
    y0, y1, y2, y3, four, space, us, vs, actp, actm, zr, zi,
):
    clear(space)
    to_freq_wide((x0, x1, x2, x3), tw, space)

    def group(g, _):
        for n in range(KG):
            rows = to_freq_tall(g * KG + n, th, space).astype(BF)
            four[g, 0, n * PM : (n + 1) * PM, :] = rows[:PM]
            four[g, 1, n * PM : (n + 1) * PM, :] = rows[PM:]

        def put(at, re, im):
            zr[at, :] = re
            zi[at, :] = im

        mlp_forward(
            four[g, 0], four[g, 1], wu[...], wv[...], w1[...], bias, us, vs, actp, actm, put,
            g * ROWS, PM, (KF - 1) * PM, PM // 2,
        )
        for n in range(KG):
            at = slice(n * PM, (n + 1) * PM)
            to_space_tall(
                g * KG + n, tht, jnp.concatenate([zr[at, :], zi[at, :]], axis=0), space
            )
        return 0

    lax.fori_loop(0, GROUPS, group, 0)
    to_space_wide(twt, space, (y0, y1, y2, y3))


def filter_scratch(rows, wide):
    big = pltpu.VMEM((rows, PAIR), F32)
    low = pltpu.VMEM((rows, PAIR), BF)
    part = pltpu.VMEM((rows, GD), BF)
    return big, low, part


def filter_forward(slabs, tabs, weights, bias):
    big, low, part = filter_scratch(ROWS, None)
    outs = pl.pallas_call(
        filter_kernel,
        in_specs=[VM] * 12,
        out_specs=[VM] * 5,
        out_shape=[shape(PACKED, BF)] * SPLIT + [shape((GROUPS, 2, ROWS, GD), BF)],
        scratch_shapes=[pltpu.VMEM((3, 2 * KP * PW, 128), F32), big, big, low, low, part, part],
        compiler_params=params(),
        name="filter_forward",
    )(*slabs, *tabs, *weights, bias)
    return outs[:SPLIT], outs[SPLIT]


def filter_back_kernel(
    own_ref, x0, x1, x2, x3, four, tw, twt, th, tht, wu, wv, w1, bias, grads_in,
    y0, y1, y2, y3, grads, ge,
    space, us, vs, actp, actm, zr, zi, gs, dp, dm, gsp, gsm, gwu, gwv, gw1,
):
    clear(space)
    gwu[...] = jnp.zeros_like(gwu)
    gwv[...] = jnp.zeros_like(gwv)
    gw1[...] = jnp.zeros_like(gw1)
    ge[...] = jnp.zeros_like(ge)
    to_freq_wide((x0, x1, x2, x3), tw, space)

    def group(g, _):
        for n in range(KG):
            rows = to_freq_tall(g * KG + n, th, space)
            gs[n * PM : (n + 1) * PM, :] = lanes(rows[:PM], rows[PM:])

        def put(re, im):
            zr[...] = re
            zi[...] = im

        mlp_backward(
            four[g, 0], four[g, 1], gs, wu[...], wv[...], w1[...], bias, us, vs, actp, actm, dp, dm,
            gsp, gsm, None, put, gwu, gwv, gw1, ge, g * ROWS, PM, (KF - 1) * PM, PM // 2,
        )
        for n in range(KG):
            at = slice(n * PM, (n + 1) * PM)
            to_space_tall(
                g * KG + n, tht, jnp.concatenate([zr[at, :], zi[at, :]], axis=0), space
            )
        return 0

    lax.fori_loop(0, GROUPS, group, 0)
    grads[...] = grads_in[...]
    own = own_ref[0]
    for (layer, part, b), value in block_grads(gwu, gwv, gw1).items():
        grads[(2 * layer + part) * NB + 2 * own + b] += value
    to_space_wide(twt, space, (y0, y1, y2, y3))


def filter_backward(own, slabs, four, tabs, weights, bias, grads_in):
    big, low, part = filter_scratch(ROWS, None)
    outs = pl.pallas_call(
        filter_back_kernel,
        in_specs=[SM] + [VM] * 14,
        out_specs=[VM] * 6,
        out_shape=[shape(PACKED, BF)] * SPLIT
        + [shape((4 * NB, BS, BS), F32), shape((2, PAIR), F32)],
        scratch_shapes=[pltpu.VMEM((3, 2 * KP * PW, 128), F32), big, big, low, low, part, part]
        + [big, big, big, low, low]
        + [pltpu.VMEM((GD, PAIR), F32)] * 2
        + [pltpu.VMEM((PAIR, PAIR), F32)],
        compiler_params=params(),
        name="filter_backward",
    )(own, *slabs, four, *tabs, *weights, bias, grads_in)
    return outs[:SPLIT], outs[SPLIT], outs[SPLIT + 1]


def lo_freq_wide(i, rows, table, space):
    area = dot(table[...], rows)
    for c in range(6):
        space[c, pl.ds(i, 2 * LK, stride=LM), :] = area[:, c * 128 : (c + 1) * 128]


def lo_freq_tall(k, table, space):
    pair = []
    for n in range(2):
        parts = []
        for base in (0, LK):
            at = pl.ds(pl.multiple_of((base + 2 * k + n) * LM, LM), LM)
            parts.append(lanes(*[space[c, at, :] for c in range(6)]))
        pair.append(dot(table[...], jnp.concatenate(parts, axis=0).astype(BF)))
    re = jnp.concatenate([p[:LM] for p in pair], axis=0)
    im = jnp.concatenate([p[LM:] for p in pair], axis=0)
    return re, im


def lo_space_tall(k, table, re, im, space):
    for n in range(2):
        cut = slice(n * LM, (n + 1) * LM)
        rows = jnp.concatenate([re[cut], im[cut]], axis=0).astype(BF)
        back = dot(table[...], rows)
        for part, base in enumerate((0, LK)):
            at = pl.ds(pl.multiple_of((base + 2 * k + n) * LM, LM), LM)
            for c in range(6):
                space[c, at, :] = back[part * LM : (part + 1) * LM, c * 128 : (c + 1) * 128]


def lo_space_wide(i, table, space):
    rows = lanes(*[space[c, pl.ds(i, 2 * LK, stride=LM), :] for c in range(6)])
    return dot(table[...], rows.astype(BF))


def filter_lo_kernel(
    x_ref, vec_ref, tw, twt, th, tht, wu, wv, w1, bias, y_ref, four,
    space, us, vs, actp, actm, zr, zi,
):
    clear(space)
    gain, shift = vec_ref[0:1, :], vec_ref[1:2, :]

    def wide(i, _):
        norm, _unused = normed(x_ref[i].astype(F32))
        lo_freq_wide(i, pad_rows(norm * gain + shift).astype(BF), tw, space)
        return 0

    lax.fori_loop(0, HL, wide, 0)

    def tall(k, _):
        re, im = lo_freq_tall(k, th, space)
        at = pl.ds(pl.multiple_of(k * PW, PW), PW)
        for g in range(SPLIT):
            cut = slice(g * GD, (g + 1) * GD)
            four[g, 0, at, :] = re[:, cut].astype(BF)
            four[g, 1, at, :] = im[:, cut].astype(BF)
        return 0

    lax.fori_loop(0, LK // 2, tall, 0)

    def group(g, _):
        def put(at, re, im):
            zr[g, at, :] = re
            zi[g, at, :] = im

        mlp_forward(
            four[g, 0], four[g, 1], wu[g], wv[g], w1[g], bias.at[g], us, vs, actp, actm, put,
            0, LM, LROWS, PW,
        )
        return 0

    lax.fori_loop(0, SPLIT, group, 0)

    def back(k, _):
        at = pl.ds(pl.multiple_of(k * PW, PW), PW)
        re = lanes(*[zr[g, at, :].astype(F32) for g in range(SPLIT)])
        im = lanes(*[zi[g, at, :].astype(F32) for g in range(SPLIT)])
        lo_space_tall(k, tht, re, im, space)
        return 0

    lax.fori_loop(0, LK // 2, back, 0)

    def last(i, _):
        y_ref[i] = lo_space_wide(i, twt, space).astype(BF)
        return 0

    lax.fori_loop(0, HL, last, 0)
    y_ref[HL] = jnp.zeros((PW, D), BF)


def lo_scratch():
    big, low, _ = filter_scratch(LROWS, None)
    part = pltpu.VMEM((SPLIT, LROWS, GD), BF)
    return [pltpu.VMEM((6, 2 * LK * LM, 128), F32), big, big, low, low, part, part]


def filter_forward_lo(samples, vectors, tabs, weights, bias):
    return pl.pallas_call(
        filter_lo_kernel,
        in_specs=[VM] * 10,
        out_specs=[VM] * 2,
        out_shape=[shape((LM, PW, D), BF), shape((SPLIT, 2, LROWS, GD), BF)],
        scratch_shapes=lo_scratch(),
        compiler_params=params(),
        name="filter_forward_lo",
    )(samples, vectors, *tabs, *weights, bias)


def filter_back_lo_kernel(
    x_ref, gm_ref, four, vec_ref, tw, twt, th, tht, wu, wv, w1, bias,
    grad_ref, grads, ge, gvec,
    space, us, vs, actp, actm, zr, zi, gs, dp, dm, gsp, gsm, gwu, gwv, gw1,
):
    clear(space)
    ge[...] = jnp.zeros_like(ge)
    gvec[...] = jnp.zeros_like(gvec)

    def wide(i, _):
        lo_freq_wide(i, gm_ref[i], tw, space)
        return 0

    lax.fori_loop(0, HL, wide, 0)

    def tall(k, _):
        re, im = lo_freq_tall(k, th, space)
        at = pl.ds(pl.multiple_of(k * PW, PW), PW)
        for g in range(SPLIT):
            cut = slice(g * GD, (g + 1) * GD)
            gs[g, at, :] = lanes(re[:, cut], im[:, cut])
        return 0

    lax.fori_loop(0, LK // 2, tall, 0)

    def group(g, _):
        gwu[...] = jnp.zeros_like(gwu)
        gwv[...] = jnp.zeros_like(gwv)
        gw1[...] = jnp.zeros_like(gw1)

        def put(re, im):
            zr[g] = re
            zi[g] = im

        mlp_backward(
            four[g, 0], four[g, 1], gs.at[g], wu[g], wv[g], w1[g], bias.at[g], us, vs, actp, actm,
            dp, dm, gsp, gsm, None, put, gwu, gwv, gw1, ge.at[g], 0, LM, LROWS, PW,
        )
        for (layer, part, b), value in block_grads(gwu, gwv, gw1).items():
            grads[(2 * layer + part) * NB + 2 * g + b] = value
        return 0

    lax.fori_loop(0, SPLIT, group, 0)

    def back(k, _):
        at = pl.ds(pl.multiple_of(k * PW, PW), PW)
        re = lanes(*[zr[g, at, :].astype(F32) for g in range(SPLIT)])
        im = lanes(*[zi[g, at, :].astype(F32) for g in range(SPLIT)])
        lo_space_tall(k, tht, re, im, space)
        return 0

    lax.fori_loop(0, LK // 2, back, 0)
    gain = vec_ref[0:1, :]

    def last(i, _):
        field = lo_space_wide(i, twt, space)[:WL]
        direct = gm_ref[i].astype(F32)[:WL]
        norm, scale = normed(x_ref[i].astype(F32))
        grad = field + direct
        gvec[0:1, :] += jnp.sum(grad * norm, axis=0, keepdims=True)
        gvec[1:2, :] += jnp.sum(grad, axis=0, keepdims=True)
        grad_ref[i] = direct + norm_back(grad, norm, scale, gain)
        return 0

    lax.fori_loop(0, HL, last, 0)


def filter_backward_lo(samples, grad_mixed, four, vectors, tabs, weights, bias):
    big, low, _ = filter_scratch(LROWS, None)
    return pl.pallas_call(
        filter_back_lo_kernel,
        in_specs=[VM] * 12,
        out_specs=[VM] * 4,
        out_shape=[
            shape((HL, WL, D), F32),
            shape((4 * NB, BS, BS), F32),
            shape((SPLIT, 2, PAIR), F32),
            shape((2, D), F32),
        ],
        scratch_shapes=lo_scratch()
        + [pltpu.VMEM((SPLIT, LROWS, PAIR), F32), big, big, low, low]
        + [pltpu.VMEM((GD, PAIR), F32)] * 2
        + [pltpu.VMEM((PAIR, PAIR), F32)],
        compiler_params=params(),
        name="filter_backward_lo",
    )(samples, grad_mixed, four, vectors, *tabs, *weights, bias)


def feed_chunks(n2, cots, c1_ref, win, wout, out_acc, gn_acc, gwi, gwo, gc1):
    out_acc[...] = jnp.zeros_like(out_acc)
    gn_acc[...] = jnp.zeros_like(gn_acc)

    def chunk(c, _):
        rows = pl.ds(pl.multiple_of(c * FC, FC), FC)
        low, cot = n2[...], cots[...]
        wi, wo = win[rows, :], wout[rows, :]
        hidden = dot_nt(low, wi) + c1_ref[pl.ds(c, 1), :]
        grad = dot_nt(cot, wo)
        square = hidden * hidden
        hp = 0.5 + 0.5 * jnp.tanh(hidden * (K0 + K1 * square))
        act = hidden * hp
        grad = grad * (hp + act * (1.0 - hp) * (2.0 * K0 + 6.0 * K1 * square))
        gc1[pl.ds(c, 1), :] += jnp.sum(grad, axis=0, keepdims=True)
        act = act.astype(BF)
        grad = grad.astype(BF)
        out_acc[...] += dot(act, wo)
        gn_acc[...] += dot(grad, wi)
        gwo[rows, :] += dot_tn(act, cot)
        gwi[rows, :] += dot_tn(grad, low)
        return 0

    lax.fori_loop(0, NC, chunk, 0)


def feed_kernel(high, own_ref, live_ref, *refs):
    count = SPLIT if high else 1
    x_ref, cot_ref = refs[:2]
    fields = refs[2 : 2 + count]
    rest = refs[2 + count :]
    vec_ref, c1_ref, win, wout = rest[:4]
    rest = rest[4:]
    if high:
        gwi0, gwo0, gc1_in, gv_in = rest[:4]
        rest = rest[4:]
    block_ref = rest[0]
    packs = rest[1 : 1 + count]
    gwi_out, gwo_out, gc1, gv, gwi, gwo, sem, mixed, n2, cots, out_acc, gn_acc, fs = rest[1 + count :]
    step = pl.program_id(0)

    @pl.when(step == 0)
    def _():
        if high:
            loads = [
                pltpu.make_async_copy(gwi0, gwi, sem.at[0]),
                pltpu.make_async_copy(gwo0, gwo, sem.at[1]),
            ]
            for load in loads:
                load.start()
            for load in loads:
                load.wait()
            gc1[...] = gc1_in[...]
            gv[...] = gv_in[...]
        else:
            gwi[...] = jnp.zeros_like(gwi)
            gwo[...] = jnp.zeros_like(gwo)
            gc1[...] = jnp.zeros_like(gc1)
            gv[...] = jnp.zeros_like(gv)

    own = own_ref[0]
    gain_one, shift_one = vec_ref[0:1, :], vec_ref[1:2, :]
    gain_two, shift_two = vec_ref[2:3, :], vec_ref[3:4, :]
    bias_out = vec_ref[4:5, :]

    def enter(plane, x, cot, field):
        at = pl.ds(pl.multiple_of(plane * PW, PW), PW)
        norm, _unused = normed(x)
        total = field + (norm * gain_one + shift_one) + x
        mixed[at, :] = total
        norm, _unused = normed(total)
        n2[at, :] = (norm * gain_two + shift_two).astype(BF)
        cots[at, :] = cot.astype(BF)

    def leave(plane):
        at = pl.ds(pl.multiple_of(plane * PW, PW), PW)
        total = mixed[at, :]
        out = total + (out_acc[at, :] + bias_out)
        norm, scale = normed(total)
        grad = gn_acc[at, :]
        cot = cots[at, :].astype(F32)
        gv[0:1, :] += jnp.sum(grad * norm, axis=0, keepdims=True)
        gv[1:2, :] += jnp.sum(grad, axis=0, keepdims=True)
        gv[2:3, :] += jnp.sum(cot, axis=0, keepdims=True)
        return out.astype(BF), cot + norm_back(grad, norm, scale, gain_two)

    if high:

        def before(i, _):
            for j in range(SPLIT):
                fs[own ^ j] = fields[j][i]
            for part, field in enumerate(unpack_pair(fs)):
                x = pad_rows(x_ref[part, i].astype(F32))
                cot = pad_rows(cot_ref[part, i].astype(F32))
                enter(part * HB + i, x, cot, field)
            return 0

        def after(i, _):
            grads = []
            for part in range(2):
                out, grad = leave(part * HB + i)
                block_ref[part, i] = out[:OWN]
                grads.append(grad)
            pack_pair(grads[0], grads[1], fs)
            for j in range(SPLIT):
                packs[j][i] = fs[own ^ j]
            return 0

        trips = HB
    else:
        live = live_ref[0].astype(F32)

        def before(i, _):
            here = (step * LB + i) < HL
            x = jnp.where(here, pad_rows(x_ref[i].astype(F32)), 0.0)
            cot = jnp.where(here, pad_rows(cot_ref[i].astype(F32)), 0.0) * live
            enter(i, x, cot, fields[0][i].astype(F32))
            return 0

        def after(i, _):
            out, grad = leave(i)
            block_ref[i] = out[:WL]
            packs[0][i] = grad.astype(BF)
            return 0

        trips = LB

    lax.fori_loop(0, trips, before, 0)
    feed_chunks(n2, cots, c1_ref, win, wout, out_acc, gn_acc, gwi, gwo, gc1)
    lax.fori_loop(0, trips, after, 0)

    @pl.when(step == pl.num_programs(0) - 1)
    def _():
        stores = [
            pltpu.make_async_copy(gwi, gwi_out, sem.at[0]),
            pltpu.make_async_copy(gwo, gwo_out, sem.at[1]),
        ]
        for store in stores:
            store.start()
        for store in stores:
            store.wait()


def feed(high, own, live, samples, cotan, fields, vectors, bias_hidden, win, wout, earlier):
    tokens = (2 * HB if high else LB) * PW
    if high:
        steps = HALF // HB
        wide, packed, packed_shape = WIDE_BLOCK, PACKED_BLOCK, PACKED
    else:
        steps = LM // LB
        wide = pl.BlockSpec((LB, WL, D), lambda i: (i, 0, 0))
        packed = pl.BlockSpec((LB, PW, D), lambda i: (i, 0, 0))
        packed_shape = (LM, PW, D)
    count = len(fields)
    return pl.pallas_call(
        functools.partial(feed_kernel, high),
        grid=(steps,),
        in_specs=[SM, SM, wide, wide]
        + [packed] * count
        + [VM] * 4
        + ([ANY, ANY, VM, VM] if high else []),
        out_specs=[wide] + [packed] * count + [ANY, ANY, VM, VM],
        out_shape=[shape(samples.shape, BF)]
        + [shape(packed_shape, BF)] * count
        + [shape((FF, D), F32)] * 2
        + [shape((NC, FC), F32), shape((8, D), F32)],
        scratch_shapes=[pltpu.VMEM((FF, D), F32)] * 2
        + [
            pltpu.SemaphoreType.DMA((2,)),
            pltpu.VMEM((tokens, D), F32),
            pltpu.VMEM((tokens, D), BF),
            pltpu.VMEM((tokens, D), BF),
            pltpu.VMEM((tokens, D), F32),
            pltpu.VMEM((tokens, D), F32),
            pltpu.VMEM((SPLIT, PW, PAIR), BF),
        ],
        compiler_params=params(),
        name="feed_hi" if high else "feed_lo",
    )(own, live, samples, cotan, *fields, vectors, bias_hidden, win, wout, *earlier)


def norm_back_kernel(own_ref, x_ref, m0, m1, m2, m3, f0, f1, f2, f3, vec_ref, grad_ref, gvec, fs, ms):
    @pl.when(pl.program_id(0) == 0)
    def _():
        gvec[...] = jnp.zeros_like(gvec)

    own = own_ref[0]
    gain = vec_ref[0:1, :]

    def one(i, _):
        for j, (m, f) in enumerate(((m0, f0), (m1, f1), (m2, f2), (m3, f3))):
            ms[own ^ j] = m[i]
            fs[own ^ j] = f[i]
        for part, (direct, field) in enumerate(zip(unpack_pair(ms), unpack_pair(fs))):
            direct, field = direct[:OWN], field[:OWN]
            norm, scale = normed(x_ref[part, i].astype(F32))
            grad = field + direct
            gvec[0:1, :] += jnp.sum(grad * norm, axis=0, keepdims=True)
            gvec[1:2, :] += jnp.sum(grad, axis=0, keepdims=True)
            grad_ref[part, i] = direct + norm_back(grad, norm, scale, gain)
        return 0

    lax.fori_loop(0, HB, one, 0)


def norm_backward(own, samples, direct, fields, vectors):
    return pl.pallas_call(
        norm_back_kernel,
        grid=(HALF // HB,),
        in_specs=[SM, WIDE_BLOCK] + [PACKED_BLOCK] * (2 * SPLIT) + [VM],
        out_specs=[WIDE_BLOCK, VM],
        out_shape=[shape(samples.shape, F32), shape((2, D), F32)],
        scratch_shapes=[pltpu.VMEM((SPLIT, PW, PAIR), BF)] * 2,
        compiler_params=params(),
        name="norm_backward",
    )(own, samples, *direct, *fields, vectors)


def newton_poly(gram, square):
    size = gram.shape[0]
    eye = lax.broadcasted_iota(jnp.int32, (size, size), 0) == lax.broadcasted_iota(
        jnp.int32, (size, size), 1
    )
    return jnp.where(eye, newton_a, 0.0) + newton_b * gram + newton_c * square


def mul(left, right):
    return jnp.dot(left, right, precision=highest, preferred_element_type=F32)


def newton_kernel(g_in, g_out, x_in, x_out, y_in, y_out, gram, poly):
    for g_ref, x_ref, y_ref in ((g_in, x_in, y_in), (g_out, x_out, y_out)):
        size = g_ref.shape[0]
        eye = lax.broadcasted_iota(jnp.int32, (size, size), 0) == lax.broadcasted_iota(
            jnp.int32, (size, size), 1
        )
        trace = jnp.sum(jnp.where(eye, g_ref[...], 0.0), keepdims=True)
        scale = 1.0 / (jnp.sqrt(trace) + 1e-07)
        gram[...] = g_ref[...] * (scale * scale)
        y_ref[...] = x_ref[...] * scale
        for turn in range(NEWTON_STEPS):
            now = y_ref[...]
            if turn < NEWTON_STEPS - 1:
                poly[...] = newton_poly(gram[...], mul(gram[...], gram[...]))
                y_ref[...] = mul(now, poly[...])
                gram[...] = mul(poly[...], gram[...])
                gram[...] = mul(gram[...], poly[...])
            else:
                once = mul(now, gram[...])
                y_ref[...] = (
                    newton_a * now + newton_b * once + newton_c * mul(once, gram[...])
                )


def newton_pair(gram_in, gram_out, x_in, x_out):
    return pl.pallas_call(
        newton_kernel,
        in_specs=[VM] * 4,
        out_specs=[VM] * 2,
        out_shape=[shape(x_in.shape, F32), shape(x_out.shape, F32)],
        scratch_shapes=[pltpu.VMEM((D, D), F32)] * 2,
        compiler_params=params(),
        name="newton",
    )(gram_in, gram_out, x_in, x_out)


def newton_small_kernel(x_ref, y_ref):
    values = x_ref[...]
    size = 1.0 / (jnp.sqrt(jnp.sum(values * values, keepdims=True)) + 1e-07)
    values = values * size
    for _ in range(NEWTON_STEPS):
        gram = lax.dot_general(
            values, values, (((0,), (0,)), ((), ())), precision=highest, preferred_element_type=F32
        )
        once = mul(values, gram)
        values = newton_a * values + newton_b * once + newton_c * mul(once, gram)
    y_ref[...] = values


def newton_small(values):
    return pl.pallas_call(
        newton_small_kernel,
        in_specs=[VM],
        out_specs=VM,
        out_shape=shape(values.shape, F32),
        name="newton_small",
    )(values)


def spread(blocks):
    pairs = blocks.reshape(SPLIT, 2, BS, 1, BS)
    eye = jnp.eye(2, dtype=blocks.dtype).reshape(1, 2, 1, 2, 1)
    return (pairs * eye).reshape(SPLIT, GD, GD)


def spectral_matrices(spectral):
    low = spectral.astype(BF).reshape(2, 2, NB, BS, BS)
    re0, im0, re1, im1 = (spread(low[layer, part]) for layer in range(2) for part in range(2))
    wu = jnp.concatenate([re0, im0], axis=2)
    wv = jnp.concatenate([-im0, re0], axis=2)
    w1 = jnp.concatenate(
        [jnp.concatenate([re1, im1], axis=2), jnp.concatenate([-im1, re1], axis=2)], axis=1
    )
    return wu, wv, w1


def body(
    samples_hi, samples_lo, cotan_hi, cotan_lo, live_slots, spectral_w, vectors, weight_in,
    weight_out, moment_spec, moment_in, moment_out, adam_first, adam_second,
):
    axes = ("dp", "sp")
    sp = lax.axis_index("sp")
    own = sp.astype(jnp.int32).reshape(1)
    wide, tall, wide_lo, tall_lo = (jnp.asarray(t, BF) for t in tables())
    wide = lax.dynamic_index_in_dim(wide, sp, 0, keepdims=False)
    tabs = (wide, wide.T, tall, tall.T)
    tabs_lo = (wide_lo, wide_lo.T, tall_lo, tall_lo.T)

    vectors_full = lax.all_gather(vectors, axes, axis=1, tiled=True)
    spectral_full = lax.all_gather(spectral_w.astype(BF), axes, axis=0, tiled=True)
    win = lax.all_gather(weight_in.T.astype(BF), axes, axis=0, tiled=True)
    wout = lax.all_gather(weight_out.astype(BF), axes, axis=0, tiled=True)

    split_hi = samples_hi.reshape(2, HALF, OWN, D)
    split_cot = cotan_hi.reshape(2, HALF, OWN, D)
    one_lo = samples_lo.reshape(HL, WL, D)
    one_cot = cotan_lo.reshape(HL, WL, D)

    slabs = exchange(norm_packed(own, split_hi, vectors_full))
    weights_lo = spectral_matrices(spectral_full)
    weights = tuple(lax.dynamic_index_in_dim(w, sp, 0, keepdims=False) for w in weights_lo)
    e = vectors_full[9:13].reshape(2, 2, SPLIT, GD)
    bias_lo = jnp.transpose(e, (2, 0, 1, 3)).reshape(SPLIT, 2, PAIR)
    bias = lax.dynamic_index_in_dim(bias_lo, sp, 0, keepdims=False)
    bias_hidden = vectors_full[5:9].reshape(NC, FC)

    field_lo, four_lo = filter_forward_lo(one_lo, vectors_full, tabs_lo, weights_lo, bias_lo)
    fields, four = filter_forward(slabs, tabs, weights, bias)
    fields = exchange(fields)

    block_lo, gm_lo, gwi, gwo, gc1, gv = feed(
        False, own, live_slots, one_lo, one_cot, [field_lo], vectors_full, bias_hidden, win, wout, ()
    )
    block_hi, p0, p1, p2, p3, gwi, gwo, gc1, gv = feed(
        True, own, live_slots, split_hi, split_cot, fields, vectors_full, bias_hidden, win, wout,
        (gwi, gwo, gc1, gv),
    )
    packs = [p0, p1, p2, p3]
    red_in = lax.psum_scatter(gwi, axes, scatter_dimension=0, tiled=True)
    red_out = lax.psum_scatter(gwo, axes, scatter_dimension=0, tiled=True)

    grad_slabs = exchange(packs)
    grad_lo, gspec, ge_lo, gv_lo = filter_backward_lo(
        one_lo, gm_lo, four_lo, vectors_full, tabs_lo, weights_lo, bias_lo
    )
    back, gspec, ge = filter_backward(own, grad_slabs, four, tabs, weights, bias, gspec)
    back = exchange(back)
    grad_hi, gv_hi = norm_backward(own, split_hi, packs, back, vectors_full)

    ge_all = lax.dynamic_update_index_in_dim(
        ge_lo, lax.dynamic_index_in_dim(ge_lo, sp, 0, keepdims=False) + ge, sp, 0
    )
    ge_rows = jnp.transpose(ge_all.reshape(SPLIT, 2, 2, GD), (1, 2, 0, 3)).reshape(4, D)
    grad_vectors = jnp.concatenate([gv_lo + gv_hi, gv[:3], gc1.reshape(4, D), ge_rows], axis=0)

    red_spec = lax.psum_scatter(
        gspec.reshape(4 * NB * BS, BS), axes, scatter_dimension=0, tiled=True
    )
    red_vectors = lax.psum_scatter(grad_vectors, axes, scatter_dimension=1, tiled=True)

    new_moment_spec = momentum * moment_spec + red_spec
    new_moment_in = momentum * moment_in.T + red_in
    new_moment_out = momentum * moment_out + red_out
    dir_in = red_in + momentum * new_moment_in
    dir_out = red_out + momentum * new_moment_out
    dir_spec = red_spec + momentum * new_moment_spec

    gram_in, gram_out = lax.psum(
        (
            jnp.dot(dir_in.T, dir_in, precision=highest),
            jnp.dot(dir_out.T, dir_out, precision=highest),
        ),
        axes,
    )
    orth_in, orth_out = newton_pair(gram_in, gram_out, dir_in, dir_out)
    rows = moment_spec.shape[0]
    if rows == BS:
        orth_spec = newton_small(dir_spec)
    else:
        whole = lax.all_gather(dir_spec, "sp", axis=0, tiled=True)
        orth_spec = lax.dynamic_slice_in_dim(newton_small(whole), sp * rows, rows, 0)

    keep_share = 1.0 - muon_rate * decay
    new_weight_in = weight_in * keep_share - muon_rate * orth_in.T
    new_weight_out = weight_out * keep_share - muon_rate * math.sqrt(max(1.0, FF / D)) * orth_out
    new_spectral = spectral_w * keep_share - muon_rate * orth_spec
    new_adam_first = beta_one * adam_first + (1.0 - beta_one) * red_vectors
    new_adam_second = beta_two * adam_second + (1.0 - beta_two) * red_vectors * red_vectors
    first_hat = new_adam_first / (1.0 - beta_one**STEP)
    second_hat = new_adam_second / (1.0 - beta_two**STEP)
    new_vectors = vectors * (1.0 - adam_rate * decay) - adam_rate * first_hat / (
        jnp.sqrt(second_hat) + 1e-08
    )
    return (
        block_hi.reshape(samples_hi.shape),
        block_lo.reshape(samples_lo.shape),
        grad_hi.reshape(samples_hi.shape),
        grad_lo.reshape(samples_lo.shape),
        new_spectral,
        new_weight_in,
        new_weight_out,
        new_moment_spec,
        new_moment_in.T,
        new_moment_out,
        new_vectors,
        new_adam_first,
        new_adam_second,
    )


def solution(mesh):
    both = ("dp", "sp")
    hi = P("dp", None, "sp", None)
    lo = P(both, None, None, None)
    rows = P(both, None)
    cols = P(None, both)
    return jax.shard_map(
        body,
        mesh=mesh,
        in_specs=(hi, lo, hi, lo, P(both), rows, cols, cols, rows, rows, cols, rows, cols, cols),
        out_specs=(hi, lo, hi, lo, rows, cols, rows, rows, cols, rows, cols, cols, cols),
        check_vma=False,
    )
```

time: 3070 us -> 1340 us (0.44)
  matrix products: 1070 us -> 6.96 us
  waiting for transfers between devices: 1250 us -> 255 us
  Pallas kernels: 0 us -> 799 us
  local copies, waits for them, and re-layouts: 460 us -> 37 us
  other arithmetic: 132 us -> 16.8 us
  blocking collectives: 123 us -> 199 us
    dot_general x152 -> x2, matrix products: 1070 us -> 6.96 us  [the longest x1 3.52 us: body(): jnp.dot(dir_out.T, dir_out, precision=highest)]
    pallas_call x0 -> x10, Pallas kernels: none -> 799 us  [the longest x2 287 us: feed(): pl.pallas_call(functools.partial(feed_kernel, high), grid=(steps,), in_sp...]
    all_gather x8 -> x2, waiting for transfers between devices: 589 us -> 0.01 us  [the longest x1 0.01 us: body(): wout = lax.all_gather(weight_out.astype(BF), axes, axis=0, tiled=True)]
    psum x5 -> x1, waiting for transfers between devices: 575 us -> 61.9 us  [body(): lax.psum((jnp.dot(dir_in.T, dir_in, precision=highest), jnp.dot(dir_out.T...]
    reshape x26 -> x7, local copies, waits for them, and re-layouts: 212 us -> 4.78 us  [the longest x1 3.8 us: body(): one_cot = cotan_lo.reshape(HL, WL, D)]
    another operation x23 -> x0, local copies, waits for them, and re-layouts: 151 us -> none
    reduce_sum x14 -> x0, other arithmetic: 88.2 us -> none  [the longest x5 56 us: column_sum(): return jnp.sum(values.astype(jnp.float32), axis=0)]
    all_gather x2, blocking collectives: 83.3 us -> 158 us  [the longest x1 113 us: body(): lax.all_gather(spectral_w.astype(BF), axes, axis=0, tiled=True)]
  transfers between devices with their start and end apart: 16 -> 18, of which waited for: 13 -> 4; matrix products, arithmetic and copies ran while one was open for 32% -> 4% of each run, Pallas kernels for 0% -> 31%
where the time goes in v1:
time: 1340 us
  Pallas kernels  799 us (60%)
  waiting for transfers between devices  255 us (19%)
  blocking collectives  199 us (15%)
  local copies, waits for them, and re-layouts  37 us (3%)
  other arithmetic  16.8 us (1%)
  between operations  15.4 us (1%)
    pallas_call x2, Pallas kernels, feed(): pl.pallas_call(functools.partial(feed_kernel, high), grid=(steps,), in_sp...  287 us
    pallas_call x1, Pallas kernels, newton_pair(): pl.pallas_call(newton_kernel, in_specs=[VM] * 4, out_specs=[VM] * 2, out_...  167 us
    pallas_call x1, Pallas kernels, filter_backward(): pl.pallas_call(filter_back_kernel, in_specs=[SM] + [VM] * 14, out_specs=[...  126 us
    all_gather x1, blocking collectives, body(): lax.all_gather(spectral_w.astype(BF), axes, axis=0, tiled=True)  113 us
    pallas_call x1, Pallas kernels, filter_forward(): pl.pallas_call(filter_kernel, in_specs=[VM] * 12, out_specs=[VM] * 5, out...  95.4 us
    reduce_scatter x1, waiting for transfers between devices, body(): lax.psum_scatter(gspec.reshape(4 * NB * BS, BS), axes, scatter_dimension=...  85.6 us
    reduce_scatter x1, waiting for transfers between devices, body(): red_in = lax.psum_scatter(gwi, axes, scatter_dimension=0, tiled=True)  65 us
    psum x1, waiting for transfers between devices, body(): lax.psum((jnp.dot(dir_in.T, dir_in, precision=highest), jnp.dot(dir_out.T...  61.9 us
  transfers between devices with their start and end apart: 18, of which 4 were waited for; matrix products, arithmetic and copies ran while one was open for 4% of the time, Pallas kernels for 31%

profile of v1, /device:TPU:0, one launch (start us, length us, event | category | flops | bytes accessed | tf_op | source)
XLA Modules:
  0.0 1337.3 jit_solution(17093047040733391532)
XLA Ops:
  7.2 1.6 convert_bitcast_fusion
  8.9 1.6 convert_element_type.32
  10.7 44.6 %all-gather = f32[32,24,13]{1,2,0:T(8,128)S(1)} all-gather(f32[1,24,13]{1,2,0:T(8,128)} %bitcast.84), channel_id=1, replica_groups=mesh['dp'=8,'sp'=4] {'dp','sp'}, dimensions={0}, use_global_device_ids=true | all-gather | bytes 41184 | tf_op jit(solution)/shard_map/all_gather | solution.py:990
  55.3 0.8 reshape.123
  56.1 16.7 %norm_pack.1 = (bf16[45,48,384]{2,1,0:T(8,128)(2,1)}, bf16[45,48,384]{2,1,0:T(8,128)(2,1)}, bf16[45,48,384]{2,1,0:T(8,128)(2,1)}, bf16[45,48,384]{2,1,0:T(8,128)(2,1)}) custom-call(s32[1]{0:T(128)} %bitcast.own_ref, bf16[2,45,45,768]{3,2,1,0:T(8,128)(2,1)} %bitcast.62, f32[13,768]{1,0:T(8,128)} %bitcast.69), custom_call_target="tpu_custom_call" | custom-call | tf_op jit(solution)/shard_map/norm_pack/pallas_call | solution.py:187
  73.1 1.5 collective-permute-start.2
  74.9 1.5 dynamic-slice_bitcast_fusion.1
  76.4 0.7 copy.53.tw
  77.4 113.4 %all_gather.13 = bf16[3072,96]{1,0:T(8,128)(2,1)S(1)} all-gather(bf16[96,96]{1,0:T(8,128)(2,1)S(1)} %convert_element_type.28), channel_id=1, replica_groups=mesh['dp'=8,'sp'=4] {'dp','sp'}, dimensions={0}, use_global_device_ids=true | all-gather | bytes 608256 | tf_op jit(solution)/shard_map/all_gather | solution.py:991
  192.8 0.6 dynamic-slice_bitcast_fusion.3.bias
  194.0 0.8 dynamic-slice_bitcast_fusion.w1
  194.8 0.9 fusion.2
  195.7 95.4 %filter_forward.1 = (bf16[45,48,384]{2,1,0:T(8,128)(2,1)}, bf16[45,48,384]{2,1,0:T(8,128)(2,1)}, bf16[45,48,384]{2,1,0:T(8,128)(2,1)}, bf16[45,48,384]{2,1,0:T(8,128)(2,1)}, bf16[13,2,672,192]{3,2,1,0:T(8,128)(2,1)}) custom-call(bf16[45,48,384]{2,1,0:T(8,128)(2,1)} %get-tuple-element.53.x0, bf16[45,48,384]{2,1,0:T(8,128)(2,1)} %collective-permute-done.x1, ...), custom_call_target="tpu_custom_call" | custom-call | tf_op jit(solution)/shard_map/filter_forward/pallas_call | solution.py:406
  291.5 1.6 collective-permute-start.4
  293.8 0.6 reshape.111.refs_4_.refs_7_
  294.4 1.5 pad_maximum_fusion.1
  295.9 3.8 copy_bitcast_fusion
  299.7 35.0 %filter_forward_lo.1 = (bf16[24,48,768]{2,1,0:T(8,128)(2,1)}, bf16[4,2,576,192]{3,2,1,0:T(8,128)(2,1)}) custom-call(bf16[23,45,768]{2,1,0:T(8,128)(2,1)} %get-tuple-element.164.x_ref.refs_0_, f32[13,768]{1,0:T(8,128)} %bitcast.70, bf16[48,48]{1,0:T(8,128)(2,1)} %constant.70.clone.tw, bf16[48,48]{1,0:T(8,128)(2,1)} %constant.81.twt, ...), custom_call_target="tpu_custom_call" | custom-call | tf_op jit(solution)/shard_map/filter_forward_lo/pallas_call | solution.py:573
  334.7 74.4 %feed_lo.1 = (bf16[23,45,768]{2,1,0:T(8,128)(2,1)}, bf16[24,48,768]{2,1,0:T(8,128)(2,1)}, f32[3072,768]{1,0:T(8,128)}, f32[3072,768]{1,0:T(8,128)}, f32[6,512]{1,0:T(8,128)}, /*index=5*/f32[8,768]{1,0:T(8,128)}) custom-call(s32[1]{0:T(128)} %bitcast.own_ref, s32[1]{0:T(128)S(6)} %copy.68.live_ref, bf16[23,45,768]{2,1,0:T(8,128)(2,1)} %get-tuple-element.164.x_ref.refs_0_, ...), custom_call_target="tpu_custom_call" | custom-call | tf_op jit(solution)/shard_map/feed_lo/pallas_call | solution.py:826
  409.2 212.2 %feed_hi.1 = (bf16[2,45,45,768]{3,2,1,0:T(8,128)(2,1)}, bf16[45,48,384]{2,1,0:T(8,128)(2,1)}, bf16[45,48,384]{2,1,0:T(8,128)(2,1)}, bf16[45,48,384]{2,1,0:T(8,12...) custom-call(s32[1]{0:T(128)} %bitcast.own_ref, ...), custom_call_target="tpu_custom_call" | custom-call | tf_op jit(solution)/shard_map/feed_hi/pallas_call | solution.py:826
  621.4 0.5 reduce-scatter.7.cloned.1.call-update
  622.0 0.9 copy-done.5
  622.9 0.5 collective-permute-start.6
  623.4 1.7 collective-permute-start.7
  625.2 44.8 %filter_backward_lo.1 = (f32[23,45,768]{2,1,0:T(8,128)}, f32[32,96,96]{2,1,0:T(8,128)}, f32[4,2,384]{2,1,0:T(2,128)}, f32[2,768]{1,0:T(2,128)}) custom-call(bf16[23,45,768]{2,1,0:T(8,128)(2,1)} %get-tuple-element.164.x_ref.refs_0_, bf16[24,48,768]{2,1,0:T(8,128)(2,1)} %get-tuple-element.73.gm_ref, bf16[4,2,576,192]{3,2,1,0:T(8,128)(2,1)} %get-tuple-element.74.four, ...), custom_call_target="tpu_custom_call" | custom-call | tf_op jit(solution)/shard_map/filter_backward_lo/pallas_call | solution.py:653
  670.0 41.4 %collective-permute-done.8.x3 = bf16[45,48,384]{2,1,0:T(8,128)(2,1)} collective-permute-done((bf16[45,48,384]{2,1,0:T(8,128)(2,1)}, bf16[45,48,384]{2,1,0:T(8,128)(2,1)}, u32[]{:S(2)}, u32[]{:S(2)}) %collective-permute-start.8) | collective-permute-done | bytes 1658912 | tf_op jit(solution)/shard_map/ppermute | solution.py:202
  711.4 125.8 %filter_backward.1 = (bf16[45,48,384]{2,1,0:T(8,128)(2,1)}, bf16[45,48,384]{2,1,0:T(8,128)(2,1)}, bf16[45,48,384]{2,1,0:T(8,128)(2,1)}, bf16[45,48,384]{2,1,0:T(...) custom-call(s32[1]{0:T(128)} %bitcast.own_ref, bf16[45,48,384]{2,1,0:T(8,128)(2,1)} %get-tuple-element.68.x0.m0, ...), custom_call_target="tpu_custom_call" | custom-call | tf_op jit(solution)/shard_map/filter_backward/pallas_call | solution.py:460
  837.5 0.7 copy-done.10
  838.2 1.7 multiply_add_fusion
  839.9 65.0 %reduce-scatter.7.cloned.1.call-done = f32[96,768]{1,0:T(8,128)} async-done(((f32[3072,768]{1,0:T(8,128)}), f32[96,768]{1,0:T(8,128)}) %reduce-scatter.7.cloned.1.call-update) | async-done | bytes 294928 | tf_op jit(solution)/shard_map/reduce_scatter | solution.py:1020
  904.9 1.7 fusion
  906.6 3.4 fusion.11
  910.1 3.5 fusion.12
  913.7 1.5 collective-permute-start.10
  915.6 4.9 copy.60
  920.6 3.2 copy.58
  924.0 85.6 %reduce-scatter.5.cloned.1.call-done = f32[96,96]{1,0:T(8,128)} async-done(((f32[3072,96]{1,0:T(8,128)}), f32[96,96]{1,0:T(8,128)}) %reduce-scatter.5.cloned.1.call-update) | async-done | bytes 36880 | tf_op jit(solution)/shard_map/reduce_scatter | solution.py:1037
  1009.6 1.4 multiply_add_fusion.3
  1011.0 4.7 newton_small.1
  1015.8 1.4 multiply_subtract_fusion.1
  1017.2 22.6 %norm_backward.1 = (f32[2,45,45,768]{3,2,1,0:T(8,128)}, f32[2,768]{1,0:T(2,128)}) custom-call(s32[1]{0:T(128)} %bitcast.own_ref, bf16[2,45,45,768]{3,2,1,0:T(8,128)(2,1)} %bitcast.64, bf16[45,48,384]{2,1,0:T(8,128)(2,1)} %get-tuple-element.68.x0.m0, bf16[45,48,384]{2,1,0:T(8,128)(2,1)} %get-tuple-element.69.m1, bf16[45,48,384]{2,1,0:T(8,128)(2,1)} %get-tuple-element.70.m2, ...), custom_call_target="tpu_custom_call" | custom-call | tf_op jit(solution)/shard_map/norm_backward/pallas_call | solution.py:878
  1039.9 15.8 %copy.59 = f32[1,90,45,768]{3,0,2,1:T(1,128)} copy(f32[1,90,45,768]{3,2,1,0:T(8,128)} %bitcast.65) | data formatting | bytes 24883200
  1055.8 40.9 %all-reduce = f32[13,768]{1,0:T(8,128)S(1)} all-reduce(f32[13,768]{1,0:T(8,128)S(1)} %pad_maximum_fusion.2), channel_id=5, replica_groups=mesh['dp'=8,'sp'=4] {'dp','sp'}, use_global_device_ids=true, to_apply=%region_5.6.clone | all-reduce | flops 9984 | bytes 79872
  1096.7 0.7 divide_subtract_fusion
  1097.4 61.9 %all-reduce.4.cloned.1.call-done = (f32[768,768]{1,0:T(8,128)}, f32[768,768]{1,0:T(8,128)}) async-done(((f32[768,768]{1,0:T(8,128)}, f32[768,768]{1,0:T(8,128)}), (f32[768,768]{1,0:T(8,128)}, f32[768,768]{1,0:T(8,128)})) %all-reduce.4.cloned.1.call-update) | async-done | bytes 4718608 | tf_op jit(solution)/shard_map/psum | solution.py:1049
  1159.3 167.5 %newton.1 = (f32[96,768]{1,0:T(8,128)}, f32[96,768]{1,0:T(8,128)}) custom-call(f32[768,768]{1,0:T(8,128)} %get-tuple-element.132.g_in, f32[768,768]{1,0:T(8,128)} %get-tuple-element.133.g_out, f32[96,768]{1,0:T(8,128)} %copy-done.2, f32[96,768]{1,0:T(8,128)} %copy-done.1), custom_call_target="tpu_custom_call" | custom-call | tf_op jit(solution)/shard_map/newton/pallas_call | solution.py:927
  1326.8 1.7 bitcast_subtract_fusion
  1328.5 1.7 multiply_subtract_fusion
  (107 shorter events, 5.2 us)
Async XLA Ops:
  7.2 327.5 %all-gather.4.cloned.1.call-start = ((), (), s32[]{:S(2)}) async-start(), calls=%async_computation.3 | async-start | bytes 4866048 | tf_op jit(solution)/shard_map/all_gather | solution.py:992
  8.9 325.8 %all-gather.6.cloned.1.call-start = ((), (), s32[]{:S(2)}) async-start(), calls=%async_computation.4 | async-start | bytes 4866048 | tf_op jit(solution)/shard_map/all_gather | solution.py:993
  10.6 826.9 %reduce-scatter.9.cloned.1.call-start = ((), (), s32[]{:S(2)}) async-start(), calls=%async_computation.7 | async-start | bytes 9732096 | tf_op jit(solution)/shard_map/reduce_scatter | solution.py:1021
  56.1 18.6 %copy-start.12 = (f32[96,96]{1,0:T(8,128)S(1)}, f32[96,96]{1,0:T(8,128)}, u32[]{:S(2)}) copy-start(f32[96,96]{1,0:T(8,128)} %param.23) | copy-start | bytes 110596
  56.1 21.1 %copy-start.4 = (f32[768,13]{0,1:T(8,128)S(1)}, f32[768,13]{0,1:T(8,128)}, u32[]{:S(2)}) copy-start(f32[768,13]{0,1:T(8,128)} %reshape.123) | copy-start | bytes 119812
  72.8 122.9 %collective-permute-start = (bf16[45,48,384]{2,1,0:T(8,128)(2,1)}, bf16[45,48,384]{2,1,0:T(8,128)(2,1)}, u32[]{:S(2)}, u32[]{:S(2)}) collective-permute-start(bf16[45,48,384]{2,1,0:T(8,128)(2,1)} %get-tuple-element.54), channel_id=1, source_target_pairs={{0,1},{1,0},{2,3},{3,2},{4,5},{5,4},{6,7},{7,6},{8,9},{9,8},{10,11... | collective-permute-start | bytes 4976648 | tf_op jit(solution)/shard_map/ppermute | solution.py:202
  73.1 122.5 %collective-permute-start.1 = (bf16[45,48,384]{2,1,0:T(8,128)(2,1)}, bf16[45,48,384]{2,1,0:T(8,128)(2,1)}, u32[]{:S(2)}, u32[]{:S(2)}) collective-permute-start(bf16[45,48,384]{2,1,0:T(8,128)(2,1)} %get-tuple-element.55), channel_id=1, source_target_pairs={{0,2},{1,3},{2,0},{3,1},{4,6},{5,7},{6,4},{7,5},{8,10},{9,11},{10,... | collective-permute-start | bytes 4976648 | tf_op jit(solution)/shard_map/ppermute | solution.py:202
  73.1 122.5 %collective-permute-start.2 = (bf16[45,48,384]{2,1,0:T(8,128)(2,1)}, bf16[45,48,384]{2,1,0:T(8,128)(2,1)}, u32[]{:S(2)}, u32[]{:S(2)}) collective-permute-start(bf16[45,48,384]{2,1,0:T(8,128)(2,1)} %get-tuple-element.56), channel_id=1, source_target_pairs={{0,3},{1,2},{2,1},{3,0},{4,7},{5,6},{6,5},{7,4},{8,11},{9,10},{10,... | collective-permute-start | bytes 4976648 | tf_op jit(solution)/shard_map/ppermute | solution.py:202
  77.4 115.4 %copy-start.13 = (f32[4,2,384]{2,1,0:T(2,128)}, f32[4,2,384]{2,1,0:T(2,128)S(1)}, u32[]{:S(2)}) copy-start(f32[4,2,384]{2,1,0:T(2,128)S(1)} %reshape.110.bias) | copy-start | bytes 36868
  194.0 97.1 %copy-start = (bf16[4,384,384]{2,1,0:T(8,128)(2,1)}, bf16[4,384,384]{2,1,0:T(8,128)(2,1)S(1)}, u32[]{:S(2)}) copy-start(bf16[4,384,384]{2,1,0:T(8,128)(2,1)S(1)} %maximum_maximum_fusion.w1) | copy-start | bytes 3538948
  291.0 4.8 copy-start.7
  291.0 118.1 %collective-permute-start.3 = (bf16[45,48,384]{2,1,0:T(8,128)(2,1)}, bf16[45,48,384]{2,1,0:T(8,128)(2,1)}, u32[]{:S(2)}, u32[]{:S(2)}) collective-permute-start(bf16[45,48,384]{2,1,0:T(8,128)(2,1)} %get-tuple-element.58), channel_id=1, source_target_pairs={{0,1},{1,0},{2,3},{3,2},{4,5},{5,4},{6,7},{7,6},{8,9},{9,8},{10,11... | collective-permute-start | bytes 4976648 | tf_op jit(solution)/shard_map/ppermute | solution.py:202
  291.5 117.7 %collective-permute-start.4 = (bf16[45,48,384]{2,1,0:T(8,128)(2,1)}, bf16[45,48,384]{2,1,0:T(8,128)(2,1)}, u32[]{:S(2)}, u32[]{:S(2)}) collective-permute-start(bf16[45,48,384]{2,1,0:T(8,128)(2,1)} %get-tuple-element.59), channel_id=1, source_target_pairs={{0,2},{1,3},{2,0},{3,1},{4,6},{5,7},{6,4},{7,5},{8,10},{9,11},{10,... | collective-permute-start | bytes 4976648 | tf_op jit(solution)/shard_map/ppermute | solution.py:202
  293.1 116.1 %collective-permute-start.5 = (bf16[45,48,384]{2,1,0:T(8,128)(2,1)}, bf16[45,48,384]{2,1,0:T(8,128)(2,1)}, u32[]{:S(2)}, u32[]{:S(2)}) collective-permute-start(bf16[45,48,384]{2,1,0:T(8,128)(2,1)} %get-tuple-element.60), channel_id=1, source_target_pairs={{0,3},{1,2},{2,1},{3,0},{4,7},{5,6},{6,5},{7,4},{8,11},{9,10},{10,... | collective-permute-start | bytes 4976648 | tf_op jit(solution)/shard_map/ppermute | solution.py:202
  621.4 283.5 %reduce-scatter.7.cloned.1.call-start = ((), (), s32[]{:S(2)}) async-start(), calls=%async_computation.6 | async-start | bytes 9732096 | tf_op jit(solution)/shard_map/reduce_scatter | solution.py:1020
  621.4 1.4 copy-start.5
  621.4 1.9 copy-start.6
  621.9 387.6 %reduce-scatter.5.cloned.1.call-start = ((), (), s32[]{:S(2)}) async-start(), calls=%async_computation.5 | async-start | bytes 1622016 | tf_op jit(solution)/shard_map/reduce_scatter | solution.py:1037
  622.9 47.2 %collective-permute-start.6 = (bf16[45,48,384]{2,1,0:T(8,128)(2,1)S(1)}, bf16[45,48,384]{2,1,0:T(8,128)(2,1)}, u32[]{:S(2)}, u32[]{:S(2)}) collective-permute-start(bf16[45,48,384]{2,1,0:T(8,128)(2,1)S(1)} %copy-done.5), channel_id=1, source_target_pairs={{0,1},{1,0},{2,3},{3,2},{4,5},{5,4},{6,7},{7,6},{8,9},{9,8},{10,11... | collective-permute-start | bytes 4976648 | tf_op jit(solution)/shard_map/ppermute | solution.py:202
  623.4 46.7 %collective-permute-start.7 = (bf16[45,48,384]{2,1,0:T(8,128)(2,1)S(1)}, bf16[45,48,384]{2,1,0:T(8,128)(2,1)}, u32[]{:S(2)}, u32[]{:S(2)}) collective-permute-start(bf16[45,48,384]{2,1,0:T(8,128)(2,1)S(1)} %copy-done.6), channel_id=1, source_target_pairs={{0,2},{1,3},{2,0},{3,1},{4,6},{5,7},{6,4},{7,5},{8,10},{9,11},{10,... | collective-permute-start | bytes 4976648 | tf_op jit(solution)/shard_map/ppermute | solution.py:202
  625.1 86.3 %collective-permute-start.8 = (bf16[45,48,384]{2,1,0:T(8,128)(2,1)}, bf16[45,48,384]{2,1,0:T(8,128)(2,1)}, u32[]{:S(2)}, u32[]{:S(2)}) collective-permute-start(bf16[45,48,384]{2,1,0:T(8,128)(2,1)} %get-tuple-element.71.m3), channel_id=1, source_target_pairs={{0,3},{1,2},{2,1},{3,0},{4,7},{5,6},{6,5},{7,4},{8,11},{9,10},{10,... | collective-permute-start | bytes 4976648 | tf_op jit(solution)/shard_map/ppermute | solution.py:202
  837.2 1.0 copy-start.10
  837.2 67.7 %copy-start.11 = (f32[768,96]{0,1:T(8,128)S(1)}, f32[768,96]{0,1:T(8,128)}, u32[]{:S(2)}) copy-start(f32[768,96]{0,1:T(8,128)} %param.28) | copy-start | bytes 884740
  837.2 322.1 %all-reduce.4.cloned.1.call-start = ((), (), s32[]{:S(2)}) async-start(), calls=%async_computation.8 | async-start | bytes 9437184 | tf_op jit(solution)/shard_map/psum | solution.py:1049
  839.9 70.2 %copy-start.1 = (f32[96,768]{1,0:T(8,128)}, f32[96,768]{1,0:T(8,128)S(1)}, u32[]{:S(2)}) copy-start(f32[96,768]{1,0:T(8,128)S(1)} %get-tuple-element.137.x_out) | copy-start | bytes 884740
  906.6 7.0 copy-start.2
  913.6 2.0 copy-start.3
  913.6 103.6 %collective-permute-start.9 = (bf16[45,48,384]{2,1,0:T(8,128)(2,1)}, bf16[45,48,384]{2,1,0:T(8,128)(2,1)}, u32[]{:S(2)}, u32[]{:S(2)}) collective-permute-start(bf16[45,48,384]{2,1,0:T(8,128)(2,1)} %get-tuple-element.77), channel_id=1, source_target_pairs={{0,1},{1,0},{2,3},{3,2},{4,5},{5,4},{6,7},{7,6},{8,9},{9,8},{10,11... | collective-permute-start | bytes 4976648 | tf_op jit(solution)/shard_map/ppermute | solution.py:202
  913.7 103.5 %collective-permute-start.10 = (bf16[45,48,384]{2,1,0:T(8,128)(2,1)}, bf16[45,48,384]{2,1,0:T(8,128)(2,1)}, u32[]{:S(2)}, u32[]{:S(2)}) collective-permute-start(bf16[45,48,384]{2,1,0:T(8,128)(2,1)} %get-tuple-element.78), channel_id=1, source_target_pairs={{0,2},{1,3},{2,0},{3,1},{4,6},{5,7},{6,4},{7,5},{8,10},{9,11},{10,... | collective-permute-start | bytes 4976648 | tf_op jit(solution)/shard_map/ppermute | solution.py:202
  915.2 102.0 %collective-permute-start.11 = (bf16[45,48,384]{2,1,0:T(8,128)(2,1)}, bf16[45,48,384]{2,1,0:T(8,128)(2,1)}, u32[]{:S(2)}, u32[]{:S(2)}) collective-permute-start(bf16[45,48,384]{2,1,0:T(8,128)(2,1)} %get-tuple-element.79), channel_id=1, source_target_pairs={{0,3},{1,2},{2,1},{3,0},{4,7},{5,6},{6,5},{7,4},{8,11},{9,10},{10,... | collective-permute-start | bytes 4976648 | tf_op jit(solution)/shard_map/ppermute | solution.py:202
  915.6 5.0 copy-start.20
  915.6 5.0 copy-start.17
  920.5 3.2 copy-start.16
  920.6 3.2 copy-start.23
  920.6 89.0 %copy-start.14 = (f32[96,96]{1,0:T(8,128)S(1)}, f32[96,96]{1,0:T(8,128)}, u32[]{:S(2)}) copy-start(f32[96,96]{1,0:T(8,128)} %param.27) | copy-start | bytes 110596
  1039.8 15.9 %copy-start.21 = (f32[2,768]{1,0:T(2,128)S(1)}, f32[2,768]{1,0:T(2,128)}, u32[]{:S(2)}) copy-start(f32[2,768]{1,0:T(2,128)} %get-tuple-element.87) | copy-start | bytes 18436
  1039.8 15.9 %copy-start.22 = (f32[2,768]{1,0:T(2,128)S(1)}, f32[2,768]{1,0:T(2,128)}, u32[]{:S(2)}) copy-start(f32[2,768]{1,0:T(2,128)} %get-tuple-element.88) | copy-start | bytes 18436
  1039.8 56.8 %copy-start.15 = (f32[13,24]{1,0:T(8,128)S(1)}, f32[13,24]{1,0:T(8,128)}, u32[]{:S(2)}) copy-start(f32[13,24]{1,0:T(8,128)} %param.24) | copy-start | bytes 3748
  1039.8 56.8 %copy-start.18 = (f32[13,24]{1,0:T(8,128)S(1)}, f32[13,24]{1,0:T(8,128)}, u32[]{:S(2)}) copy-start(f32[13,24]{1,0:T(8,128)} %param.30) | copy-start | bytes 3748
  1039.9 56.8 %copy-start.19 = (f32[13,24]{1,0:T(8,128)S(1)}, f32[13,24]{1,0:T(8,128)}, u32[]{:S(2)}) copy-start(f32[13,24]{1,0:T(8,128)} %param.31) | copy-start | bytes 3748
  1159.3 167.5 %copy-start.8 = (f32[768,96]{0,1:T(8,128)S(1)}, f32[768,96]{0,1:T(8,128)}, u32[]{:S(2)}) copy-start(f32[768,96]{0,1:T(8,128)} %param.25) | copy-start | bytes 884740
  1159.3 169.2 %copy-start.9 = (f32[96,768]{1,0:T(8,128)S(1)}, f32[96,768]{1,0:T(8,128)}, u32[]{:S(2)}) copy-start(f32[96,768]{1,0:T(8,128)} %param.26) | copy-start | bytes 884740
Sparse Core Ops, SparseCore 0:
  11.5 68.7 all-gather.3
  83.2 72.4 all-gather.5
  621.5 141.8 reduce-scatter.8
  770.1 134.7 reduce-scatter.6
  910.0 99.5 reduce-scatter.4
  1015.3 143.9 all-reduce.3

commit v2 on v1

v2 whole, which is shorter than its diff:
```python
import functools
import math

import jax
import jax.numpy as jnp
import numpy as np
from jax import lax
from jax.experimental import pallas as pl
from jax.experimental.pallas import tpu as pltpu
from jax.sharding import PartitionSpec as P

D = 768
FF = 3072
NB = 8
BS = 96
H = 90
W = 180
HL = 23
WL = 45
STEP = 10
NEWTON_STEPS = 5

F32 = jnp.float32
BF = jnp.bfloat16
highest = lax.Precision.HIGHEST
epsilon = 1e-06
shrink_level = 0.01
shrink_sharp = 10.0
momentum = 0.95
newton_a = 3.4445
newton_b = -4.775
newton_c = 2.0315
muon_rate = 0.5
adam_rate = 0.3
decay = 0.01
beta_one = 0.9
beta_two = 0.999

K0 = math.sqrt(2.0 / math.pi)
K1 = K0 * 0.044715

SPLIT = 4
GD = D // SPLIT
PAIR = 2 * GD
HALF = H // 2
OWN = W // SPLIT
PW = 48
PM = 96
KF = W // 2 + 1
KP = 96
KG = 7
GROUPS = KF // KG
ROWS = KG * PM
LH = 24
LK = HL // 2 + 1
LROWS = LK * PW
HB = 5
LB = 15
FC = 512
NC = FF // FC
VMEM_LIMIT = 60 * 2**20
UNROLL = 5
CHUNK = 48


def wave(length, rows, cols):
    phase = np.outer(rows, cols) % length
    angle = phase * (2.0 * math.pi / length)
    factor = 1.0 / math.sqrt(length)
    return np.cos(angle) * factor, np.sin(angle) * factor


def tables():
    wide = np.zeros((SPLIT, 2 * KP, SPLIT * PW))
    for s in range(SPLIT):
        for j in range(SPLIT):
            cols = (s ^ j) * OWN + np.arange(OWN)
            c, d = wave(W, np.arange(KF), cols)
            wide[s, :KF, j * PW : j * PW + OWN] = c
            wide[s, KP : KP + KF, j * PW : j * PW + OWN] = -d
    tall = np.zeros((2 * PM, 2 * PM))
    for part in range(2):
        c, d = wave(H, np.arange(H), part * HALF + np.arange(HALF))
        re, im = part * PW, PM + part * PW
        tall[:H, re : re + HALF] = c
        tall[:H, im : im + HALF] = d
        tall[PM : PM + H, re : re + HALF] = -d
        tall[PM : PM + H, im : im + HALF] = c
    wide_lo = np.zeros((2 * LK, LH))
    c, d = wave(HL, np.arange(LK), np.arange(HL))
    wide_lo[:LK, :HL] = c
    wide_lo[LK:, :HL] = -d
    tall_lo = np.zeros((2 * PW, 2 * PW))
    c, d = wave(WL, np.arange(WL), np.arange(WL))
    tall_lo[:WL, :WL] = c
    tall_lo[:WL, PW : PW + WL] = d
    tall_lo[PW : PW + WL, :WL] = -d
    tall_lo[PW : PW + WL, PW : PW + WL] = c
    return wide, tall, wide_lo, tall_lo


def loop(count, unroll, one):
    def some(i, carry):
        for n in range(unroll):
            one(i * unroll + n)
        return carry

    lax.fori_loop(0, count // unroll, some, 0)


def dot(left, right):
    return jnp.dot(left, right, preferred_element_type=F32)


def dot_nt(left, right):
    return lax.dot_general(left, right, (((1,), (1,)), ((), ())), preferred_element_type=F32)


def dot_tn(left, right):
    return lax.dot_general(left, right, (((0,), (0,)), ((), ())), preferred_element_type=F32)


def normed(values):
    center = values - jnp.mean(values, axis=-1, keepdims=True)
    scale = lax.rsqrt(jnp.mean(center * center, axis=-1, keepdims=True) + epsilon)
    return center * scale, scale


def norm_back(grad, norm, scale, gain):
    pushed = grad * gain
    return scale * (
        pushed
        - jnp.mean(pushed, axis=-1, keepdims=True)
        - norm * jnp.mean(pushed * norm, axis=-1, keepdims=True)
    )


def pad_rows(values, rows=PW):
    return jnp.concatenate(
        [values, jnp.zeros((rows - values.shape[0], values.shape[1]), values.dtype)], axis=0
    )


def lanes(*pieces):
    return jnp.concatenate(pieces, axis=1)


def unpack_pair(fs):
    pieces = [fs[g].astype(F32) for g in range(SPLIT)]
    return (
        lanes(*[p[:, :GD] for p in pieces]),
        lanes(*[p[:, GD:] for p in pieces]),
    )


def pack_pair(row_a, row_b, fs):
    for g in range(SPLIT):
        cut = slice(g * GD, (g + 1) * GD)
        fs[g] = lanes(row_a[:, cut], row_b[:, cut]).astype(BF)


SP = ("sy", "sc")
VM = pl.BlockSpec(memory_space=pltpu.VMEM)
SM = pl.BlockSpec(memory_space=pltpu.SMEM)
ANY = pl.BlockSpec(memory_space=pl.ANY)


def params():
    return pltpu.CompilerParams(vmem_limit_bytes=VMEM_LIMIT)


def cost(us):
    return pl.CostEstimate(flops=us * 10**9, bytes_accessed=us * 10**6, transcendentals=0)


def shape(dims, kind):
    return jax.ShapeDtypeStruct(dims, kind)


PACKED = (HALF, PW, PAIR)
PACKED_BLOCK = pl.BlockSpec((HB, PW, PAIR), lambda i: (i, 0, 0))
WIDE_BLOCK = pl.BlockSpec((2, HB, OWN, D), lambda i: (0, i, 0, 0))


def pack_kernel(own_ref, x_ref, vec_ref, o0, o1, o2, o3, fs):
    own = own_ref[0]
    gain, shift = vec_ref[0:1, :], vec_ref[1:2, :]

    for i in range(HB):
        rows = []
        for part in range(2):
            norm, _unused = normed(x_ref[part, i].astype(F32))
            rows.append(pad_rows(norm * gain + shift))
        pack_pair(rows[0], rows[1], fs.at[i])
    for i in range(HB):
        for j, out in enumerate((o0, o1, o2, o3)):
            out[i] = fs[i, own ^ j]


def norm_packed(own, samples, vectors):
    return pl.pallas_call(
        pack_kernel,
        grid=(HALF // HB,),
        in_specs=[SM, WIDE_BLOCK, VM],
        out_specs=[PACKED_BLOCK] * SPLIT,
        out_shape=[shape(PACKED, BF)] * SPLIT,
        scratch_shapes=[pltpu.VMEM((HB, SPLIT, PW, PAIR), BF)],
        compiler_params=params(),
        name="norm_pack",
        cost_estimate=cost(16),
    )(own, samples, vectors)


def exchange(slabs):
    moved = [slabs[0]]
    for j in range(1, SPLIT):
        moved.append(lax.ppermute(slabs[j], SP, [(i, i ^ j) for i in range(SPLIT)]))
    return moved


def to_freq_wide(slabs, table, space):
    def one(i):
        rows = jnp.concatenate([slab[i] for slab in slabs], axis=0)
        area = dot(table[...], rows)
        for c in range(3):
            space[c, pl.ds(i, 2 * KP, stride=PW), :] = area[:, c * 128 : (c + 1) * 128]

    loop(HALF, UNROLL, one)


def to_freq_tall(k, table, space):
    re = lanes(*[space[c, pl.ds(pl.multiple_of(k * PW, PW), PW), :] for c in range(3)])
    im = lanes(*[space[c, pl.ds(pl.multiple_of((KP + k) * PW, PW), PW), :] for c in range(3)])
    rows = jnp.concatenate([re[:, :GD], re[:, GD:], im[:, :GD], im[:, GD:]], axis=0)
    return dot(table[...], rows.astype(BF))


def to_space_tall(k, table, four, space):
    back = dot(table[...], four)
    for part in range(2):
        base = part * PM
        packed = lanes(back[base : base + PW], back[base + PW : base + PM])
        at = pl.ds(pl.multiple_of((part * KP + k) * PW, PW), PW)
        for c in range(3):
            space[c, at, :] = packed[:, c * 128 : (c + 1) * 128]


def to_space_wide(table, space, outs):
    def one(i):
        rows = lanes(*[space[c, pl.ds(i, 2 * KP, stride=PW), :] for c in range(3)])
        field = dot(table[...], rows.astype(BF)).astype(BF)
        for j, out in enumerate(outs):
            out[i] = field[j * PW : (j + 1) * PW]

    loop(HALF, UNROLL, one)


def clear(ref):
    def one(i, _):
        for c in range(ref.shape[0]):
            ref[c, pl.ds(pl.multiple_of(i * 96, 96), 96), :] = jnp.zeros((96, 128), F32)
        return 0

    lax.fori_loop(0, ref.shape[1] // 96, one, 0)


def keep_minus(row, width, first, last):
    at = row + lax.broadcasted_iota(jnp.int32, (width, 1), 0)
    return jnp.where((at >= first) & (at < last), 1.0, 0.0).astype(F32)


def mlp_forward(fre, fim, wu, wv, w1, bias, us, vs, actp, actm, put, base, first, last, chunk):
    rows = us.shape[0]
    us[...] = dot(fre, wu)
    vs[...] = dot(fim, wv)
    b0, b1 = bias[0:1, :], bias[1:2, :]

    def act(i, _):
        at = pl.ds(pl.multiple_of(i * chunk, chunk), chunk)
        u = us[at, :] + b0
        v = vs[at, :]
        for ref, value in ((actp, u + v), (actm, u - v)):
            t = jnp.tanh(value * (K0 + K1 * (value * value)))
            ref[at, :] = (value * (0.5 + 0.5 * t)).astype(BF)
        return 0

    lax.fori_loop(0, rows // chunk, act, 0)
    us[...] = dot(actp[...], w1)
    vs[...] = dot(actm[...], w1)

    def shrunk(i, _):
        at = pl.ds(pl.multiple_of(i * chunk, chunk), chunk)
        p = us[at, :] + b1
        m = vs[at, :] + b1
        p = p - shrink_level * jnp.tanh(shrink_sharp * p)
        m = (m - shrink_level * jnp.tanh(shrink_sharp * m)) * keep_minus(
            base + i * chunk, chunk, first, last
        )
        put(at, (p[:, :GD] + m[:, :GD]).astype(BF), (p[:, GD:] - m[:, GD:]).astype(BF))
        return 0

    lax.fori_loop(0, rows // chunk, shrunk, 0)


def mlp_backward(
    fre, fim, gs, wu, wv, w1, bias, us, vs, actp, actm, dp, dm, gsp, gsm, sums, put,
    gwu, gwv, gw1, ge, base, first, last, chunk,
):
    rows = us.shape[0]
    us[...] = dot(fre, wu)
    vs[...] = dot(fim, wv)
    b0, b1 = bias[0:1, :], bias[1:2, :]
    sign = jnp.where(lax.broadcasted_iota(jnp.int32, (1, PAIR), 1) < GD, 1.0, -1.0).astype(F32)

    def act(i, _):
        at = pl.ds(pl.multiple_of(i * chunk, chunk), chunk)
        u = us[at, :] + b0
        v = vs[at, :]
        for ref, slope, value in ((actp, dp, u + v), (actm, dm, u - v)):
            square = value * value
            hp = 0.5 + 0.5 * jnp.tanh(value * (K0 + K1 * square))
            on = value * hp
            ref[at, :] = on.astype(BF)
            slope[at, :] = hp + on * (1.0 - hp) * (2.0 * K0 + 6.0 * K1 * square)
        return 0

    lax.fori_loop(0, rows // chunk, act, 0)
    us[...] = dot(actp[...], w1)
    vs[...] = dot(actm[...], w1)

    def second(i, total):
        at = pl.ds(pl.multiple_of(i * chunk, chunk), chunk)
        grad = gs[at, :]
        tp = jnp.tanh(shrink_sharp * (us[at, :] + b1))
        tm = jnp.tanh(shrink_sharp * (vs[at, :] + b1))
        flat = 1.0 - shrink_level * shrink_sharp
        bend = shrink_level * shrink_sharp
        p = grad * (flat + bend * (tp * tp))
        m = (grad * (sign * keep_minus(base + i * chunk, chunk, first, last))) * (
            flat + bend * (tm * tm)
        )
        gsp[at, :] = p.astype(BF)
        gsm[at, :] = m.astype(BF)
        return total + jnp.sum(p + m, axis=0, keepdims=True)

    ge[1:2, :] += lax.fori_loop(0, rows // chunk, second, jnp.zeros((1, PAIR), F32))
    us[...] = dot_nt(gsp[...], w1)
    vs[...] = dot_nt(gsm[...], w1)
    gw1[...] += dot_tn(actp[...], gsp[...]) + dot_tn(actm[...], gsm[...])

    def first_grad(i, total):
        at = pl.ds(pl.multiple_of(i * chunk, chunk), chunk)
        p = us[at, :] * dp[at, :]
        m = vs[at, :] * dm[at, :]
        both = p + m
        gsp[at, :] = both.astype(BF)
        gsm[at, :] = (p - m).astype(BF)
        return total + jnp.sum(both, axis=0, keepdims=True)

    ge[0:1, :] += lax.fori_loop(0, rows // chunk, first_grad, jnp.zeros((1, PAIR), F32))
    gwu[...] += dot_tn(fre, gsp[...])
    gwv[...] += dot_tn(fim, gsm[...])
    put(dot_nt(gsp[...], wu).astype(BF), dot_nt(gsm[...], wv).astype(BF))


def block_grads(gwu, gwv, gw1):
    cells = {}
    for b in range(2):
        r = slice(b * BS, (b + 1) * BS)
        i = slice(GD + b * BS, GD + (b + 1) * BS)
        cells[0, 0, b] = gwu[r, r] + gwv[r, i]
        cells[0, 1, b] = gwu[r, i] - gwv[r, r]
        cells[1, 0, b] = gw1[r, r] + gw1[i, i]
        cells[1, 1, b] = gw1[r, i] - gw1[i, r]
    return cells


def filter_kernel(
    own_ref, x0, x1, x2, x3, tw, twt, th, tht, wu, wv, w1, bias,
    y0, y1, y2, y3, four, space, us, vs, actp, actm, zr, zi,
):
    own = own_ref[0]
    clear(space)
    to_freq_wide((x0, x1, x2, x3), tw.at[own], space)

    def group(g, _):
        for n in range(KG):
            rows = to_freq_tall(g * KG + n, th, space).astype(BF)
            four[g, 0, n * PM : (n + 1) * PM, :] = rows[:PM]
            four[g, 1, n * PM : (n + 1) * PM, :] = rows[PM:]

        def put(at, re, im):
            zr[at, :] = re
            zi[at, :] = im

        mlp_forward(
            four[g, 0], four[g, 1], wu[own], wv[own], w1[own], bias.at[own], us, vs, actp, actm, put,
            g * ROWS, PM, (KF - 1) * PM, CHUNK,
        )
        for n in range(KG):
            at = slice(n * PM, (n + 1) * PM)
            to_space_tall(
                g * KG + n, tht, jnp.concatenate([zr[at, :], zi[at, :]], axis=0), space
            )
        return 0

    lax.fori_loop(0, GROUPS, group, 0)
    to_space_wide(twt.at[own], space, (y0, y1, y2, y3))


def filter_scratch(rows, wide):
    big = pltpu.VMEM((rows, PAIR), F32)
    low = pltpu.VMEM((rows, PAIR), BF)
    part = pltpu.VMEM((rows, GD), BF)
    return big, low, part


def filter_forward(own, slabs, tabs, weights, bias):
    big, low, part = filter_scratch(ROWS, None)
    outs = pl.pallas_call(
        filter_kernel,
        in_specs=[SM] + [VM] * 12,
        out_specs=[VM] * 5,
        out_shape=[shape(PACKED, BF)] * SPLIT + [shape((GROUPS, 2, ROWS, GD), BF)],
        scratch_shapes=[pltpu.VMEM((3, 2 * KP * PW, 128), F32), big, big, low, low, part, part],
        compiler_params=params(),
        name="filter_forward",
        cost_estimate=cost(95),
    )(own, *slabs, *tabs, *weights, bias)
    return outs[:SPLIT], outs[SPLIT]


def filter_back_kernel(
    own_ref, x0, x1, x2, x3, four, tw, twt, th, tht, wu, wv, w1, bias,
    y0, y1, y2, y3, grads, ge,
    space, us, vs, actp, actm, zr, zi, gs, dp, dm, gsp, gsm, gwu, gwv, gw1,
):
    own = own_ref[0]
    clear(space)
    gwu[...] = jnp.zeros_like(gwu)
    gwv[...] = jnp.zeros_like(gwv)
    gw1[...] = jnp.zeros_like(gw1)
    ge[...] = jnp.zeros_like(ge)
    to_freq_wide((x0, x1, x2, x3), tw.at[own], space)

    def group(g, _):
        for n in range(KG):
            rows = to_freq_tall(g * KG + n, th, space)
            gs[n * PM : (n + 1) * PM, :] = lanes(rows[:PM], rows[PM:])

        def put(re, im):
            zr[...] = re
            zi[...] = im

        mlp_backward(
            four[g, 0], four[g, 1], gs, wu[own], wv[own], w1[own], bias.at[own], us, vs, actp, actm, dp, dm,
            gsp, gsm, None, put, gwu, gwv, gw1, ge, g * ROWS, PM, (KF - 1) * PM, CHUNK,
        )
        for n in range(KG):
            at = slice(n * PM, (n + 1) * PM)
            to_space_tall(
                g * KG + n, tht, jnp.concatenate([zr[at, :], zi[at, :]], axis=0), space
            )
        return 0

    lax.fori_loop(0, GROUPS, group, 0)
    grads[...] = jnp.zeros_like(grads)
    for (layer, part, b), value in block_grads(gwu, gwv, gw1).items():
        grads[(2 * layer + part) * NB + 2 * own + b] = value
    to_space_wide(twt.at[own], space, (y0, y1, y2, y3))


def filter_backward(own, slabs, four, tabs, weights, bias):
    big, low, part = filter_scratch(ROWS, None)
    outs = pl.pallas_call(
        filter_back_kernel,
        in_specs=[SM] + [VM] * 13,
        out_specs=[VM] * 6,
        out_shape=[shape(PACKED, BF)] * SPLIT
        + [shape((4 * NB, BS, BS), F32), shape((2, PAIR), F32)],
        scratch_shapes=[pltpu.VMEM((3, 2 * KP * PW, 128), F32), big, big, low, low, part, part]
        + [big, big, big, low, low]
        + [pltpu.VMEM((GD, PAIR), F32)] * 2
        + [pltpu.VMEM((PAIR, PAIR), F32)],
        compiler_params=params(),
        name="filter_backward",
        cost_estimate=cost(125),
    )(own, *slabs, four, *tabs, *weights, bias)
    return outs[:SPLIT], outs[SPLIT], outs[SPLIT + 1]


def lo_freq_wide(i, rows, table, space):
    area = dot(table[...], rows)
    for c in range(6):
        space[c, pl.ds(i, 2 * LK, stride=PW), :] = area[:, c * 128 : (c + 1) * 128]


def lo_freq_tall(k, table, space):
    parts = []
    for base in (0, LK):
        at = pl.ds(pl.multiple_of((base + k) * PW, PW), PW)
        parts.append(lanes(*[space[c, at, :] for c in range(6)]))
    rows = dot(table[...], jnp.concatenate(parts, axis=0).astype(BF))
    return rows[:PW], rows[PW:]


def lo_space_tall(k, table, re, im, space):
    back = dot(table[...], jnp.concatenate([re, im], axis=0).astype(BF))
    for part, base in enumerate((0, LK)):
        at = pl.ds(pl.multiple_of((base + k) * PW, PW), PW)
        for c in range(6):
            space[c, at, :] = back[part * PW : (part + 1) * PW, c * 128 : (c + 1) * 128]


def lo_space_wide(i, table, space):
    rows = lanes(*[space[c, pl.ds(i, 2 * LK, stride=PW), :] for c in range(6)])
    return dot(table[...], rows.astype(BF))


def filter_lo_kernel(
    x_ref, vec_ref, tw, twt, th, tht, wu, wv, w1, bias, y_ref, four,
    space, us, vs, actp, actm, zr, zi,
):
    clear(space)
    gain, shift = vec_ref[0:1, :], vec_ref[1:2, :]

    def wide(i):
        norm, _unused = normed(x_ref[i].astype(F32))
        lo_freq_wide(i, pad_rows(norm * gain + shift, LH).astype(BF), tw, space)

    loop(WL, UNROLL, wide)

    def tall(k):
        re, im = lo_freq_tall(k, th, space)
        at = pl.ds(pl.multiple_of(k * PW, PW), PW)
        for g in range(SPLIT):
            cut = slice(g * GD, (g + 1) * GD)
            four[g, 0, at, :] = re[:, cut].astype(BF)
            four[g, 1, at, :] = im[:, cut].astype(BF)

    loop(LK, 3, tall)

    def group(g, _):
        def put(at, re, im):
            zr[g, at, :] = re
            zi[g, at, :] = im

        mlp_forward(
            four[g, 0], four[g, 1], wu[g], wv[g], w1[g], bias.at[g], us, vs, actp, actm, put,
            0, PW, LROWS, CHUNK,
        )
        return 0

    lax.fori_loop(0, SPLIT, group, 0)

    def back(k):
        at = pl.ds(pl.multiple_of(k * PW, PW), PW)
        re = lanes(*[zr[g, at, :].astype(F32) for g in range(SPLIT)])
        im = lanes(*[zi[g, at, :].astype(F32) for g in range(SPLIT)])
        lo_space_tall(k, tht, re, im, space)

    loop(LK, 3, back)

    def last(i):
        y_ref[i] = lo_space_wide(i, twt, space).astype(BF)

    loop(WL, UNROLL, last)


def lo_scratch():
    big, low, _ = filter_scratch(LROWS, None)
    part = pltpu.VMEM((SPLIT, LROWS, GD), BF)
    return [pltpu.VMEM((6, 2 * LK * PW, 128), F32), big, big, low, low, part, part]


def filter_forward_lo(samples, vectors, tabs, weights, bias):
    return pl.pallas_call(
        filter_lo_kernel,
        in_specs=[VM] * 10,
        out_specs=[VM] * 2,
        out_shape=[shape((WL, LH, D), BF), shape((SPLIT, 2, LROWS, GD), BF)],
        scratch_shapes=lo_scratch(),
        compiler_params=params(),
        name="filter_forward_lo",
        cost_estimate=cost(35),
    )(samples, vectors, *tabs, *weights, bias)


def filter_back_lo_kernel(
    x_ref, gm_ref, four, vec_ref, tw, twt, th, tht, wu, wv, w1, bias, grads_in,
    grad_ref, grads, ge, gvec,
    space, us, vs, actp, actm, zr, zi, gs, dp, dm, gsp, gsm, gwu, gwv, gw1,
):
    clear(space)
    ge[...] = jnp.zeros_like(ge)
    gvec[...] = jnp.zeros_like(gvec)

    def wide(i):
        lo_freq_wide(i, gm_ref[i], tw, space)

    loop(WL, UNROLL, wide)

    def tall(k):
        re, im = lo_freq_tall(k, th, space)
        at = pl.ds(pl.multiple_of(k * PW, PW), PW)
        for g in range(SPLIT):
            cut = slice(g * GD, (g + 1) * GD)
            gs[g, at, :] = lanes(re[:, cut], im[:, cut])

    loop(LK, 3, tall)

    def group(g, _):
        gwu[...] = jnp.zeros_like(gwu)
        gwv[...] = jnp.zeros_like(gwv)
        gw1[...] = jnp.zeros_like(gw1)

        def put(re, im):
            zr[g] = re
            zi[g] = im

        mlp_backward(
            four[g, 0], four[g, 1], gs.at[g], wu[g], wv[g], w1[g], bias.at[g], us, vs, actp, actm,
            dp, dm, gsp, gsm, None, put, gwu, gwv, gw1, ge.at[g], 0, PW, LROWS, CHUNK,
        )
        for (layer, part, b), value in block_grads(gwu, gwv, gw1).items():
            at = (2 * layer + part) * NB + 2 * g + b
            grads[at] = grads_in[at] + value
        return 0

    lax.fori_loop(0, SPLIT, group, 0)

    def back(k):
        at = pl.ds(pl.multiple_of(k * PW, PW), PW)
        re = lanes(*[zr[g, at, :].astype(F32) for g in range(SPLIT)])
        im = lanes(*[zi[g, at, :].astype(F32) for g in range(SPLIT)])
        lo_space_tall(k, tht, re, im, space)

    loop(LK, 3, back)
    gain = vec_ref[0:1, :]

    def last(t, _):
        sums = []
        for n in range(UNROLL):
            i = t * UNROLL + n
            field = lo_space_wide(i, twt, space)[:HL]
            direct = gm_ref[i].astype(F32)[:HL]
            norm, scale = normed(x_ref[i].astype(F32))
            grad = field + direct
            sums.append((jnp.sum(grad * norm, axis=0, keepdims=True), jnp.sum(grad, axis=0, keepdims=True)))
            value = direct + norm_back(grad, norm, scale, gain)
            for c in range(6):
                at = pl.ds(6 * i + c, HL, stride=6 * WL)
                grad_ref[at, 0, :] = value[:, c * 128 : (c + 1) * 128]
        gvec[0:1, :] += sum(a for a, b in sums)
        gvec[1:2, :] += sum(b for a, b in sums)
        return 0

    lax.fori_loop(0, WL // UNROLL, last, 0)


def filter_backward_lo(samples, grad_mixed, four, vectors, tabs, weights, bias, grads_in):
    big, low, _ = filter_scratch(LROWS, None)
    return pl.pallas_call(
        filter_back_lo_kernel,
        in_specs=[VM] * 13,
        out_specs=[VM] * 4,
        out_shape=[
            shape((HL * WL * 6, 1, 128), F32),
            shape((4 * NB, BS, BS), F32),
            shape((SPLIT, 2, PAIR), F32),
            shape((2, D), F32),
        ],
        scratch_shapes=lo_scratch()
        + [pltpu.VMEM((SPLIT, LROWS, PAIR), F32), big, big, low, low]
        + [pltpu.VMEM((GD, PAIR), F32)] * 2
        + [pltpu.VMEM((PAIR, PAIR), F32)],
        compiler_params=params(),
        name="filter_backward_lo",
        cost_estimate=cost(45),
    )(samples, grad_mixed, four, vectors, *tabs, *weights, bias, grads_in)


def feed_chunks(n2, cots, c1_ref, win, wout, out_acc, gn_acc, gw, gc1):
    out_acc[...] = jnp.zeros_like(out_acc)
    gn_acc[...] = jnp.zeros_like(gn_acc)

    def chunk(c, _):
        rows = pl.ds(c * FC, FC)
        low, cot = n2[...].reshape(-1, D), cots[...].reshape(-1, D)
        wi, wo = win[rows, :], wout[rows, :]
        hidden = dot_nt(low, wi) + c1_ref[pl.ds(c, 1), :]
        grad = dot_nt(cot, wo)
        square = hidden * hidden
        hp = 0.5 + 0.5 * jnp.tanh(hidden * (K0 + K1 * square))
        act = hidden * hp
        grad = grad * (hp + act * (1.0 - hp) * (2.0 * K0 + 6.0 * K1 * square))
        gc1[pl.ds(c, 1), :] += jnp.sum(grad, axis=0, keepdims=True)
        act = act.astype(BF)
        grad = grad.astype(BF)
        out_acc[...] += dot(act, wo)
        gn_acc[...] += dot(grad, wi)
        gw[1, rows, :] += dot_tn(act, cot)
        gw[0, rows, :] += dot_tn(grad, low)
        return 0

    for c in range(NC):
        chunk(c, 0)


def feed_kernel(high, own_ref, live_ref, *refs):
    count = SPLIT if high else 1
    x_ref, cot_ref = refs[:2]
    fields = refs[2 : 2 + count]
    rest = refs[2 + count :]
    vec_ref, c1_ref, win, wout = rest[:4]
    rest = rest[4:]
    if high:
        gw_in, gc1_in, gv_in = rest[:3]
        rest = rest[3:]
    block_ref = rest[0]
    packs = rest[1 : 1 + count]
    rest = rest[1 + count :]
    keep_out = rest[0]
    if high:
        give_out = rest[1]
        rest = rest[1:]
    gc1, gv, gw, sem, mixed, n2, cots, out_acc, gn_acc, fs = rest[1:]
    step = pl.program_id(0)

    @pl.when(step == 0)
    def _():
        if high:
            load = pltpu.make_async_copy(gw_in, gw, sem)
            load.start()
            load.wait()
            gc1[...] = gc1_in[...]
            gv[...] = gv_in[...]
        else:
            gw[...] = jnp.zeros_like(gw)
            gc1[...] = jnp.zeros_like(gc1)
            gv[...] = jnp.zeros_like(gv)

    own = own_ref[0]
    tall = PW if high else LH
    gain_one, shift_one = vec_ref[0:1, :], vec_ref[1:2, :]
    gain_two, shift_two = vec_ref[2:3, :], vec_ref[3:4, :]
    bias_out = vec_ref[4:5, :]

    def enter(plane, x, cot, field):
        at = pl.ds(plane * tall, tall)
        norm, _unused = normed(x)
        total = field + (norm * gain_one + shift_one) + x
        mixed[at, :] = total
        norm, _unused = normed(total)
        n2[plane] = (norm * gain_two + shift_two).astype(BF)
        cots[plane] = cot.astype(BF)

    def leave(plane):
        at = pl.ds(plane * tall, tall)
        total = mixed[at, :]
        out = total + (out_acc[at, :] + bias_out)
        norm, scale = normed(total)
        grad = gn_acc[at, :]
        cot = cots[plane].astype(F32)
        sums.append(
            tuple(jnp.sum(v, axis=0, keepdims=True) for v in (grad * norm, grad, cot))
        )
        return out.astype(BF), cot + norm_back(grad, norm, scale, gain_two)

    sums = []

    def add_sums():
        for row in range(3):
            gv[row : row + 1, :] += sum(entry[row] for entry in sums)
        sums.clear()

    if high:

        def before():
            for i in range(HB):
                for j in range(SPLIT):
                    fs[i, own ^ j] = fields[j][i]
            for i in range(HB):
                for part, field in enumerate(unpack_pair(fs.at[i])):
                    x = pad_rows(x_ref[part, i].astype(F32))
                    cot = pad_rows(cot_ref[part, i].astype(F32))
                    enter(part * HB + i, x, cot, field)

        def after():
            for i in range(HB):
                grads = []
                for part in range(2):
                    out, grad = leave(part * HB + i)
                    block_ref[part, i] = out[:OWN]
                    grads.append(grad)
                pack_pair(grads[0], grads[1], fs.at[i])
            add_sums()
            for i in range(HB):
                for j in range(SPLIT):
                    packs[j][i] = fs[i, own ^ j]

    else:
        live = live_ref[0].astype(F32)

        def before():
            for i in range(LB):
                x = pad_rows(x_ref[i].astype(F32), LH)
                cot = pad_rows(cot_ref[i].astype(F32), LH) * live
                enter(i, x, cot, fields[0][i].astype(F32))

        def after():
            for i in range(LB):
                out, grad = leave(i)
                block_ref[i] = out[:HL]
                packs[0][i] = grad.astype(BF)
            add_sums()

    before()
    feed_chunks(n2, cots, c1_ref, win, wout, out_acc, gn_acc, gw, gc1)
    after()

    @pl.when(step == pl.num_programs(0) - 1)
    def _():
        if not high:
            store = pltpu.make_async_copy(gw, keep_out, sem)
            store.start()
            store.wait()
        else:
            mine = lax.rem(own, 2)
            store = pltpu.make_async_copy(gw.at[mine], keep_out, sem)
            store.start()

            def low(c, _):
                rows = pl.ds(pl.multiple_of(c * FC, FC), FC)
                give_out[rows, :] = gw[1 - mine, rows, :].astype(BF)
                return 0

            lax.fori_loop(0, NC, low, 0)
            store.wait()


def feed(high, own, live, samples, cotan, fields, vectors, bias_hidden, win, wout, earlier):
    planes, tall = (2 * HB, PW) if high else (LB, LH)
    tokens = planes * tall
    if high:
        steps = HALF // HB
        wide, packed, packed_shape = WIDE_BLOCK, PACKED_BLOCK, PACKED
    else:
        steps = WL // LB
        wide = pl.BlockSpec((LB, HL, D), lambda i: (i, 0, 0))
        packed = pl.BlockSpec((LB, LH, D), lambda i: (i, 0, 0))
        packed_shape = (WL, LH, D)
    count = len(fields)
    return pl.pallas_call(
        functools.partial(feed_kernel, high),
        grid=(steps,),
        in_specs=[SM, SM, wide, wide]
        + [packed] * count
        + [VM] * 4
        + ([ANY, VM, VM] if high else []),
        out_specs=[wide] + [packed] * count + ([ANY, VM] if high else [ANY]) + [VM, VM],
        out_shape=[shape(samples.shape, BF)]
        + [shape(packed_shape, BF)] * count
        + ([shape((FF, D), F32), shape((FF, D), BF)] if high else [shape((2, FF, D), F32)])
        + [shape((NC, FC), F32), shape((8, D), F32)],
        scratch_shapes=[
            pltpu.VMEM((2, FF, D), F32),
            pltpu.SemaphoreType.DMA,
            pltpu.VMEM((tokens, D), F32),
            pltpu.VMEM((planes, tall, D), BF),
            pltpu.VMEM((planes, tall, D), BF),
            pltpu.VMEM((tokens, D), F32),
            pltpu.VMEM((tokens, D), F32),
            pltpu.VMEM((HB, SPLIT, PW, PAIR), BF),
        ],
        compiler_params=params(),
        name="feed_hi" if high else "feed_lo",
        cost_estimate=cost(210 if high else 70),
    )(own, live, samples, cotan, *fields, vectors, bias_hidden, win, wout, *earlier)


def norm_back_kernel(own_ref, x_ref, m0, m1, m2, m3, f0, f1, f2, f3, vec_ref, grad_ref, gvec, fs, ms):
    @pl.when(pl.program_id(0) == 0)
    def _():
        gvec[...] = jnp.zeros_like(gvec)

    own = own_ref[0]
    gain = vec_ref[0:1, :]

    for i in range(HB):
        for j, (m, f) in enumerate(((m0, f0), (m1, f1), (m2, f2), (m3, f3))):
            ms[i, own ^ j] = m[i]
            fs[i, own ^ j] = f[i]
    sums = []
    for i in range(HB):
        for part, (direct, field) in enumerate(zip(unpack_pair(ms.at[i]), unpack_pair(fs.at[i]))):
            direct, field = direct[:OWN], field[:OWN]
            norm, scale = normed(x_ref[part, i].astype(F32))
            grad = field + direct
            sums.append((jnp.sum(grad * norm, axis=0, keepdims=True), jnp.sum(grad, axis=0, keepdims=True)))
            value = direct + norm_back(grad, norm, scale, gain)
            for c in range(6):
                at = pl.ds(i * (6 * OWN) + c, OWN, stride=6)
                grad_ref[part, at, 0, :] = value[:, c * 128 : (c + 1) * 128]
    gvec[0:1, :] += sum(a for a, b in sums)
    gvec[1:2, :] += sum(b for a, b in sums)


def norm_backward(own, samples, direct, fields, vectors):
    return pl.pallas_call(
        norm_back_kernel,
        grid=(HALF // HB,),
        in_specs=[SM, WIDE_BLOCK] + [PACKED_BLOCK] * (2 * SPLIT) + [VM],
        out_specs=[pl.BlockSpec((2, HB * OWN * 6, 1, 128), lambda i: (0, i, 0, 0)), VM],
        out_shape=[shape((2, HALF * OWN * 6, 1, 128), F32), shape((2, D), F32)],
        scratch_shapes=[pltpu.VMEM((HB, SPLIT, PW, PAIR), BF)] * 2,
        compiler_params=params(),
        name="norm_backward",
        cost_estimate=cost(22),
    )(own, samples, *direct, *fields, vectors)


def eye_of(size):
    return lax.broadcasted_iota(jnp.int32, (size, size), 0) == lax.broadcasted_iota(
        jnp.int32, (size, size), 1
    )


def mul(left, right):
    return jnp.dot(left, right, precision=highest, preferred_element_type=F32)


def split_three(values):
    top = values.astype(BF)
    rest = values - top.astype(F32)
    middle = rest.astype(BF)
    return top, middle, (rest - middle.astype(F32)).astype(BF)


TILE = 256


def mul_parts(left, right_ref, parts, full, out, finish=None):
    size = right_ref.shape[0]
    rows = left.shape[0]
    tile = TILE if rows % TILE == 0 else rows

    def cut(i, _):
        at = pl.ds(pl.multiple_of(i * TILE, TILE), TILE)
        for n, part in enumerate(split_three(right_ref[at, :])):
            parts[n, at, :] = part
        return 0

    lax.fori_loop(0, size // TILE, cut, 0)

    def one(i, _):
        at = pl.ds(pl.multiple_of(i * tile, tile), tile)
        top, middle, low = split_three(left[at, :])
        total = dot(middle, parts[0]) + dot(top, parts[1])
        if full:
            total = total + (dot(middle, parts[1]) + dot(top, parts[2]) + dot(low, parts[0]))
        total = total + dot(top, parts[0])
        out[at, :] = total if finish is None else finish(at, total)
        return 0

    lax.fori_loop(0, rows // tile, one, 0)


def newton_kernel(g_ref, x_ref, y_ref, gram, poly, hold, parts, once, twice):
    size = g_ref.shape[0]
    trace = jnp.sum(jnp.where(eye_of(size), g_ref[...], 0.0), keepdims=True)
    scale = 1.0 / (jnp.sqrt(trace) + 1e-07)
    gram[...] = g_ref[...] * (scale * scale)
    y_ref[...] = x_ref[...] * scale

    def turn(full):
        def polynomial(at, square):
            rows = at.start + lax.broadcasted_iota(jnp.int32, (TILE, size), 0)
            diagonal = rows == lax.broadcasted_iota(jnp.int32, (TILE, size), 1)
            return jnp.where(diagonal, newton_a, 0.0) + newton_b * gram[at, :] + newton_c * square

        mul_parts(gram, gram, parts, full, poly, polynomial)
        mul_parts(gram, poly, parts, full, hold)
        mul_parts(y_ref, poly, parts, full, once)
        y_ref[...] = once[...]
        mul_parts(poly, hold, parts, full, gram)

    turn(True)

    def later(_, carry):
        turn(False)
        return carry

    lax.fori_loop(1, NEWTON_STEPS - 1, later, 0)
    mul_parts(y_ref, gram, parts, False, once)
    mul_parts(once, gram, parts, False, twice)
    y_ref[...] = newton_a * y_ref[...] + newton_b * once[...] + newton_c * twice[...]


def newton_one(gram, rows):
    return pl.pallas_call(
        newton_kernel,
        in_specs=[VM] * 2,
        out_specs=VM,
        out_shape=shape(rows.shape, F32),
        scratch_shapes=[pltpu.VMEM((D, D), F32)] * 3
        + [pltpu.VMEM((3, D, D), BF)]
        + [pltpu.VMEM(rows.shape, F32)] * 2,
        compiler_params=params(),
        name="newton",
        cost_estimate=cost(60),
    )(gram, rows)


SWAP = [(0, 1), (1, 0)]


def choose(first, when_first, when_second):
    return jnp.where(first, when_first, when_second)


def both_rows(first, of_first, of_second):
    keep = choose(first, of_first, of_second)
    other = lax.ppermute(choose(first, of_second, of_first), "sc", SWAP)
    return jnp.concatenate(
        [choose(first, keep, other), choose(first, other, keep)], axis=0
    )


def own_rows(first, rows):
    upper, lower = jnp.split(rows, 2, axis=0)
    keep = choose(first, upper, lower)
    other = lax.ppermute(choose(first, lower, upper), "sc", SWAP)
    return choose(first, keep, other), choose(first, other, keep)


def newton_small_kernel(x_ref, y_ref):
    values = x_ref[...]
    size = 1.0 / (jnp.sqrt(jnp.sum(values * values, keepdims=True)) + 1e-07)
    values = values * size
    for _ in range(NEWTON_STEPS):
        gram = lax.dot_general(
            values, values, (((0,), (0,)), ((), ())), precision=highest, preferred_element_type=F32
        )
        once = mul(values, gram)
        values = newton_a * values + newton_b * once + newton_c * mul(once, gram)
    y_ref[...] = values


def newton_small(values):
    return pl.pallas_call(
        newton_small_kernel,
        in_specs=[VM],
        out_specs=VM,
        out_shape=shape(values.shape, F32),
        name="newton_small",
    )(values)


def place(dp, sp):
    return (dp, sp // 2, lax.rem(sp, 2))


def greet(count):
    dp, sp = lax.axis_index("dp"), lax.axis_index("sy") * 2 + lax.axis_index("sc")
    barrier = pltpu.get_barrier_semaphore()
    for o in range(1, count):
        pl.semaphore_signal(
            barrier, inc=1, device_id=place(lax.rem(dp + o, count), sp),
            device_id_type=pl.DeviceIdType.MESH,
        )
    for j in range(1, SPLIT):
        pl.semaphore_signal(
            barrier, inc=1, device_id=place(dp, sp ^ j), device_id_type=pl.DeviceIdType.MESH
        )
    pl.semaphore_wait(barrier, count - 1 + SPLIT - 1)
    return dp, sp


def send(source, target, out_sem, in_sem, device):
    copy = pltpu.make_async_remote_copy(
        src_ref=source, dst_ref=target, send_sem=out_sem, recv_sem=in_sem, device_id=device,
        device_id_type=pl.DeviceIdType.MESH,
    )
    copy.start()
    return copy


def gather_kernel(
    count, vec_ref, spec_ref, vec_out, wu, wv, w1, bias, c1,
    vbuf, sbuf, send_v, recv_v, send_s, recv_s, send_w, recv_w, send_t, recv_t,
):
    rows, cols = spec_ref.shape[0], vec_ref.shape[1]
    dp, sp = greet(count)
    vbuf[sp, dp] = jnp.zeros(vbuf.shape[2:], F32)
    vbuf[sp, dp, : vec_ref.shape[0], :cols] = vec_ref[...]
    sbuf[sp, dp] = jnp.zeros(sbuf.shape[2:], BF)
    sbuf[sp, dp, :, :BS] = spec_ref[...].astype(BF)
    copies = []
    for o in range(1, count):
        device = place(lax.rem(dp + o, count), sp)
        here = vbuf.at[sp, dp]
        copies.append(send(here, here, send_v.at[o], recv_v.at[o], device))
        here = sbuf.at[sp, dp]
        copies.append(send(here, here, send_s.at[o], recv_s.at[o], device))
    for ref in (wu, wv, w1):
        ref[...] = jnp.zeros_like(ref)
    for copy in copies:
        copy.wait()
    copies = []
    for j in range(1, SPLIT):
        device = place(dp, sp ^ j)
        copies.append(send(vbuf.at[sp], vbuf.at[sp], send_w.at[j], recv_w.at[j], device))
        copies.append(send(sbuf.at[sp], sbuf.at[sp], send_t.at[j], recv_t.at[j], device))
    for copy in copies:
        copy.wait()
    for i in range(count * SPLIT):
        vec_out[: vec_ref.shape[0], i * cols : (i + 1) * cols] = vbuf[
            i % SPLIT, i // SPLIT, : vec_ref.shape[0], :cols
        ]
        value = sbuf[i % SPLIT, i // SPLIT][:, :BS]
        cell, off = divmod(i * rows, BS)
        layer, part, g, b = cell // 16, (cell // 8) % 2, (cell % 8) // 2, cell % 2
        re = slice(b * BS + off, b * BS + off + rows)
        im = slice(GD + b * BS + off, GD + b * BS + off + rows)
        to_re, to_im = slice(b * BS, (b + 1) * BS), slice(GD + b * BS, GD + (b + 1) * BS)
        if layer == 0 and part == 0:
            wu[g, re, to_re] = value
            wv[g, re, to_im] = value
        elif layer == 0:
            wu[g, re, to_im] = value
            wv[g, re, to_re] = -value
        elif part == 0:
            w1[g, re, to_re] = value
            w1[g, im, to_im] = value
        else:
            w1[g, re, to_im] = value
            w1[g, im, to_re] = -value
    for g in range(SPLIT):
        cut = slice(g * GD, (g + 1) * GD)
        for layer in range(2):
            row = 9 + 2 * layer
            bias[g, layer : layer + 1, :GD] = vec_out[row : row + 1, cut]
            bias[g, layer : layer + 1, GD:] = vec_out[row + 1 : row + 2, cut]
    for piece in range(12):
        r, k = divmod(piece, 3)
        c, m = divmod(piece, 2)
        c1[c : c + 1, m * 256 : (m + 1) * 256] = vec_out[5 + r : 6 + r, k * 256 : (k + 1) * 256]


def dma_sems(*counts):
    return [pltpu.SemaphoreType.DMA((n,)) for n in counts]


def gather_small(count, vectors, spectral):
    rows = spectral.shape[0]
    return pl.pallas_call(
        functools.partial(gather_kernel, count),
        in_specs=[VM] * 2,
        out_specs=[VM] * 6,
        out_shape=[
            shape((16, D), F32),
            shape((SPLIT, GD, PAIR), BF),
            shape((SPLIT, GD, PAIR), BF),
            shape((SPLIT, PAIR, PAIR), BF),
            shape((SPLIT, 2, PAIR), F32),
            shape((NC, FC), F32),
        ],
        scratch_shapes=[
            pltpu.VMEM((SPLIT, count, 16, 128), F32),
            pltpu.VMEM((SPLIT, count, rows, 128), BF),
        ]
        + dma_sems(count, count, count, count, SPLIT, SPLIT, SPLIT, SPLIT),
        compiler_params=pltpu.CompilerParams(
            vmem_limit_bytes=VMEM_LIMIT, collective_id=0, has_side_effects=True
        ),
        name="gather_small",
        cost_estimate=cost(20),
    )(vectors, spectral)


def scatter_sums(count, dp, sp, jobs):
    copies = []
    for x_ref, land, total, land_two, (send_a, recv_a, send_b, recv_b) in jobs:
        for j in range(1, SPLIT):
            source = x_ref.at[:, sp ^ j]
            copies.append(
                send(source, land.at[j - 1], send_a.at[j], recv_a.at[j], place(dp, sp ^ j))
            )
    for copy in copies:
        copy.wait()
    copies = []
    for x_ref, land, total, land_two, (send_a, recv_a, send_b, recv_b) in jobs:
        total[...] = (x_ref[:, sp] + land[0]) + (land[1] + land[2])
        for o in range(1, count):
            to = lax.rem(dp + o, count)
            copies.append(
                send(total.at[to], land_two.at[o - 1], send_b.at[o], recv_b.at[o], place(to, sp))
            )
    for copy in copies:
        copy.wait()
    results = []
    for x_ref, land, total, land_two, sems in jobs:
        result = total[dp]
        for o in range(1, count):
            result = result + land_two[o - 1]
        results.append(result)
    return results


def scatter_scratch(count, rows, width):
    return [
        pltpu.VMEM((SPLIT - 1, count, rows, width), F32),
        pltpu.VMEM((count, rows, width), F32),
        pltpu.VMEM((count, rows, width), F32),
    ] + dma_sems(SPLIT, SPLIT, count, count)


def vectors_kernel(
    count, gspec, gv_lo, gv_hi, gv, gc1, ge_lo, ge, vec_ref, first_ref, second_ref,
    red_spec, new_vec, new_first, new_second, full, esum, x_ref, *scratch,
):
    height, cols = vec_ref.shape
    dp, sp = greet(count)
    full[...] = jnp.zeros_like(full)
    full[0:2, :] = gv_lo[...] + gv_hi[...]
    full[2:5, :] = gv[0:3, :]
    esum[...] = ge_lo[...]
    esum[sp] += ge[...]
    for piece in range(12):
        r, k = divmod(piece, 3)
        c, m = divmod(piece, 2)
        full[5 + r : 6 + r, k * 256 : (k + 1) * 256] = gc1[c : c + 1, m * 256 : (m + 1) * 256]
    for g in range(SPLIT):
        cut = slice(g * GD, (g + 1) * GD)
        for layer in range(2):
            row = 9 + 2 * layer
            full[row : row + 1, cut] = esum[g, layer : layer + 1, :GD]
            full[row + 1 : row + 2, cut] = esum[g, layer : layer + 1, GD:]
    x_ref[...] = jnp.zeros_like(x_ref)
    for i in range(count * SPLIT):
        x_ref[i // SPLIT, i % SPLIT, :, :cols] = full[:, i * cols : (i + 1) * cols]
    jobs = [
        (ref, *mine[:3], mine[3:]) for ref, mine in ((gspec, scratch[:7]), (x_ref, scratch[7:]))
    ]
    red_spec[...], grad = scatter_sums(count, dp, sp, jobs)
    grad = grad[:height, :cols]
    first = beta_one * first_ref[...] + (1.0 - beta_one) * grad
    second = beta_two * second_ref[...] + (1.0 - beta_two) * grad * grad
    new_first[...] = first
    new_second[...] = second
    first_hat = first / (1.0 - beta_one**STEP)
    second_hat = second / (1.0 - beta_two**STEP)
    new_vec[...] = vec_ref[...] * (1.0 - adam_rate * decay) - adam_rate * first_hat / (
        jnp.sqrt(second_hat) + 1e-08
    )


def update_small(count, grads, pieces, vectors, first, second):
    rows = 4 * NB * BS // (count * SPLIT)
    return pl.pallas_call(
        functools.partial(vectors_kernel, count),
        in_specs=[VM] * 10,
        out_specs=[VM] * 4,
        out_shape=[shape((rows, BS), F32)] + [shape(vectors.shape, F32)] * 3,
        scratch_shapes=[
            pltpu.VMEM((16, D), F32),
            pltpu.VMEM((SPLIT, 2, PAIR), F32),
            pltpu.VMEM((count, SPLIT, 16, 128), F32),
        ]
        + scatter_scratch(count, rows, BS)
        + scatter_scratch(count, 16, 128),
        compiler_params=pltpu.CompilerParams(
            vmem_limit_bytes=VMEM_LIMIT, collective_id=2, has_side_effects=True
        ),
        name="update_small",
        cost_estimate=cost(25),
    )(grads.reshape(count, SPLIT, rows, BS), *pieces, vectors, first, second)


def reduce_kernel(
    bits, keep, give, moment, new_moment, direction, gram,
    acc, land, red, load_sem, give_sems, *scratch,
):
    half = moment.shape[0] // 2
    dp, sy, sc = (lax.axis_index(name) for name in ("dp", "sy", "sc"))
    swap = (dp, sy, 1 - sc)
    partners = [(dp, 1 - sy, sc)] + [(dp ^ (1 << b), sy, sc) for b in range(bits - 1)]
    mine = [sy] + [lax.rem(dp // (1 << b), 2) for b in range(bits - 1)]
    barrier = pltpu.get_barrier_semaphore()
    for device in [swap] + partners:
        pl.semaphore_signal(barrier, inc=1, device_id=device, device_id_type=pl.DeviceIdType.MESH)
    load = pltpu.make_async_copy(keep, acc, load_sem)
    load.start()
    pl.semaphore_wait(barrier, bits + 1)
    copy = send(give, land, give_sems.at[0], give_sems.at[1], swap)
    load.wait()
    copy.wait()

    def join(o, _):
        for t in range(2):
            acc[o, t] = acc[o, t] + land[o, t].astype(F32)
        return 0

    lax.fori_loop(0, 2**bits, join, 0)
    streams = []
    for t in range(2):
        order = list(range(1, bits)) + [0]
        if t == 1:
            order[0], order[1] = order[1], order[0]
        streams.append(order)
    left = [list(range(bits)), list(range(bits))]
    current = [lambda block, t=t: acc.at[block, t] for t in range(2)]
    for stage in range(bits):
        count = 2 ** (bits - 1 - stage)
        copies = []
        for t in range(2):
            outgoing, incoming, _sum, sems = scratch[(stage * 2 + t) * 4 : (stage * 2 + t) * 4 + 4]
            bit = streams[t][stage]
            step = 1 << left[t].index(bit)
            side = mine[bit]

            def cast(o, _, t=t, outgoing=outgoing, step=step, side=side):
                block = (o // step) * (2 * step) + (1 - side) * step + lax.rem(o, step)
                outgoing[o] = current[t](block)[...].astype(BF)
                return 0

            lax.fori_loop(0, count, cast, 0)
            copies.append(send(outgoing, incoming, sems.at[0], sems.at[1], partners[bit]))
        following = []
        for t in range(2):
            outgoing, incoming, total, sems = scratch[(stage * 2 + t) * 4 : (stage * 2 + t) * 4 + 4]
            bit = streams[t][stage]
            step = 1 << left[t].index(bit)
            side = mine[bit]
            left[t].remove(bit)
            copies[t].wait()

            def add(o, _, t=t, incoming=incoming, total=total, step=step, side=side):
                block = (o // step) * (2 * step) + side * step + lax.rem(o, step)
                total[o] = current[t](block)[...] + incoming[o].astype(F32)
                return 0

            lax.fori_loop(0, count, add, 0)
            following.append(lambda block, total=total: total.at[block])
        current = following
    for t in range(2):
        red[t * half : (t + 1) * half, :] = current[t](0)[...]
    new = momentum * moment[...] + red[...]
    new_moment[...] = new
    pushed = red[...] + momentum * new
    direction[...] = pushed
    top, middle, low = split_three(pushed)
    gram[...] = (
        (dot_tn(middle, middle) + dot_tn(top, low) + dot_tn(low, top))
        + (dot_tn(top, middle) + dot_tn(middle, top))
    ) + dot_tn(top, top)


def reduce_feed(count, keep, give, moment):
    rows = moment.shape[0]
    blocks = FF // rows
    bits = blocks.bit_length() - 1
    whole = (blocks, 2, rows // 2, D)
    scratch = []
    for stage in range(bits):
        for _ in range(2):
            part = (2 ** (bits - 1 - stage), rows // 2, D)
            scratch += [pltpu.VMEM(part, BF), pltpu.VMEM(part, BF), pltpu.VMEM(part, F32)] + dma_sems(2)
    return pl.pallas_call(
        functools.partial(reduce_kernel, bits),
        in_specs=[ANY, ANY, VM],
        out_specs=[VM] * 3,
        out_shape=[shape((rows, D), F32)] * 2 + [shape((D, D), F32)],
        scratch_shapes=[
            pltpu.VMEM(whole, F32),
            pltpu.VMEM(whole, BF),
            pltpu.VMEM((rows, D), F32),
            pltpu.SemaphoreType.DMA,
        ]
        + dma_sems(2)
        + scratch,
        compiler_params=pltpu.CompilerParams(
            vmem_limit_bytes=VMEM_LIMIT, collective_id=1, has_side_effects=True
        ),
        name="reduce_feed",
        cost_estimate=cost(80),
    )(keep.reshape(whole), give.reshape(whole), moment)


def after(values, earlier):
    return lax.optimization_barrier((values, earlier))[0]


def body(
    count, samples_hi, samples_lo, cotan_hi, cotan_lo, live_slots, spectral_w, vectors, weight_in,
    weight_out, moment_spec, moment_in, moment_out, adam_first, adam_second,
):
    axes = ("dp", *SP)
    chips = ("dp", "sy")
    sp = lax.axis_index(SP)
    first = lax.axis_index("sc") == 0
    own = sp.astype(jnp.int32).reshape(1)
    wide, tall, wide_lo, tall_lo = (t.astype(BF) for t in tables())
    tabs = (wide, np.swapaxes(wide, 1, 2), tall, tall.T)
    tabs_lo = (wide_lo, wide_lo.T, tall_lo, tall_lo.T)
    tabs = tuple(jnp.asarray(np.ascontiguousarray(t)) for t in tabs)
    tabs_lo = tuple(jnp.asarray(np.ascontiguousarray(t)) for t in tabs_lo)

    vec, wu, wv, w1, bias, bias_hidden = gather_small(count, vectors, spectral_w)
    weights = (wu, wv, w1)
    slice_in, slice_out = after((weight_in, weight_out), vec)
    win = lax.all_gather(slice_in.T.astype(BF), axes, axis=0, tiled=True)
    wout = lax.all_gather(slice_out.astype(BF), axes, axis=0, tiled=True)

    split_hi = samples_hi.reshape(2, HALF, OWN, D)
    split_cot = cotan_hi.reshape(2, HALF, OWN, D)
    one_lo = samples_lo.reshape(HL, WL, D).transpose(1, 0, 2)
    one_cot = cotan_lo.reshape(HL, WL, D).transpose(1, 0, 2)

    moment = both_rows(first, moment_in.T, moment_out)
    slabs = exchange(norm_packed(own, split_hi, vec))
    field_lo, four_lo = filter_forward_lo(one_lo, vec, tabs_lo, weights, bias)
    slabs = after(slabs, field_lo)
    fields, four = filter_forward(own, slabs, tabs, weights, bias)
    field_lo = after(field_lo, fields)
    fields = exchange(fields)
    block_lo, gm_lo, gw, gc1, gv = feed(
        False, own, live_slots, one_lo, one_cot, [field_lo], vec, bias_hidden, win, wout, ()
    )
    block_hi, p0, p1, p2, p3, keep, give, gc1, gv = feed(
        True, own, live_slots, split_hi, split_cot, fields, vec, bias_hidden, win, wout,
        (gw, gc1, gv),
    )
    packs = [p0, p1, p2, p3]
    grad_slabs = exchange(packs)
    new_moment, direction, gram = reduce_feed(count, keep, give, moment)
    gram = lax.psum(gram, chips)
    grad_slabs = after(grad_slabs, direction)
    back, gspec, ge = filter_backward(own, grad_slabs, four, tabs, weights, bias)
    back = exchange(back)
    gm_lo = after(gm_lo, gspec)
    grad_lo, gspec, ge_lo, gv_lo = filter_backward_lo(
        one_lo, gm_lo, four_lo, vec, tabs_lo, weights, bias, gspec
    )
    gram = after(gram, gspec)
    orth = newton_one(gram, direction)
    back = after(back, orth)
    grad_hi, gv_hi = norm_backward(own, split_hi, packs, back, vec)
    red_spec, new_vectors, new_adam_first, new_adam_second = update_small(
        count, gspec, (gv_lo, gv_hi, gv, gc1, ge_lo, ge), vectors, adam_first, adam_second
    )
    new_moment_in, new_moment_out = own_rows(first, new_moment)
    orth_in, orth_out = own_rows(first, orth)
    new_moment_spec = momentum * moment_spec + red_spec
    dir_spec = red_spec + momentum * new_moment_spec
    rows = moment_spec.shape[0]
    if rows == BS:
        orth_spec = newton_small(dir_spec)
    else:
        gathered = lax.all_gather(dir_spec, SP, axis=0, tiled=True)
        orth_spec = lax.dynamic_slice_in_dim(newton_small(gathered), sp * rows, rows, 0)

    keep_share = 1.0 - muon_rate * decay
    new_weight_in = weight_in * keep_share - muon_rate * orth_in.T
    new_weight_out = weight_out * keep_share - muon_rate * math.sqrt(max(1.0, FF / D)) * orth_out
    new_spectral = spectral_w * keep_share - muon_rate * orth_spec
    return (
        block_hi.reshape(samples_hi.shape),
        block_lo.transpose(1, 0, 2).reshape(samples_lo.shape),
        grad_hi.reshape(samples_hi.shape),
        grad_lo.reshape(samples_lo.shape),
        new_spectral,
        new_weight_in,
        new_weight_out,
        new_moment_spec,
        new_moment_in.T,
        new_moment_out,
        new_vectors,
        new_adam_first,
        new_adam_second,
    )


def solution(mesh):
    count = mesh.shape["dp"]
    fine = jax.sharding.Mesh(mesh.devices.reshape(count, 2, 2), ("dp", *SP))
    both = ("dp", *SP)
    hi = P("dp", None, SP, None)
    lo = P(both, None, None, None)
    rows = P(both, None)
    cols = P(None, both)
    return jax.shard_map(
        functools.partial(body, count),
        mesh=fine,
        in_specs=(hi, lo, hi, lo, P(both), rows, cols, cols, rows, rows, cols, rows, cols, cols),
        out_specs=(hi, lo, hi, lo, rows, cols, rows, rows, cols, rows, cols, cols, cols),
        check_vma=False,
    )
```

time: 1340 us -> 908 us (0.68)
  blocking collectives: 199 us -> 0 us
  waiting for transfers between devices: 255 us -> 67.8 us
  local copies, waits for them, and re-layouts: 37 us -> 7.28 us
    all_gather x2 -> x0, blocking collectives: 158 us -> none  [the longest x1 113 us: body(): lax.all_gather(spectral_w.astype(BF), axes, axis=0, tiled=True)]
    reduce_scatter x3 -> x0, waiting for transfers between devices: 151 us -> none  [the longest x1 85.6 us: body(): lax.psum_scatter(gspec.reshape(4 * NB * BS, BS), axes, scatter_dimension=...]
    psum x1, waiting for transfers between devices: 61.9 us -> 0.01 us  [body(): gram = lax.psum(gram, chips)]
    unnamed x1 -> x0, blocking collectives: 40.9 us -> none
    pallas_call x2, Pallas kernels: 287 us -> 249 us  [feed(): pl.pallas_call(functools.partial(feed_kernel, high), grid=(steps,), in_sp...]
    pallas_call x4 -> x7, Pallas kernels: 433 us -> 471 us  [the longest x1 116 us: filter_backward(): pl.pallas_call(filter_back_kernel, in_specs=[SM] + [VM] * 13, out_specs=[...]
    ppermute x12 -> x15, waiting for transfers between devices: 41.4 us -> 67.7 us  [the longest x12 67.7 us: exchange(): moved.append(lax.ppermute(slabs[j], SP, [(i, i ^ j) for i in range(SPLIT)]))]
    unnamed x52 -> x37, local copies, waits for them, and re-layouts: 26.4 us -> 7.28 us
  transfers between devices with their start and end apart: 18 -> 18, of which waited for: 4 -> 3; matrix products, arithmetic and copies ran while one was open for 4% -> 1% of each run, Pallas kernels for 31% -> 56%
where the time goes in v2:
time: 908 us; the launch traced here: 906 us
  Pallas kernels  794 us (87%)
  waiting for transfers between devices  67.8 us (7%)
  between operations  14.9 us (2%)
  other arithmetic  11.5 us (1%)
  starting transfers between devices  11.3 us (1%)
    pallas_call x2, Pallas kernels, feed(): pl.pallas_call(functools.partial(feed_kernel, high), grid=(steps,), in_sp...  249 us
    pallas_call x1, Pallas kernels, filter_backward(): pl.pallas_call(filter_back_kernel, in_specs=[SM] + [VM] * 13, out_specs=[...  116 us
    pallas_call x1, Pallas kernels, reduce_feed(): pl.pallas_call(functools.partial(reduce_kernel, bits), in_specs=[ANY, ANY...  94.9 us
    pallas_call x1, Pallas kernels, filter_forward(): pl.pallas_call(filter_kernel, in_specs=[SM] + [VM] * 12, out_specs=[VM] *...  85.9 us
    pallas_call x1, Pallas kernels, newton_one(): pl.pallas_call(newton_kernel, in_specs=[VM] * 2, out_specs=VM, out_shape=...  70.6 us
    ppermute x12, waiting for transfers between devices, exchange(): moved.append(lax.ppermute(slabs[j], SP, [(i, i ^ j) for i in range(SPLIT)]))  67.7 us
    pallas_call x1, Pallas kernels, filter_backward_lo(): pl.pallas_call(filter_back_lo_kernel, in_specs=[VM] * 13, out_specs=[VM]...  40.4 us
    pallas_call x1, Pallas kernels, update_small(): pl.pallas_call(functools.partial(vectors_kernel, count), in_specs=[VM] *...  38.4 us
  transfers between devices with their start and end apart: 18, of which 3 were waited for; matrix products, arithmetic and copies ran while one was open for 1% of the time, Pallas kernels for 56%

profile of v2, /device:TPU:0, one launch (start us, length us, event | category | flops | bytes accessed | tf_op | source)
XLA Modules:
  0.0 906.3 jit_solution(1884662122073092422)
XLA Ops:
  7.2 24.8 %gather_small.1 = (f32[16,768]{1,0:T(8,128)}, bf16[4,192,384]{2,1,0:T(8,128)(2,1)}, bf16[4,192,384]{2,1,0:T(8,128)(2,1)}, bf16[4,384,384]{2,1,0:T(8,128)(2,1)}, f32[4,2,384]{2,1,0:T(2,128)}, /*index=5*/f32[6,512]{1,0:T(8,128)}) custom-call(f32[13,24]{1,0:T(8,128)} %vec_ref.3, f32[96,96]{1,0:T(8,128)} %spec_ref.1), custom_call_target="tpu_custom_call" | custom-call | flops 20000000000 | bytes 20000000 | tf_op jit(solution)/shard_map/gather_small/pallas_call | solution.py:1157
  32.0 0.7 convert_bitcast_fusion
  32.8 12.6 %norm_pack.1 = (bf16[45,48,384]{2,1,0:T(8,128)(2,1)}, bf16[45,48,384]{2,1,0:T(8,128)(2,1)}, bf16[45,48,384]{2,1,0:T(8,128)(2,1)}, bf16[45,48,384]{2,1,0:T(8,128)(2,1)}) custom-call(s32[1]{0:T(128)} %bitcast.own_ref, bf16[2,45,45,768]{3,2,1,0:T(8,128)(2,1)} %bitcast.32, f32[16,768]{1,0:T(8,128)} %get-tuple-element.80.vec_ref.refs_3_.refs_6_), custom_call_target="tpu_custom_call" | custom-call | flops 16000000000 | bytes 16000000 | tf_op jit(solution)/shard_map/norm_pack/pallas_call | solution.py:201
  45.4 1.8 collective-permute-start
  47.2 0.4 collective-permute-start.1
  47.6 1.0 collective-permute-start.2
  48.7 0.8 collective-permute-start.9
  49.5 0.7 convert_element_type.11
  50.2 26.8 %filter_forward_lo.1 = (bf16[45,24,768]{2,1,0:T(8,128)(2,1)}, bf16[4,2,576,192]{3,2,1,0:T(8,128)(2,1)}) custom-call(bf16[45,23,768]{2,1,0:T(8,128)(2,1)} %bitcast.36, f32[16,768]{1,0:T(8,128)} %get-tuple-element.80.vec_ref.refs_3_.refs_6_, bf16[24,24]{1,0:T(8,128)(2,1)} %constant.39.clone.tw, bf16[24,24]{1,0:T(8,128)(2,1)} %constant.40.clone.twt, ...), custom_call_target="tpu_custom_call" | custom-call | flops 35000000512 | bytes 35000000 | tf_op jit(solution)/shard_map/filter_forward_lo/pallas_call | solution.py:577
  77.7 0.1 broadcast_select_fusion.2
  77.7 0.9 pad_maximum_fusion.moment
  78.6 17.6 %collective-permute-done.1.x2 = bf16[45,48,384]{2,1,0:T(8,128)(2,1)} collective-permute-done((bf16[45,48,384]{2,1,0:T(8,128)(2,1)}, bf16[45,48,384]{2,1,0:T(8,128)(2,1)}, u32[]{:S(2)}, u32[]{:S(2)}) %collective-permute-start.1) | collective-permute-done | bytes 1658912 | tf_op jit(solution)/shard_map/ppermute | solution.py:217
  96.3 35.7 %collective-permute-done.2.x3 = bf16[45,48,384]{2,1,0:T(8,128)(2,1)} collective-permute-done((bf16[45,48,384]{2,1,0:T(8,128)(2,1)}, bf16[45,48,384]{2,1,0:T(8,128)(2,1)}, u32[]{:S(2)}, u32[]{:S(2)}) %collective-permute-start.2) | collective-permute-done | bytes 1658912 | tf_op jit(solution)/shard_map/ppermute | solution.py:217
  131.9 85.9 %filter_forward.1 = (bf16[45,48,384]{2,1,0:T(8,128)(2,1)}, bf16[45,48,384]{2,1,0:T(8,128)(2,1)}, bf16[45,48,384]{2,1,0:T(8,128)(2,1)}, bf16[45,48,384]{2,1,0:T(8,128)(2,1)}, bf16[13,2,672,192]{3,2,1,0:T(8,128)(2,1)}) custom-call(s32[1]{0:T(128)} %bitcast.own_ref, bf16[45,48,384]{2,1,0:T(8,128)(2,1)} %get-tuple-element.90.x0, ...), custom_call_target="tpu_custom_call" | custom-call | flops 95000002560 | bytes 95000000 | tf_op jit(solution)/shard_map/filter_forward/pallas_call | solution.py:420
  217.8 0.7 collective-permute-start.3
  218.6 0.2 collective-permute-start.4
  218.8 1.2 collective-permute-start.5
  220.0 57.4 %feed_lo.1 = (bf16[45,23,768]{2,1,0:T(8,128)(2,1)}, bf16[45,24,768]{2,1,0:T(8,128)(2,1)}, f32[2,3072,768]{2,1,0:T(8,128)}, f32[6,512]{1,0:T(8,128)}, f32[8,768]{1,0:T(8,128)}) custom-call(s32[1]{0:T(128)} %bitcast.own_ref, s32[1]{0:T(128)S(6)} %copy.43.live_ref, bf16[45,23,768]{2,1,0:T(8,128)(2,1)} %bitcast.37, bf16[45,23,768]{2,1,0:T(8,128)(2,1)} %bitcast.35, ...), custom_call_target="tpu_custom_call" | custom-call | flops 70000001024 | bytes 70000000 | tf_op jit(solution)/shard_map/feed_lo/pallas_call | solution.py:854
  277.4 14.3 %collective-permute-done.5.refs_5_ = bf16[45,48,384]{2,1,0:T(8,128)(2,1)} collective-permute-done((bf16[45,48,384]{2,1,0:T(8,128)(2,1)}, bf16[45,48,384]{2,1,0:T(8,128)(2,1)}, u32[]{:S(2)}, u32[]{:S(2)}) %collective-permute-start.5) | collective-permute-done | bytes 1658912 | tf_op jit(solution)/shard_map/ppermute | solution.py:217
  291.8 191.2 %feed_hi.1 = (bf16[2,45,45,768]{3,2,1,0:T(8,128)(2,1)}, bf16[45,48,384]{2,1,0:T(8,128)(2,1)}, bf16[45,48,384]{2,1,0:T(8,128)(2,1)}, bf16[45,48,384]{2,1,0:T(8,12...) custom-call(s32[1]{0:T(128)} %bitcast.own_ref, ...), custom_call_target="tpu_custom_call" | custom-call | flops 210000003072 | bytes 210000000 | tf_op jit(solution)/shard_map/feed_hi/pallas_call | solution.py:854
  483.0 0.9 collective-permute-start.6
  483.9 0.3 collective-permute-start.7
  484.2 1.1 collective-permute-start.8
  485.3 94.9 %reduce_feed.1 = (f32[192,768]{1,0:T(8,128)}, f32[192,768]{1,0:T(8,128)}, f32[768,768]{1,0:T(8,128)}) custom-call(f32[16,2,96,768]{3,2,1,0:T(8,128)} %bitcast.40, bf16[16,2,96,768]{3,2,1,0:T(8,128)(2,1)} %bitcast.42, f32[192,768]{1,0:T(8,128)} %pad_maximum_fusion.moment), custom_call_target="tpu_custom_call" | custom-call | flops 80000000000 | bytes 80000000 | tf_op jit(solution)/shard_map/reduce_feed/pallas_call | solution.py:1370
  580.2 1.8 slice_select_fusion.2
  582.1 1.1 copy-done.14
  583.2 0.5 copy-done.16
  583.8 116.1 %filter_backward.1 = (bf16[45,48,384]{2,1,0:T(8,128)(2,1)}, bf16[45,48,384]{2,1,0:T(8,128)(2,1)}, bf16[45,48,384]{2,1,0:T(8,128)(2,1)}, bf16[45,48,384]{2,1,0:T(...) custom-call(s32[1]{0:T(128)} %bitcast.own_ref, bf16[45,48,384]{2,1,0:T(8,128)(2,1)} %get-tuple-element.114.x0.m0, ...), custom_call_target="tpu_custom_call" | custom-call | flops 124999999488 | bytes 125000000 | tf_op jit(solution)/shard_map/filter_backward/pallas_call | solution.py:475
  699.8 0.5 collective-permute-start.10
  700.3 1.2 collective-permute-start.11
  701.5 0.3 collective-permute-start.12
  701.8 40.4 %filter_backward_lo.1 = (f32[6210,1,128]{2,1,0:T(1,128)}, f32[32,96,96]{2,1,0:T(8,128)}, f32[4,2,384]{2,1,0:T(2,128)}, f32[2,768]{1,0:T(2,128)}) custom-call(bf16[45,23,768]{2,1,0:T(8,128)(2,1)} %bitcast.38, bf16[45,24,768]{2,1,0:T(8,128)(2,1)} %get-tuple-element.126.gm_ref, bf16[4,2,576,192]{3,2,1,0:T(8,128)(2,1)} %get-tuple-element.127.four, ...), custom_call_target="tpu_custom_call" | custom-call | flops 44999999488 | bytes 45000000 | tf_op jit(solution)/shard_map/filter_backward_lo/pallas_call | solution.py:663
  742.2 70.6 %newton.1 = f32[192,768]{1,0:T(8,128)} custom-call(f32[768,768]{1,0:T(8,128)} %all-reduce.2.cloned.1.call-done.g_ref, f32[192,768]{1,0:T(8,128)} %get-tuple-element.113.x_ref), custom_call_target="tpu_custom_call" | custom-call | flops 60000002048 | bytes 60000000 | tf_op jit(solution)/shard_map/newton/pallas_call | solution.py:1001
  812.8 1.2 slice_select_fusion
  814.0 0.8 collective-permute-start.13
  814.8 1.8 broadcast_select_fusion
  816.6 0.8 select_subtract_fusion
  817.4 0.8 bitcast_subtract_fusion
  818.2 1.1 copy-done.10
  819.3 0.5 copy-done.11
  819.9 29.7 %norm_backward.1 = (f32[2,12150,1,128]{3,2,1,0:T(1,128)}, f32[2,768]{1,0:T(2,128)}) custom-call(s32[1]{0:T(128)} %bitcast.own_ref, bf16[2,45,45,768]{3,2,1,0:T(8,128)(2,1)} %bitcast.34, bf16[45,48,384]{2,1,0:T(8,128)(2,1)} %get-tuple-element.114.x0.m0, bf16[45,48,384]{2,1,0:T(8,128)(2,1)} %get-tuple-element.108.m1, ...), custom_call_target="tpu_custom_call" | custom-call | flops 22000001024 | bytes 22000000 | tf_op jit(solution)/shard_map/norm_backward/pallas_call | solution.py:910
  849.6 38.4 %update_small.1 = (f32[96,96]{1,0:T(8,128)}, f32[13,24]{1,0:T(8,128)}, f32[13,24]{1,0:T(8,128)}, f32[13,24]{1,0:T(8,128)}) custom-call(f32[8,4,96,96]{3,2,1,0:T(8,128)} %bitcast.45, f32[2,768]{1,0:T(2,128)} %get-tuple-element.136.gv_lo, f32[2,768]{1,0:T(2,128)} %get-tuple-element.137.gv_hi, f32[8,768]{1,0:T(8,128)} %get-tuple-element.138.gv, ...), custom_call_target="tpu_custom_call" | custom-call | flops 24999999488 | bytes 25000000 | tf_op jit(solution)/shard_map/update_small/pallas_call | solution.py:1261
  888.0 1.4 multiply_add_fusion
  889.5 4.7 newton_small.1
  894.2 1.4 multiply_subtract_fusion
  895.6 1.3 copy.44
  896.9 1.3 copy.45
  898.2 1.3 copy.46
  (53 shorter events, 0.3 us)
Async XLA Ops:
  7.2 24.8 %copy-start.6 = (f32[768,96]{0,1:T(8,128)S(1)}, f32[768,96]{0,1:T(8,128)}, u32[]{:S(2)}) copy-start(f32[768,96]{0,1:T(8,128)} %param.29) | copy-start | bytes 884740
  7.2 212.8 %all-gather.3.cloned.1.call-start = ((), (), s32[]{:S(2)}) async-start(), calls=%async_computation | async-start | bytes 4866048 | tf_op jit(solution)/shard_map/all_gather | solution.py:1413
  32.7 187.3 %all-gather.5.cloned.1.call-start = ((), (), s32[]{:S(2)}) async-start(), calls=%async_computation.1 | async-start | bytes 4866048 | tf_op jit(solution)/shard_map/all_gather | solution.py:1414
  32.8 15.9 %copy-start.2 = (f32[96,768]{1,0:T(8,128)S(1)}, f32[96,768]{1,0:T(8,128)}, u32[]{:S(2)}) copy-start(f32[96,768]{1,0:T(8,128)} %param.33) | copy-start | bytes 884740
  32.8 15.8 %copy-start.3 = (f32[768,96]{0,1:T(8,128)S(1)}, f32[768,96]{0,1:T(8,128)}, u32[]{:S(2)}) copy-start(f32[768,96]{0,1:T(8,128)} %param.32) | copy-start | bytes 884740
  32.8 16.7 %copy-start.4 = (f32[96,768]{1,0:T(8,128)S(1)}, f32[96,768]{1,0:T(8,128)}, u32[]{:S(2)}) copy-start(f32[96,768]{1,0:T(8,128)} %param.30) | copy-start | bytes 884740
  45.4 33.2 %collective-permute-start = (bf16[45,48,384]{2,1,0:T(8,128)(2,1)}, bf16[45,48,384]{2,1,0:T(8,128)(2,1)S(1)}, u32[]{:S(2)}, u32[]{:S(2)}) collective-permute-start(bf16[45,48,384]{2,1,0:T(8,128)(2,1)} %get-tuple-element.82), channel_id=1, source_target_pairs={{0,1},{1,0},{2,3},{3,2},{4,5},{5,4},{6,7},{7,6},{8,9},{9,8},{10,11... | collective-permute-start | bytes 4976648 | tf_op jit(solution)/shard_map/ppermute | solution.py:217
  47.2 49.0 %collective-permute-start.1 = (bf16[45,48,384]{2,1,0:T(8,128)(2,1)}, bf16[45,48,384]{2,1,0:T(8,128)(2,1)}, u32[]{:S(2)}, u32[]{:S(2)}) collective-permute-start(bf16[45,48,384]{2,1,0:T(8,128)(2,1)} %get-tuple-element.83), channel_id=1, source_target_pairs={{0,2},{1,3},{2,0},{3,1},{4,6},{5,7},{6,4},{7,5},{8,10},{9,11},{10,... | collective-permute-start | bytes 4976648 | tf_op jit(solution)/shard_map/ppermute | solution.py:217
  47.6 84.4 %collective-permute-start.2 = (bf16[45,48,384]{2,1,0:T(8,128)(2,1)}, bf16[45,48,384]{2,1,0:T(8,128)(2,1)}, u32[]{:S(2)}, u32[]{:S(2)}) collective-permute-start(bf16[45,48,384]{2,1,0:T(8,128)(2,1)} %get-tuple-element.84), channel_id=1, source_target_pairs={{0,3},{1,2},{2,1},{3,0},{4,7},{5,6},{6,5},{7,4},{8,11},{9,10},{10,... | collective-permute-start | bytes 4976648 | tf_op jit(solution)/shard_map/ppermute | solution.py:217
  48.7 29.0 %collective-permute-start.9 = (f32[96,768]{1,0:T(8,128)S(1)}, f32[96,768]{1,0:T(8,128)S(1)}, u32[]{:S(2)}, u32[]{:S(2)}) collective-permute-start(f32[96,768]{1,0:T(8,128)S(1)} %bitcast_select_fusion), channel_id=1, source_target_pairs={{0,1},{1,0},{2,3},{3,2},{4,5},{5,4},{6,7},{7,6},{8,9},{9,8},{10,11... | collective-permute-start | bytes 884744 | tf_op jit(solution)/shard_map/ppermute | solution.py:1024
  50.2 692.0 %all-reduce.2.cloned.1.call-start = ((), (), s32[]{:S(2)}) async-start(), calls=%async_computation.2 | async-start | bytes 4718592 | tf_op jit(solution)/shard_map/psum | solution.py:1438
  78.6 53.3 %copy-start.12 = (bf16[45,48,384]{2,1,0:T(8,128)(2,1)}, bf16[45,48,384]{2,1,0:T(8,128)(2,1)S(1)}, u32[]{:S(2)}) copy-start(bf16[45,48,384]{2,1,0:T(8,128)(2,1)S(1)} %collective-permute-done.x1) | copy-start | bytes 4976644
  217.8 59.5 %collective-permute-start.3 = (bf16[45,48,384]{2,1,0:T(8,128)(2,1)}, bf16[45,48,384]{2,1,0:T(8,128)(2,1)S(1)}, u32[]{:S(2)}, u32[]{:S(2)}) collective-permute-start(bf16[45,48,384]{2,1,0:T(8,128)(2,1)} %get-tuple-element.95), channel_id=1, source_target_pairs={{0,1},{1,0},{2,3},{3,2},{4,5},{5,4},{6,7},{7,6},{8,9},{9,8},{10,11... | collective-permute-start | bytes 4976648 | tf_op jit(solution)/shard_map/ppermute | solution.py:217
  218.6 58.8 %collective-permute-start.4 = (bf16[45,48,384]{2,1,0:T(8,128)(2,1)}, bf16[45,48,384]{2,1,0:T(8,128)(2,1)S(1)}, u32[]{:S(2)}, u32[]{:S(2)}) collective-permute-start(bf16[45,48,384]{2,1,0:T(8,128)(2,1)} %get-tuple-element.96), channel_id=1, source_target_pairs={{0,2},{1,3},{2,0},{3,1},{4,6},{5,7},{6,4},{7,5},{8,10},{9,11},{10,... | collective-permute-start | bytes 4976648 | tf_op jit(solution)/shard_map/ppermute | solution.py:217
  218.8 72.9 %collective-permute-start.5 = (bf16[45,48,384]{2,1,0:T(8,128)(2,1)}, bf16[45,48,384]{2,1,0:T(8,128)(2,1)}, u32[]{:S(2)}, u32[]{:S(2)}) collective-permute-start(bf16[45,48,384]{2,1,0:T(8,128)(2,1)} %get-tuple-element.97), channel_id=1, source_target_pairs={{0,3},{1,2},{2,1},{3,0},{4,7},{5,6},{6,5},{7,4},{8,11},{9,10},{10,... | collective-permute-start | bytes 4976648 | tf_op jit(solution)/shard_map/ppermute | solution.py:217
  277.4 14.4 %copy-start.13 = (bf16[45,48,384]{2,1,0:T(8,128)(2,1)}, bf16[45,48,384]{2,1,0:T(8,128)(2,1)S(1)}, u32[]{:S(2)}) copy-start(bf16[45,48,384]{2,1,0:T(8,128)(2,1)S(1)} %collective-permute-done.3.refs_3_) | copy-start | bytes 4976644
  277.4 14.3 %copy-start.15 = (bf16[45,48,384]{2,1,0:T(8,128)(2,1)}, bf16[45,48,384]{2,1,0:T(8,128)(2,1)S(1)}, u32[]{:S(2)}) copy-start(bf16[45,48,384]{2,1,0:T(8,128)(2,1)S(1)} %collective-permute-done.4.refs_4_) | copy-start | bytes 4976644
  483.0 99.0 %collective-permute-start.6 = (bf16[45,48,384]{2,1,0:T(8,128)(2,1)}, bf16[45,48,384]{2,1,0:T(8,128)(2,1)S(1)}, u32[]{:S(2)}, u32[]{:S(2)}) collective-permute-start(bf16[45,48,384]{2,1,0:T(8,128)(2,1)} %get-tuple-element.108.m1), channel_id=1, source_target_pairs={{0,1},{1,0},{2,3},{3,2},{4,5},{5,4},{6,7},{7,6},{8,9},{9,8},{10,11... | collective-permute-start | bytes 4976648 | tf_op jit(solution)/shard_map/ppermute | solution.py:217
  483.9 98.2 %collective-permute-start.7 = (bf16[45,48,384]{2,1,0:T(8,128)(2,1)}, bf16[45,48,384]{2,1,0:T(8,128)(2,1)S(1)}, u32[]{:S(2)}, u32[]{:S(2)}) collective-permute-start(bf16[45,48,384]{2,1,0:T(8,128)(2,1)} %get-tuple-element.109.m2), channel_id=1, source_target_pairs={{0,2},{1,3},{2,0},{3,1},{4,6},{5,7},{6,4},{7,5},{8,10},{9,11},{10,... | collective-permute-start | bytes 4976648 | tf_op jit(solution)/shard_map/ppermute | solution.py:217
  484.2 97.9 %collective-permute-start.8 = (bf16[45,48,384]{2,1,0:T(8,128)(2,1)}, bf16[45,48,384]{2,1,0:T(8,128)(2,1)}, u32[]{:S(2)}, u32[]{:S(2)}) collective-permute-start(bf16[45,48,384]{2,1,0:T(8,128)(2,1)} %get-tuple-element.110.m3), channel_id=1, source_target_pairs={{0,3},{1,2},{2,1},{3,0},{4,7},{5,6},{6,5},{7,4},{8,11},{9,10},{10,... | collective-permute-start | bytes 4976648 | tf_op jit(solution)/shard_map/ppermute | solution.py:217
  582.0 232.8 %collective-permute-start.14 = (f32[96,768]{1,0:T(8,128)}, f32[96,768]{1,0:T(8,128)}, u32[]{:S(2)}, u32[]{:S(2)}) collective-permute-start(f32[96,768]{1,0:T(8,128)} %slice_select_fusion.2), channel_id=1, source_target_pairs={{0,1},{1,0},{2,3},{3,2},{4,5},{5,4},{6,7},{7,6},{8,9},{9,8},{10,11... | collective-permute-start | bytes 884744 | tf_op jit(solution)/shard_map/ppermute | solution.py:1033
  582.0 1.2 copy-start.14
  582.1 1.7 copy-start.16
  699.8 118.3 %collective-permute-start.10 = (bf16[45,48,384]{2,1,0:T(8,128)(2,1)}, bf16[45,48,384]{2,1,0:T(8,128)(2,1)S(1)}, u32[]{:S(2)}, u32[]{:S(2)}) collective-permute-start(bf16[45,48,384]{2,1,0:T(8,128)(2,1)} %get-tuple-element.120), channel_id=1, source_target_pairs={{0,1},{1,0},{2,3},{3,2},{4,5},{5,4},{6,7},{7,6},{8,9},{9,8},{10,11... | collective-permute-start | bytes 4976648 | tf_op jit(solution)/shard_map/ppermute | solution.py:217
  700.3 117.8 %collective-permute-start.11 = (bf16[45,48,384]{2,1,0:T(8,128)(2,1)}, bf16[45,48,384]{2,1,0:T(8,128)(2,1)S(1)}, u32[]{:S(2)}, u32[]{:S(2)}) collective-permute-start(bf16[45,48,384]{2,1,0:T(8,128)(2,1)} %get-tuple-element.121), channel_id=1, source_target_pairs={{0,2},{1,3},{2,0},{3,1},{4,6},{5,7},{6,4},{7,5},{8,10},{9,11},{10,... | collective-permute-start | bytes 4976648 | tf_op jit(solution)/shard_map/ppermute | solution.py:217
  701.5 116.7 %collective-permute-start.12 = (bf16[45,48,384]{2,1,0:T(8,128)(2,1)}, bf16[45,48,384]{2,1,0:T(8,128)(2,1)}, u32[]{:S(2)}, u32[]{:S(2)}) collective-permute-start(bf16[45,48,384]{2,1,0:T(8,128)(2,1)} %get-tuple-element.122), channel_id=1, source_target_pairs={{0,3},{1,2},{2,1},{3,0},{4,7},{5,6},{6,5},{7,4},{8,11},{9,10},{10,... | collective-permute-start | bytes 4976648 | tf_op jit(solution)/shard_map/ppermute | solution.py:217
  742.2 72.6 %copy-start.1 = (f32[192,768]{1,0:T(8,128)S(1)}, f32[192,768]{1,0:T(8,128)}, u32[]{:S(2)}) copy-start(f32[192,768]{1,0:T(8,128)} %get-tuple-element.143) | copy-start | bytes 1769476
  812.8 3.8 copy-start
  812.8 3.8 copy-start.5
  814.0 3.4 copy-start.7
  814.0 2.6 collective-permute-start.13
  818.2 1.2 copy-start.10
  818.2 1.7 copy-start.11
  849.6 38.4 %copy-start.8 = (f32[96,96]{1,0:T(8,128)S(1)}, f32[96,96]{1,0:T(8,128)}, u32[]{:S(2)}) copy-start(f32[96,96]{1,0:T(8,128)} %param.31) | copy-start | bytes 110596
  849.6 44.6 %copy-start.9 = (f32[96,96]{1,0:T(8,128)S(1)}, f32[96,96]{1,0:T(8,128)}, u32[]{:S(2)}) copy-start(f32[96,96]{1,0:T(8,128)} %spec_ref.1) | copy-start | bytes 110596
Sparse Core Ops, SparseCore 0:
  32.8 74.2 all-gather.2
  110.6 62.4 all-gather.4
  582.1 129.3 all-reduce.1

commit v3 on v2

--- a/solution.py
+++ b/solution.py
@@ -56,11 +56,11 @@
 LROWS = LK * PW
 HB = 5
 LB = 15
-FC = 512
+FC = 768
 NC = FF // FC
 VMEM_LIMIT = 60 * 2**20
-UNROLL = 5
-CHUNK = 48
+UNROLL = 9
+PITCH = 56
 
 
 def wave(length, rows, cols):
@@ -182,33 +182,32 @@
 WIDE_BLOCK = pl.BlockSpec((2, HB, OWN, D), lambda i: (0, i, 0, 0))
 
 
-def pack_kernel(own_ref, x_ref, vec_ref, o0, o1, o2, o3, fs):
+def pack_kernel(own_ref, x_ref, o0, o1, o2, o3, fs):
     own = own_ref[0]
-    gain, shift = vec_ref[0:1, :], vec_ref[1:2, :]
 
     for i in range(HB):
         rows = []
         for part in range(2):
             norm, _unused = normed(x_ref[part, i].astype(F32))
-            rows.append(pad_rows(norm * gain + shift))
+            rows.append(pad_rows(norm))
         pack_pair(rows[0], rows[1], fs.at[i])
     for i in range(HB):
         for j, out in enumerate((o0, o1, o2, o3)):
             out[i] = fs[i, own ^ j]
 
 
-def norm_packed(own, samples, vectors):
+def norm_packed(own, samples):
     return pl.pallas_call(
         pack_kernel,
         grid=(HALF // HB,),
-        in_specs=[SM, WIDE_BLOCK, VM],
+        in_specs=[SM, WIDE_BLOCK],
         out_specs=[PACKED_BLOCK] * SPLIT,
         out_shape=[shape(PACKED, BF)] * SPLIT,
         scratch_shapes=[pltpu.VMEM((HB, SPLIT, PW, PAIR), BF)],
         compiler_params=params(),
         name="norm_pack",
         cost_estimate=cost(16),
-    )(own, samples, vectors)
+    )(own, samples)
 
 
 def exchange(slabs):
@@ -218,19 +217,21 @@
     return moved
 
 
-def to_freq_wide(slabs, table, space):
+def to_freq_wide(slabs, table, space, lead=None):
     def one(i):
         rows = jnp.concatenate([slab[i] for slab in slabs], axis=0)
+        if lead is not None:
+            rows = (rows.astype(F32) * lead[0:1, :] + lead[1:2, :]).astype(BF)
         area = dot(table[...], rows)
         for c in range(3):
-            space[c, pl.ds(i, 2 * KP, stride=PW), :] = area[:, c * 128 : (c + 1) * 128]
+            space[c, pl.ds(i, 2 * KP, stride=PITCH), :] = area[:, c * 128 : (c + 1) * 128]
 
     loop(HALF, UNROLL, one)
 
 
 def to_freq_tall(k, table, space):
-    re = lanes(*[space[c, pl.ds(pl.multiple_of(k * PW, PW), PW), :] for c in range(3)])
-    im = lanes(*[space[c, pl.ds(pl.multiple_of((KP + k) * PW, PW), PW), :] for c in range(3)])
+    re = lanes(*[space[c, pl.ds(pl.multiple_of(k * PITCH, 8), PW), :] for c in range(3)])
+    im = lanes(*[space[c, pl.ds(pl.multiple_of((KP + k) * PITCH, 8), PW), :] for c in range(3)])
     rows = jnp.concatenate([re[:, :GD], re[:, GD:], im[:, :GD], im[:, GD:]], axis=0)
     return dot(table[...], rows.astype(BF))
 
@@ -240,14 +241,14 @@
     for part in range(2):
         base = part * PM
         packed = lanes(back[base : base + PW], back[base + PW : base + PM])
-        at = pl.ds(pl.multiple_of((part * KP + k) * PW, PW), PW)
+        at = pl.ds(pl.multiple_of((part * KP + k) * PITCH, 8), PW)
         for c in range(3):
             space[c, at, :] = packed[:, c * 128 : (c + 1) * 128]
 
 
 def to_space_wide(table, space, outs):
     def one(i):
-        rows = lanes(*[space[c, pl.ds(i, 2 * KP, stride=PW), :] for c in range(3)])
+        rows = lanes(*[space[c, pl.ds(i, 2 * KP, stride=PITCH), :] for c in range(3)])
         field = dot(table[...], rows.astype(BF)).astype(BF)
         for j, out in enumerate(outs):
             out[i] = field[j * PW : (j + 1) * PW]
@@ -255,13 +256,10 @@
     loop(HALF, UNROLL, one)
 
 
-def clear(ref):
-    def one(i, _):
-        for c in range(ref.shape[0]):
-            ref[c, pl.ds(pl.multiple_of(i * 96, 96), 96), :] = jnp.zeros((96, 128), F32)
-        return 0
-
-    lax.fori_loop(0, ref.shape[1] // 96, one, 0)
+def clear_pads(space, used, count):
+    for c in range(space.shape[0]):
+        for row in range(used, PW):
+            space[c, pl.ds(row, count, stride=PITCH), :] = jnp.zeros((count, 128), F32)
 
 
 def keep_minus(row, width, first, last):
@@ -271,12 +269,14 @@
 
 def mlp_forward(fre, fim, wu, wv, w1, bias, us, vs, actp, actm, put, base, first, last, chunk):
     rows = us.shape[0]
-    us[...] = dot(fre, wu)
-    vs[...] = dot(fim, wv)
+    cuts = [slice(i * chunk, (i + 1) * chunk) for i in range(rows // chunk)]
+    for at in cuts:
+        us[at, :] = dot(fre[at, :], wu)
+        vs[at, :] = dot(fim[at, :], wv)
     b0, b1 = bias[0:1, :], bias[1:2, :]
 
     def act(i, _):
-        at = pl.ds(pl.multiple_of(i * chunk, chunk), chunk)
+        at = slice(i * chunk, (i + 1) * chunk)
         u = us[at, :] + b0
         v = vs[at, :]
         for ref, value in ((actp, u + v), (actm, u - v)):
@@ -284,12 +284,14 @@
             ref[at, :] = (value * (0.5 + 0.5 * t)).astype(BF)
         return 0
 
-    lax.fori_loop(0, rows // chunk, act, 0)
-    us[...] = dot(actp[...], w1)
-    vs[...] = dot(actm[...], w1)
+    for i in range(rows // chunk):
+        act(i, 0)
+    for at in cuts:
+        us[at, :] = dot(actp[at, :], w1)
+        vs[at, :] = dot(actm[at, :], w1)
 
     def shrunk(i, _):
-        at = pl.ds(pl.multiple_of(i * chunk, chunk), chunk)
+        at = slice(i * chunk, (i + 1) * chunk)
         p = us[at, :] + b1
         m = vs[at, :] + b1
         p = p - shrink_level * jnp.tanh(shrink_sharp * p)
@@ -299,7 +301,8 @@
         put(at, (p[:, :GD] + m[:, :GD]).astype(BF), (p[:, GD:] - m[:, GD:]).astype(BF))
         return 0
 
-    lax.fori_loop(0, rows // chunk, shrunk, 0)
+    for i in range(rows // chunk):
+        shrunk(i, 0)
 
 
 def mlp_backward(
@@ -313,7 +316,7 @@
     sign = jnp.where(lax.broadcasted_iota(jnp.int32, (1, PAIR), 1) < GD, 1.0, -1.0).astype(F32)
 
     def act(i, _):
-        at = pl.ds(pl.multiple_of(i * chunk, chunk), chunk)
+        at = slice(i * chunk, (i + 1) * chunk)
         u = us[at, :] + b0
         v = vs[at, :]
         for ref, slope, value in ((actp, dp, u + v), (actm, dm, u - v)):
@@ -324,12 +327,13 @@
             slope[at, :] = hp + on * (1.0 - hp) * (2.0 * K0 + 6.0 * K1 * square)
         return 0
 
-    lax.fori_loop(0, rows // chunk, act, 0)
+    for i in range(rows // chunk):
+        act(i, 0)
     us[...] = dot(actp[...], w1)
     vs[...] = dot(actm[...], w1)
 
     def second(i, total):
-        at = pl.ds(pl.multiple_of(i * chunk, chunk), chunk)
+        at = slice(i * chunk, (i + 1) * chunk)
         grad = gs[at, :]
         tp = jnp.tanh(shrink_sharp * (us[at, :] + b1))
         tm = jnp.tanh(shrink_sharp * (vs[at, :] + b1))
@@ -343,13 +347,16 @@
         gsm[at, :] = m.astype(BF)
         return total + jnp.sum(p + m, axis=0, keepdims=True)
 
-    ge[1:2, :] += lax.fori_loop(0, rows // chunk, second, jnp.zeros((1, PAIR), F32))
+    total = jnp.zeros((1, PAIR), F32)
+    for i in range(rows // chunk):
+        total = second(i, total)
+    ge[1:2, :] += total
     us[...] = dot_nt(gsp[...], w1)
     vs[...] = dot_nt(gsm[...], w1)
     gw1[...] += dot_tn(actp[...], gsp[...]) + dot_tn(actm[...], gsm[...])
 
     def first_grad(i, total):
-        at = pl.ds(pl.multiple_of(i * chunk, chunk), chunk)
+        at = slice(i * chunk, (i + 1) * chunk)
         p = us[at, :] * dp[at, :]
         m = vs[at, :] * dm[at, :]
         both = p + m
@@ -357,7 +364,10 @@
         gsm[at, :] = (p - m).astype(BF)
         return total + jnp.sum(both, axis=0, keepdims=True)
 
-    ge[0:1, :] += lax.fori_loop(0, rows // chunk, first_grad, jnp.zeros((1, PAIR), F32))
+    total = jnp.zeros((1, PAIR), F32)
+    for i in range(rows // chunk):
+        total = first_grad(i, total)
+    ge[0:1, :] += total
     gwu[...] += dot_tn(fre, gsp[...])
     gwv[...] += dot_tn(fim, gsm[...])
     put(dot_nt(gsp[...], wu).astype(BF), dot_nt(gsm[...], wv).astype(BF))
@@ -376,12 +386,12 @@
 
 
 def filter_kernel(
-    own_ref, x0, x1, x2, x3, tw, twt, th, tht, wu, wv, w1, bias,
+    own_ref, x0, x1, x2, x3, tw, twt, th, tht, wu, wv, w1, bias, lead,
     y0, y1, y2, y3, four, space, us, vs, actp, actm, zr, zi,
 ):
     own = own_ref[0]
-    clear(space)
-    to_freq_wide((x0, x1, x2, x3), tw.at[own], space)
+    clear_pads(space, HALF, 2 * KP)
+    to_freq_wide((x0, x1, x2, x3), tw.at[own], space, lead.at[own])
 
     def group(g, _):
         for n in range(KG):
@@ -395,7 +405,7 @@
 
         mlp_forward(
             four[g, 0], four[g, 1], wu[own], wv[own], w1[own], bias.at[own], us, vs, actp, actm, put,
-            g * ROWS, PM, (KF - 1) * PM, CHUNK,
+            g * ROWS, PM, (KF - 1) * PM, ROWS // 3,
         )
         for n in range(KG):
             at = slice(n * PM, (n + 1) * PM)
@@ -415,28 +425,28 @@
     return big, low, part
 
 
-def filter_forward(own, slabs, tabs, weights, bias):
+def filter_forward(own, slabs, tabs, weights, bias, lead):
     big, low, part = filter_scratch(ROWS, None)
     outs = pl.pallas_call(
         filter_kernel,
-        in_specs=[SM] + [VM] * 12,
+        in_specs=[SM] + [VM] * 13,
         out_specs=[VM] * 5,
         out_shape=[shape(PACKED, BF)] * SPLIT + [shape((GROUPS, 2, ROWS, GD), BF)],
-        scratch_shapes=[pltpu.VMEM((3, 2 * KP * PW, 128), F32), big, big, low, low, part, part],
+        scratch_shapes=[pltpu.VMEM((3, 2 * KP * PITCH, 128), F32), big, big, low, low, part, part],
         compiler_params=params(),
         name="filter_forward",
         cost_estimate=cost(95),
-    )(own, *slabs, *tabs, *weights, bias)
+    )(own, *slabs, *tabs, *weights, bias, lead)
     return outs[:SPLIT], outs[SPLIT]
 
 
 def filter_back_kernel(
-    own_ref, x0, x1, x2, x3, four, tw, twt, th, tht, wu, wv, w1, bias,
+    own_ref, x0, x1, x2, x3, four, tw, twt, th, tht, wu, wv, w1, bias, grads_in,
     y0, y1, y2, y3, grads, ge,
     space, us, vs, actp, actm, zr, zi, gs, dp, dm, gsp, gsm, gwu, gwv, gw1,
 ):
     own = own_ref[0]
-    clear(space)
+    clear_pads(space, HALF, 2 * KP)
     gwu[...] = jnp.zeros_like(gwu)
     gwv[...] = jnp.zeros_like(gwv)
     gw1[...] = jnp.zeros_like(gw1)
@@ -454,7 +464,7 @@
 
         mlp_backward(
             four[g, 0], four[g, 1], gs, wu[own], wv[own], w1[own], bias.at[own], us, vs, actp, actm, dp, dm,
-            gsp, gsm, None, put, gwu, gwv, gw1, ge, g * ROWS, PM, (KF - 1) * PM, CHUNK,
+            gsp, gsm, None, put, gwu, gwv, gw1, ge, g * ROWS, PM, (KF - 1) * PM, ROWS // 2,
         )
         for n in range(KG):
             at = slice(n * PM, (n + 1) * PM)
@@ -464,41 +474,41 @@
         return 0
 
     lax.fori_loop(0, GROUPS, group, 0)
-    grads[...] = jnp.zeros_like(grads)
+    grads[...] = grads_in[...]
     for (layer, part, b), value in block_grads(gwu, gwv, gw1).items():
-        grads[(2 * layer + part) * NB + 2 * own + b] = value
+        grads[(2 * layer + part) * NB + 2 * own + b] += value
     to_space_wide(twt.at[own], space, (y0, y1, y2, y3))
 
 
-def filter_backward(own, slabs, four, tabs, weights, bias):
+def filter_backward(own, slabs, four, tabs, weights, bias, grads_in):
     big, low, part = filter_scratch(ROWS, None)
     outs = pl.pallas_call(
         filter_back_kernel,
-        in_specs=[SM] + [VM] * 13,
+        in_specs=[SM] + [VM] * 14,
         out_specs=[VM] * 6,
         out_shape=[shape(PACKED, BF)] * SPLIT
         + [shape((4 * NB, BS, BS), F32), shape((2, PAIR), F32)],
-        scratch_shapes=[pltpu.VMEM((3, 2 * KP * PW, 128), F32), big, big, low, low, part, part]
+        scratch_shapes=[pltpu.VMEM((3, 2 * KP * PITCH, 128), F32), big, big, low, low, part, part]
         + [big, big, big, low, low]
         + [pltpu.VMEM((GD, PAIR), F32)] * 2
         + [pltpu.VMEM((PAIR, PAIR), F32)],
         compiler_params=params(),
         name="filter_backward",
         cost_estimate=cost(125),
-    )(own, *slabs, four, *tabs, *weights, bias)
+    )(own, *slabs, four, *tabs, *weights, bias, grads_in)
     return outs[:SPLIT], outs[SPLIT], outs[SPLIT + 1]
 
 
 def lo_freq_wide(i, rows, table, space):
     area = dot(table[...], rows)
     for c in range(6):
-        space[c, pl.ds(i, 2 * LK, stride=PW), :] = area[:, c * 128 : (c + 1) * 128]
+        space[c, pl.ds(i, 2 * LK, stride=PITCH), :] = area[:, c * 128 : (c + 1) * 128]
 
 
 def lo_freq_tall(k, table, space):
     parts = []
     for base in (0, LK):
-        at = pl.ds(pl.multiple_of((base + k) * PW, PW), PW)
+        at = pl.ds(pl.multiple_of((base + k) * PITCH, 8), PW)
         parts.append(lanes(*[space[c, at, :] for c in range(6)]))
     rows = dot(table[...], jnp.concatenate(parts, axis=0).astype(BF))
     return rows[:PW], rows[PW:]
@@ -507,13 +517,13 @@
 def lo_space_tall(k, table, re, im, space):
     back = dot(table[...], jnp.concatenate([re, im], axis=0).astype(BF))
     for part, base in enumerate((0, LK)):
-        at = pl.ds(pl.multiple_of((base + k) * PW, PW), PW)
+        at = pl.ds(pl.multiple_of((base + k) * PITCH, 8), PW)
         for c in range(6):
             space[c, at, :] = back[part * PW : (part + 1) * PW, c * 128 : (c + 1) * 128]
 
 
 def lo_space_wide(i, table, space):
-    rows = lanes(*[space[c, pl.ds(i, 2 * LK, stride=PW), :] for c in range(6)])
+    rows = lanes(*[space[c, pl.ds(i, 2 * LK, stride=PITCH), :] for c in range(6)])
     return dot(table[...], rows.astype(BF))
 
 
@@ -521,7 +531,7 @@
     x_ref, vec_ref, tw, twt, th, tht, wu, wv, w1, bias, y_ref, four,
     space, us, vs, actp, actm, zr, zi,
 ):
-    clear(space)
+    clear_pads(space, WL, 2 * LK)
     gain, shift = vec_ref[0:1, :], vec_ref[1:2, :]
 
     def wide(i):
@@ -547,7 +557,7 @@
 
         mlp_forward(
             four[g, 0], four[g, 1], wu[g], wv[g], w1[g], bias.at[g], us, vs, actp, actm, put,
-            0, PW, LROWS, CHUNK,
+            0, PW, LROWS, LROWS // 3,
         )
         return 0
 
@@ -570,7 +580,7 @@
 def lo_scratch():
     big, low, _ = filter_scratch(LROWS, None)
     part = pltpu.VMEM((SPLIT, LROWS, GD), BF)
-    return [pltpu.VMEM((6, 2 * LK * PW, 128), F32), big, big, low, low, part, part]
+    return [pltpu.VMEM((6, 2 * LK * PITCH, 128), F32), big, big, low, low, part, part]
 
 
 def filter_forward_lo(samples, vectors, tabs, weights, bias):
@@ -587,11 +597,11 @@
 
 
 def filter_back_lo_kernel(
-    x_ref, gm_ref, four, vec_ref, tw, twt, th, tht, wu, wv, w1, bias, grads_in,
+    x_ref, gm_ref, four, vec_ref, tw, twt, th, tht, wu, wv, w1, bias,
     grad_ref, grads, ge, gvec,
     space, us, vs, actp, actm, zr, zi, gs, dp, dm, gsp, gsm, gwu, gwv, gw1,
 ):
-    clear(space)
+    clear_pads(space, WL, 2 * LK)
     ge[...] = jnp.zeros_like(ge)
     gvec[...] = jnp.zeros_like(gvec)
 
@@ -620,11 +630,11 @@
 
         mlp_backward(
             four[g, 0], four[g, 1], gs.at[g], wu[g], wv[g], w1[g], bias.at[g], us, vs, actp, actm,
-            dp, dm, gsp, gsm, None, put, gwu, gwv, gw1, ge.at[g], 0, PW, LROWS, CHUNK,
+            dp, dm, gsp, gsm, None, put, gwu, gwv, gw1, ge.at[g], 0, PW, LROWS, LROWS // 2,
         )
         for (layer, part, b), value in block_grads(gwu, gwv, gw1).items():
             at = (2 * layer + part) * NB + 2 * g + b
-            grads[at] = grads_in[at] + value
+            grads[at] = value
         return 0
 
     lax.fori_loop(0, SPLIT, group, 0)
@@ -658,11 +668,11 @@
     lax.fori_loop(0, WL // UNROLL, last, 0)
 
 
-def filter_backward_lo(samples, grad_mixed, four, vectors, tabs, weights, bias, grads_in):
+def filter_backward_lo(samples, grad_mixed, four, vectors, tabs, weights, bias):
     big, low, _ = filter_scratch(LROWS, None)
     return pl.pallas_call(
         filter_back_lo_kernel,
-        in_specs=[VM] * 13,
+        in_specs=[VM] * 12,
         out_specs=[VM] * 4,
         out_shape=[
             shape((HL * WL * 6, 1, 128), F32),
@@ -677,17 +687,19 @@
         compiler_params=params(),
         name="filter_backward_lo",
         cost_estimate=cost(45),
-    )(samples, grad_mixed, four, vectors, *tabs, *weights, bias, grads_in)
-
-
-def feed_chunks(n2, cots, c1_ref, win, wout, out_acc, gn_acc, gw, gc1):
+    )(samples, grad_mixed, four, vectors, *tabs, *weights, bias)
+
+
+def feed_chunks(n2, cots, c1_ref, wts, out_acc, gn_acc, gw, gc1):
     out_acc[...] = jnp.zeros_like(out_acc)
     gn_acc[...] = jnp.zeros_like(gn_acc)
 
     def chunk(c, _):
         rows = pl.ds(c * FC, FC)
         low, cot = n2[...].reshape(-1, D), cots[...].reshape(-1, D)
-        wi, wo = win[rows, :], wout[rows, :]
+        half, part = divmod(c * FC, FF // 2)
+        blocks = slice(part // wts.shape[3], (part + FC) // wts.shape[3])
+        wi, wo = (wts[half, blocks, m].reshape(FC, D) for m in range(2))
         hidden = dot_nt(low, wi) + c1_ref[pl.ds(c, 1), :]
         grad = dot_nt(cot, wo)
         square = hidden * hidden
@@ -712,7 +724,8 @@
     x_ref, cot_ref = refs[:2]
     fields = refs[2 : 2 + count]
     rest = refs[2 + count :]
-    vec_ref, c1_ref, win, wout = rest[:4]
+    vec_ref, c1_ref = rest[:2]
+    weights_here, weights_there = rest[2:4]
     rest = rest[4:]
     if high:
         gw_in, gc1_in, gv_in = rest[:3]
@@ -724,11 +737,19 @@
     if high:
         give_out = rest[1]
         rest = rest[1:]
-    gc1, gv, gw, sem, mixed, n2, cots, out_acc, gn_acc, fs = rest[1:]
+    gc1, gv, wts, wsem, gw, sem, mixed, n2, cots, out_acc, gn_acc, fs = rest[1:]
     step = pl.program_id(0)
+
+    side = lax.rem(own_ref[0], 2)
 
     @pl.when(step == 0)
     def _():
+        loads = [
+            pltpu.make_async_copy(weights_here, wts.at[side], wsem.at[0]),
+            pltpu.make_async_copy(weights_there, wts.at[1 - side], wsem.at[1]),
+        ]
+        for load in loads:
+            load.start()
         if high:
             load = pltpu.make_async_copy(gw_in, gw, sem)
             load.start()
@@ -739,6 +760,8 @@
             gw[...] = jnp.zeros_like(gw)
             gc1[...] = jnp.zeros_like(gc1)
             gv[...] = jnp.zeros_like(gv)
+        for load in loads:
+            load.wait()
 
     own = own_ref[0]
     tall = PW if high else LH
@@ -816,7 +839,7 @@
             add_sums()
 
     before()
-    feed_chunks(n2, cots, c1_ref, win, wout, out_acc, gn_acc, gw, gc1)
+    feed_chunks(n2, cots, c1_ref, wts, out_acc, gn_acc, gw, gc1)
     after()
 
     @pl.when(step == pl.num_programs(0) - 1)
@@ -839,7 +862,7 @@
             store.wait()
 
 
-def feed(high, own, live, samples, cotan, fields, vectors, bias_hidden, win, wout, earlier):
+def feed(high, own, live, samples, cotan, fields, vectors, bias_hidden, weights, earlier):
     planes, tall = (2 * HB, PW) if high else (LB, LH)
     tokens = planes * tall
     if high:
@@ -856,7 +879,7 @@
         grid=(steps,),
         in_specs=[SM, SM, wide, wide]
         + [packed] * count
-        + [VM] * 4
+        + [VM, VM, ANY, ANY]
         + ([ANY, VM, VM] if high else []),
         out_specs=[wide] + [packed] * count + ([ANY, VM] if high else [ANY]) + [VM, VM],
         out_shape=[shape(samples.shape, BF)]
@@ -864,6 +887,8 @@
         + ([shape((FF, D), F32), shape((FF, D), BF)] if high else [shape((2, FF, D), F32)])
         + [shape((NC, FC), F32), shape((8, D), F32)],
         scratch_shapes=[
+            pltpu.VMEM((2, *weights[0].shape), BF),
+            pltpu.SemaphoreType.DMA((2,)),
             pltpu.VMEM((2, FF, D), F32),
             pltpu.SemaphoreType.DMA,
             pltpu.VMEM((tokens, D), F32),
@@ -876,48 +901,7 @@
         compiler_params=params(),
         name="feed_hi" if high else "feed_lo",
         cost_estimate=cost(210 if high else 70),
-    )(own, live, samples, cotan, *fields, vectors, bias_hidden, win, wout, *earlier)
-
-
-def norm_back_kernel(own_ref, x_ref, m0, m1, m2, m3, f0, f1, f2, f3, vec_ref, grad_ref, gvec, fs, ms):
-    @pl.when(pl.program_id(0) == 0)
-    def _():
-        gvec[...] = jnp.zeros_like(gvec)
-
-    own = own_ref[0]
-    gain = vec_ref[0:1, :]
-
-    for i in range(HB):
-        for j, (m, f) in enumerate(((m0, f0), (m1, f1), (m2, f2), (m3, f3))):
-            ms[i, own ^ j] = m[i]
-            fs[i, own ^ j] = f[i]
-    sums = []
-    for i in range(HB):
-        for part, (direct, field) in enumerate(zip(unpack_pair(ms.at[i]), unpack_pair(fs.at[i]))):
-            direct, field = direct[:OWN], field[:OWN]
-            norm, scale = normed(x_ref[part, i].astype(F32))
-            grad = field + direct
-            sums.append((jnp.sum(grad * norm, axis=0, keepdims=True), jnp.sum(grad, axis=0, keepdims=True)))
-            value = direct + norm_back(grad, norm, scale, gain)
-            for c in range(6):
-                at = pl.ds(i * (6 * OWN) + c, OWN, stride=6)
-                grad_ref[part, at, 0, :] = value[:, c * 128 : (c + 1) * 128]
-    gvec[0:1, :] += sum(a for a, b in sums)
-    gvec[1:2, :] += sum(b for a, b in sums)
-
-
-def norm_backward(own, samples, direct, fields, vectors):
-    return pl.pallas_call(
-        norm_back_kernel,
-        grid=(HALF // HB,),
-        in_specs=[SM, WIDE_BLOCK] + [PACKED_BLOCK] * (2 * SPLIT) + [VM],
-        out_specs=[pl.BlockSpec((2, HB * OWN * 6, 1, 128), lambda i: (0, i, 0, 0)), VM],
-        out_shape=[shape((2, HALF * OWN * 6, 1, 128), F32), shape((2, D), F32)],
-        scratch_shapes=[pltpu.VMEM((HB, SPLIT, PW, PAIR), BF)] * 2,
-        compiler_params=params(),
-        name="norm_backward",
-        cost_estimate=cost(22),
-    )(own, samples, *direct, *fields, vectors)
+    )(own, live, samples, cotan, *fields, vectors, bias_hidden, *weights, *earlier)
 
 
 def eye_of(size):
@@ -956,9 +940,9 @@
     def one(i, _):
         at = pl.ds(pl.multiple_of(i * tile, tile), tile)
         top, middle, low = split_three(left[at, :])
-        total = dot(middle, parts[0]) + dot(top, parts[1])
+        total = dot(lanes(middle, top), parts[0:2].reshape(2 * size, size))
         if full:
-            total = total + (dot(middle, parts[1]) + dot(top, parts[2]) + dot(low, parts[0]))
+            total = total + dot(lanes(low, middle, top), parts[...].reshape(3 * size, size))
         total = total + dot(top, parts[0])
         out[at, :] = total if finish is None else finish(at, total)
         return 0
@@ -1035,16 +1019,7 @@
 
 
 def newton_small_kernel(x_ref, y_ref):
-    values = x_ref[...]
-    size = 1.0 / (jnp.sqrt(jnp.sum(values * values, keepdims=True)) + 1e-07)
-    values = values * size
-    for _ in range(NEWTON_STEPS):
-        gram = lax.dot_general(
-            values, values, (((0,), (0,)), ((), ())), precision=highest, preferred_element_type=F32
-        )
-        once = mul(values, gram)
-        values = newton_a * values + newton_b * once + newton_c * mul(once, gram)
-    y_ref[...] = values
+    y_ref[...] = newton_rows(x_ref[...])
 
 
 def newton_small(values):
@@ -1077,47 +1052,59 @@
     return dp, sp
 
 
-def send(source, target, out_sem, in_sem, device):
-    copy = pltpu.make_async_remote_copy(
+def remote_copy(source, target, out_sem, in_sem, device):
+    return pltpu.make_async_remote_copy(
         src_ref=source, dst_ref=target, send_sem=out_sem, recv_sem=in_sem, device_id=device,
         device_id_type=pl.DeviceIdType.MESH,
     )
+
+
+def send(source, target, out_sem, in_sem, device):
+    copy = remote_copy(source, target, out_sem, in_sem, device)
     copy.start()
     return copy
 
 
-def gather_kernel(
-    count, vec_ref, spec_ref, vec_out, wu, wv, w1, bias, c1,
-    vbuf, sbuf, send_v, recv_v, send_s, recv_s, send_w, recv_w, send_t, recv_t,
-):
-    rows, cols = spec_ref.shape[0], vec_ref.shape[1]
-    dp, sp = greet(count)
-    vbuf[sp, dp] = jnp.zeros(vbuf.shape[2:], F32)
-    vbuf[sp, dp, : vec_ref.shape[0], :cols] = vec_ref[...]
-    sbuf[sp, dp] = jnp.zeros(sbuf.shape[2:], BF)
-    sbuf[sp, dp, :, :BS] = spec_ref[...].astype(BF)
+def spread_out(count, dp, sp, jobs):
     copies = []
-    for o in range(1, count):
-        device = place(lax.rem(dp + o, count), sp)
-        here = vbuf.at[sp, dp]
-        copies.append(send(here, here, send_v.at[o], recv_v.at[o], device))
-        here = sbuf.at[sp, dp]
-        copies.append(send(here, here, send_s.at[o], recv_s.at[o], device))
-    for ref in (wu, wv, w1):
-        ref[...] = jnp.zeros_like(ref)
+    for buf, sems in jobs:
+        here = buf.at[sp, dp]
+        for o in range(1, count):
+            to = place(lax.rem(dp + o, count), sp)
+            copies.append(send(here, here, sems[0].at[o], sems[1].at[o], to))
     for copy in copies:
         copy.wait()
     copies = []
-    for j in range(1, SPLIT):
-        device = place(dp, sp ^ j)
-        copies.append(send(vbuf.at[sp], vbuf.at[sp], send_w.at[j], recv_w.at[j], device))
-        copies.append(send(sbuf.at[sp], sbuf.at[sp], send_t.at[j], recv_t.at[j], device))
+    for buf, sems in jobs:
+        for j in range(1, SPLIT):
+            here = buf.at[sp]
+            copies.append(send(here, here, sems[2].at[j], sems[3].at[j], place(dp, sp ^ j)))
     for copy in copies:
         copy.wait()
+
+
+def gather_kernel(count, vec_ref, spec_ref, vec_out, bias, lead, wu, wv, w1, buf, sbuf, *sems):
+    height, cols = vec_ref.shape
+    rows = spec_ref.shape[0]
+    dp, sp = greet(count)
+    buf[sp, dp] = jnp.zeros(buf.shape[2:], F32)
+    buf[sp, dp, :height, :cols] = vec_ref[...]
+    sbuf[sp, dp] = jnp.zeros(sbuf.shape[2:], BF)
+    sbuf[sp, dp, :, :BS] = spec_ref[...].astype(BF)
+    spread_out(count, dp, sp, [(buf, sems[:4]), (sbuf, sems[4:])])
+    for ref in (wu, wv, w1):
+        ref[...] = jnp.zeros_like(ref)
     for i in range(count * SPLIT):
-        vec_out[: vec_ref.shape[0], i * cols : (i + 1) * cols] = vbuf[
-            i % SPLIT, i // SPLIT, : vec_ref.shape[0], :cols
-        ]
+        vec_out[:height, i * cols : (i + 1) * cols] = buf[i % SPLIT, i // SPLIT, :height, :cols]
+    for g in range(SPLIT):
+        cut = slice(g * GD, (g + 1) * GD)
+        for layer in range(2):
+            row = 9 + 2 * layer
+            bias[g, layer : layer + 1, :GD] = vec_out[row : row + 1, cut]
+            bias[g, layer : layer + 1, GD:] = vec_out[row + 1 : row + 2, cut]
+            for part in (slice(GD), slice(GD, PAIR)):
+                lead[g, layer : layer + 1, part] = vec_out[layer : layer + 1, cut]
+    for i in range(count * SPLIT):
         value = sbuf[i % SPLIT, i // SPLIT][:, :BS]
         cell, off = divmod(i * rows, BS)
         layer, part, g, b = cell // 16, (cell // 8) % 2, (cell % 8) // 2, cell % 2
@@ -1136,76 +1123,68 @@
         else:
             w1[g, re, to_im] = value
             w1[g, im, to_re] = -value
-    for g in range(SPLIT):
-        cut = slice(g * GD, (g + 1) * GD)
-        for layer in range(2):
-            row = 9 + 2 * layer
-            bias[g, layer : layer + 1, :GD] = vec_out[row : row + 1, cut]
-            bias[g, layer : layer + 1, GD:] = vec_out[row + 1 : row + 2, cut]
-    for piece in range(12):
-        r, k = divmod(piece, 3)
-        c, m = divmod(piece, 2)
-        c1[c : c + 1, m * 256 : (m + 1) * 256] = vec_out[5 + r : 6 + r, k * 256 : (k + 1) * 256]
 
 
 def dma_sems(*counts):
     return [pltpu.SemaphoreType.DMA((n,)) for n in counts]
 
 
+def remote(number):
+    return pltpu.CompilerParams(
+        vmem_limit_bytes=VMEM_LIMIT, collective_id=number, has_side_effects=True
+    )
+
+
 def gather_small(count, vectors, spectral):
-    rows = spectral.shape[0]
     return pl.pallas_call(
         functools.partial(gather_kernel, count),
         in_specs=[VM] * 2,
         out_specs=[VM] * 6,
         out_shape=[
             shape((16, D), F32),
+            shape((SPLIT, 2, PAIR), F32),
+            shape((SPLIT, 2, PAIR), F32),
             shape((SPLIT, GD, PAIR), BF),
             shape((SPLIT, GD, PAIR), BF),
             shape((SPLIT, PAIR, PAIR), BF),
-            shape((SPLIT, 2, PAIR), F32),
-            shape((NC, FC), F32),
         ],
         scratch_shapes=[
             pltpu.VMEM((SPLIT, count, 16, 128), F32),
-            pltpu.VMEM((SPLIT, count, rows, 128), BF),
+            pltpu.VMEM((SPLIT, count, spectral.shape[0], 128), BF),
         ]
-        + dma_sems(count, count, count, count, SPLIT, SPLIT, SPLIT, SPLIT),
-        compiler_params=pltpu.CompilerParams(
-            vmem_limit_bytes=VMEM_LIMIT, collective_id=0, has_side_effects=True
-        ),
+        + dma_sems(count, count, SPLIT, SPLIT) * 2,
+        compiler_params=remote(0),
         name="gather_small",
-        cost_estimate=cost(20),
+        cost_estimate=cost(70),
     )(vectors, spectral)
 
 
-def scatter_sums(count, dp, sp, jobs):
+def scatter_near(dp, sp, x_ref, land, sems):
+    return [
+        remote_copy(
+            x_ref.at[:, sp ^ j], land.at[j - 1], sems[0].at[j], sems[1].at[j], place(dp, sp ^ j)
+        )
+        for j in range(1, SPLIT)
+    ]
+
+
+def scatter_far(count, dp, sp, total, land_two, sems):
     copies = []
-    for x_ref, land, total, land_two, (send_a, recv_a, send_b, recv_b) in jobs:
-        for j in range(1, SPLIT):
-            source = x_ref.at[:, sp ^ j]
-            copies.append(
-                send(source, land.at[j - 1], send_a.at[j], recv_a.at[j], place(dp, sp ^ j))
+    for o in range(1, count):
+        to = lax.rem(dp + o, count)
+        copies.append(
+            remote_copy(
+                total.at[to], land_two.at[o - 1], sems[2].at[o], sems[3].at[o], place(to, sp)
             )
-    for copy in copies:
-        copy.wait()
-    copies = []
-    for x_ref, land, total, land_two, (send_a, recv_a, send_b, recv_b) in jobs:
-        total[...] = (x_ref[:, sp] + land[0]) + (land[1] + land[2])
-        for o in range(1, count):
-            to = lax.rem(dp + o, count)
-            copies.append(
-                send(total.at[to], land_two.at[o - 1], send_b.at[o], recv_b.at[o], place(to, sp))
-            )
-    for copy in copies:
-        copy.wait()
-    results = []
-    for x_ref, land, total, land_two, sems in jobs:
-        result = total[dp]
-        for o in range(1, count):
-            result = result + land_two[o - 1]
-        results.append(result)
-    return results
+        )
+    return copies
+
+
+def scatter_total(count, dp, total, land_two):
+    result = total[dp]
+    for o in range(1, count):
+        result = result + land_two[o - 1]
+    return result
 
 
 def scatter_scratch(count, rows, width):
@@ -1216,21 +1195,76 @@
     ] + dma_sems(SPLIT, SPLIT, count, count)
 
 
+def spec_kernel(count, x_ref, out_ref, land, total, land_two, *sems):
+    dp, sp = greet(count)
+    copies = []
+    for o in range(1, count):
+        to = lax.rem(dp + o, count)
+        copies.append(
+            send(x_ref.at[to], land.at[o - 1], sems[0].at[o], sems[1].at[o], place(to, sp))
+        )
+    for copy in copies:
+        copy.wait()
+    value = x_ref[dp]
+    for o in range(1, count):
+        value = value + land[o - 1]
+    total[...] = value
+    copies = []
+    for j in range(1, SPLIT):
+        source = total.at[sp ^ j]
+        copies.append(
+            send(source, land_two.at[j - 1], sems[2].at[j], sems[3].at[j], place(dp, sp ^ j))
+        )
+    for copy in copies:
+        copy.wait()
+    out_ref[...] = (total[sp] + land_two[0]) + (land_two[1] + land_two[2])
+
+
+def scatter_spec(count, grads):
+    rows = 4 * NB * BS // (count * SPLIT)
+    return pl.pallas_call(
+        functools.partial(spec_kernel, count),
+        in_specs=[VM],
+        out_specs=VM,
+        out_shape=shape((rows, BS), F32),
+        scratch_shapes=[
+            pltpu.VMEM((count - 1, SPLIT, rows, BS), F32),
+            pltpu.VMEM((SPLIT, rows, BS), F32),
+            pltpu.VMEM((SPLIT - 1, rows, BS), F32),
+        ]
+        + dma_sems(count, count, SPLIT, SPLIT),
+        compiler_params=remote(4),
+        name="scatter_spec",
+        cost_estimate=cost(25),
+    )(grads.reshape(count, SPLIT, rows, BS))
+
+
+def newton_rows(values):
+    size = 1.0 / (jnp.sqrt(jnp.sum(values * values, keepdims=True)) + 1e-07)
+    values = values * size
+    for _ in range(NEWTON_STEPS):
+        gram = lax.dot_general(
+            values, values, (((0,), (0,)), ((), ())), precision=highest, preferred_element_type=F32
+        )
+        once = mul(values, gram)
+        values = newton_a * values + newton_b * once + newton_c * mul(once, gram)
+    return values
+
+
 def vectors_kernel(
-    count, gspec, gv_lo, gv_hi, gv, gc1, ge_lo, ge, vec_ref, first_ref, second_ref,
-    red_spec, new_vec, new_first, new_second, full, esum, x_ref, *scratch,
+    count, gv_lo, gv_hi, gv, gc1, ge_lo, ge, vec_ref, first_ref, second_ref,
+    red_spec, spec_ref, moment_ref,
+    new_vec, new_first, new_second, new_spec, new_moment,
+    full, esum, x_ref, land, total, land_two, *sems,
 ):
     height, cols = vec_ref.shape
     dp, sp = greet(count)
     full[...] = jnp.zeros_like(full)
     full[0:2, :] = gv_lo[...] + gv_hi[...]
     full[2:5, :] = gv[0:3, :]
+    full[5:9, :] = gc1[...]
     esum[...] = ge_lo[...]
     esum[sp] += ge[...]
-    for piece in range(12):
-        r, k = divmod(piece, 3)
-        c, m = divmod(piece, 2)
-        full[5 + r : 6 + r, k * 256 : (k + 1) * 256] = gc1[c : c + 1, m * 256 : (m + 1) * 256]
     for g in range(SPLIT):
         cut = slice(g * GD, (g + 1) * GD)
         for layer in range(2):
@@ -1240,11 +1274,25 @@
     x_ref[...] = jnp.zeros_like(x_ref)
     for i in range(count * SPLIT):
         x_ref[i // SPLIT, i % SPLIT, :, :cols] = full[:, i * cols : (i + 1) * cols]
-    jobs = [
-        (ref, *mine[:3], mine[3:]) for ref, mine in ((gspec, scratch[:7]), (x_ref, scratch[7:]))
-    ]
-    red_spec[...], grad = scatter_sums(count, dp, sp, jobs)
-    grad = grad[:height, :cols]
+    copies = scatter_near(dp, sp, x_ref, land, sems)
+    for copy in copies:
+        copy.start()
+    moment = momentum * moment_ref[...] + red_spec[...]
+    new_moment[...] = moment
+    push = red_spec[...] + momentum * moment
+    if red_spec.shape[0] == BS:
+        new_spec[...] = spec_ref[...] * (1.0 - muon_rate * decay) - muon_rate * newton_rows(push)
+    else:
+        new_spec[...] = push
+    for copy in copies:
+        copy.wait()
+    total[...] = (x_ref[:, sp] + land[0]) + (land[1] + land[2])
+    copies = scatter_far(count, dp, sp, total, land_two, sems)
+    for copy in copies:
+        copy.start()
+    for copy in copies:
+        copy.wait()
+    grad = scatter_total(count, dp, total, land_two)[:height, :cols]
     first = beta_one * first_ref[...] + (1.0 - beta_one) * grad
     second = beta_two * second_ref[...] + (1.0 - beta_two) * grad * grad
     new_first[...] = first
@@ -1256,26 +1304,63 @@
     )
 
 
-def update_small(count, grads, pieces, vectors, first, second):
-    rows = 4 * NB * BS // (count * SPLIT)
+def update_small(count, pieces, vectors, first, second, red_spec, spectral, moment):
     return pl.pallas_call(
         functools.partial(vectors_kernel, count),
-        in_specs=[VM] * 10,
-        out_specs=[VM] * 4,
-        out_shape=[shape((rows, BS), F32)] + [shape(vectors.shape, F32)] * 3,
+        in_specs=[VM] * 12,
+        out_specs=[VM] * 5,
+        out_shape=[shape(vectors.shape, F32)] * 3 + [shape(red_spec.shape, F32)] * 2,
         scratch_shapes=[
             pltpu.VMEM((16, D), F32),
             pltpu.VMEM((SPLIT, 2, PAIR), F32),
             pltpu.VMEM((count, SPLIT, 16, 128), F32),
         ]
-        + scatter_scratch(count, rows, BS)
         + scatter_scratch(count, 16, 128),
-        compiler_params=pltpu.CompilerParams(
-            vmem_limit_bytes=VMEM_LIMIT, collective_id=2, has_side_effects=True
-        ),
+        compiler_params=remote(2),
         name="update_small",
-        cost_estimate=cost(25),
-    )(grads.reshape(count, SPLIT, rows, BS), *pieces, vectors, first, second)
+        cost_estimate=cost(15),
+    )(*pieces, vectors, first, second, red_spec, spectral, moment)
+
+
+def norm_back_kernel(own_ref, x_ref, m0, m1, m2, m3, f0, f1, f2, f3, vec_ref, grad_ref, gvec, fs, ms):
+    @pl.when(pl.program_id(0) == 0)
+    def _():
+        gvec[...] = jnp.zeros_like(gvec)
+
+    own = own_ref[0]
+    gain = vec_ref[0:1, :]
+
+    for i in range(HB):
+        for j, (m, f) in enumerate(((m0, f0), (m1, f1), (m2, f2), (m3, f3))):
+            ms[i, own ^ j] = m[i]
+            fs[i, own ^ j] = f[i]
+    sums = []
+    for i in range(HB):
+        for part, (direct, field) in enumerate(zip(unpack_pair(ms.at[i]), unpack_pair(fs.at[i]))):
+            direct, field = direct[:OWN], field[:OWN]
+            norm, scale = normed(x_ref[part, i].astype(F32))
+            grad = field + direct
+            sums.append((jnp.sum(grad * norm, axis=0, keepdims=True), jnp.sum(grad, axis=0, keepdims=True)))
+            value = direct + norm_back(grad, norm, scale, gain)
+            for c in range(6):
+                at = pl.ds(i * (6 * OWN) + c, OWN, stride=6)
+                grad_ref[part, at, 0, :] = value[:, c * 128 : (c + 1) * 128]
+    gvec[0:1, :] += sum(a for a, b in sums)
+    gvec[1:2, :] += sum(b for a, b in sums)
+
+
+def norm_backward(own, samples, direct, fields, vectors):
+    return pl.pallas_call(
+        norm_back_kernel,
+        grid=(HALF // HB,),
+        in_specs=[SM, WIDE_BLOCK] + [PACKED_BLOCK] * (2 * SPLIT) + [VM],
+        out_specs=[pl.BlockSpec((2, HB * OWN * 6, 1, 128), lambda i: (0, i, 0, 0)), VM],
+        out_shape=[shape((2, HALF * OWN * 6, 1, 128), F32), shape((2, D), F32)],
+        scratch_shapes=[pltpu.VMEM((HB, SPLIT, PW, PAIR), BF)] * 2,
+        compiler_params=params(),
+        name="norm_backward",
+        cost_estimate=cost(30),
+    )(own, samples, *direct, *fields, vectors)
 
 
 def reduce_kernel(
@@ -1293,16 +1378,21 @@
     load = pltpu.make_async_copy(keep, acc, load_sem)
     load.start()
     pl.semaphore_wait(barrier, bits + 1)
-    copy = send(give, land, give_sems.at[0], give_sems.at[1], swap)
+    halves = [
+        send(give.at[t], land.at[t], give_sems.at[2 * t], give_sems.at[2 * t + 1], swap)
+        for t in range(2)
+    ]
     load.wait()
-    copy.wait()
-
-    def join(o, _):
-        for t in range(2):
-            acc[o, t] = acc[o, t] + land[o, t].astype(F32)
-        return 0
-
-    lax.fori_loop(0, 2**bits, join, 0)
+
+    def join_half(t):
+        halves[t].wait()
+
+        def join(o, _):
+            acc[t, o] = acc[t, o] + land[t, o].astype(F32)
+            return 0
+
+        lax.fori_loop(0, 2**bits, join, 0)
+
     streams = []
     for t in range(2):
         order = list(range(1, bits)) + [0]
@@ -1310,7 +1400,7 @@
             order[0], order[1] = order[1], order[0]
         streams.append(order)
     left = [list(range(bits)), list(range(bits))]
-    current = [lambda block, t=t: acc.at[block, t] for t in range(2)]
+    current = [lambda block, t=t: acc.at[t, block] for t in range(2)]
     for stage in range(bits):
         count = 2 ** (bits - 1 - stage)
         copies = []
@@ -1319,6 +1409,8 @@
             bit = streams[t][stage]
             step = 1 << left[t].index(bit)
             side = mine[bit]
+            if stage == 0:
+                join_half(t)
 
             def cast(o, _, t=t, outgoing=outgoing, step=step, side=side):
                 block = (o // step) * (2 * step) + (1 - side) * step + lax.rem(o, step)
@@ -1361,7 +1453,7 @@
     rows = moment.shape[0]
     blocks = FF // rows
     bits = blocks.bit_length() - 1
-    whole = (blocks, 2, rows // 2, D)
+    whole = (2, blocks, rows // 2, D)
     scratch = []
     for stage in range(bits):
         for _ in range(2):
@@ -1378,7 +1470,7 @@
             pltpu.VMEM((rows, D), F32),
             pltpu.SemaphoreType.DMA,
         ]
-        + dma_sems(2)
+        + dma_sems(4)
         + scratch,
         compiler_params=pltpu.CompilerParams(
             vmem_limit_bytes=VMEM_LIMIT, collective_id=1, has_side_effects=True
@@ -1407,64 +1499,63 @@
     tabs = tuple(jnp.asarray(np.ascontiguousarray(t)) for t in tabs)
     tabs_lo = tuple(jnp.asarray(np.ascontiguousarray(t)) for t in tabs_lo)
 
-    vec, wu, wv, w1, bias, bias_hidden = gather_small(count, vectors, spectral_w)
-    weights = (wu, wv, w1)
-    slice_in, slice_out = after((weight_in, weight_out), vec)
-    win = lax.all_gather(slice_in.T.astype(BF), axes, axis=0, tiled=True)
-    wout = lax.all_gather(slice_out.astype(BF), axes, axis=0, tiled=True)
-
+    own_width = weight_in.shape[1]
     split_hi = samples_hi.reshape(2, HALF, OWN, D)
     split_cot = cotan_hi.reshape(2, HALF, OWN, D)
     one_lo = samples_lo.reshape(HL, WL, D).transpose(1, 0, 2)
     one_cot = cotan_lo.reshape(HL, WL, D).transpose(1, 0, 2)
 
     moment = both_rows(first, moment_in.T, moment_out)
-    slabs = exchange(norm_packed(own, split_hi, vec))
-    field_lo, four_lo = filter_forward_lo(one_lo, vec, tabs_lo, weights, bias)
-    slabs = after(slabs, field_lo)
-    fields, four = filter_forward(own, slabs, tabs, weights, bias)
-    field_lo = after(field_lo, fields)
+    piece = jnp.stack([weight_in.T.astype(BF), weight_out.astype(BF)])
+    here = lax.all_gather(piece, chips, axis=0)
+    packed = norm_packed(own, split_hi)
+    vec, bias, lead, *weights = gather_small(count, *after((vectors, spectral_w), packed))
+    bias_hidden = vec[5:9].reshape(2 * count, 2, own_width).transpose(1, 0, 2).reshape(NC, FC)
+    slabs = after(exchange(packed), vec)
+    slabs, here = after((slabs, here), (slabs[1], here))
+    feed_weights = (here, lax.ppermute(here, "sc", SWAP))
+    fields, four = filter_forward(own, slabs, tabs, weights, bias, lead)
+    lo_after = after(one_lo, fields)
     fields = exchange(fields)
+    field_lo, four_lo = filter_forward_lo(lo_after, vec, tabs_lo, weights, bias)
     block_lo, gm_lo, gw, gc1, gv = feed(
-        False, own, live_slots, one_lo, one_cot, [field_lo], vec, bias_hidden, win, wout, ()
+        False, own, live_slots, one_lo, one_cot, [field_lo], vec, bias_hidden, feed_weights, ()
     )
     block_hi, p0, p1, p2, p3, keep, give, gc1, gv = feed(
-        True, own, live_slots, split_hi, split_cot, fields, vec, bias_hidden, win, wout,
+        True, own, live_slots, split_hi, split_cot, fields, vec, bias_hidden, feed_weights,
         (gw, gc1, gv),
     )
     packs = [p0, p1, p2, p3]
     grad_slabs = exchange(packs)
     new_moment, direction, gram = reduce_feed(count, keep, give, moment)
     gram = lax.psum(gram, chips)
-    grad_slabs = after(grad_slabs, direction)
-    back, gspec, ge = filter_backward(own, grad_slabs, four, tabs, weights, bias)
+    gm_lo, grad_slabs = after((gm_lo, grad_slabs), (direction, grad_slabs[1]))
+    grad_lo, gspec, ge_lo, gv_lo = filter_backward_lo(
+        one_lo, gm_lo, four_lo, vec, tabs_lo, weights, bias
+    )
+    back, gspec, ge = filter_backward(own, grad_slabs, four, tabs, weights, bias, gspec)
+    red_spec = scatter_spec(count, gspec)
+    back, gram = after((back, gram), red_spec)
     back = exchange(back)
-    gm_lo = after(gm_lo, gspec)
-    grad_lo, gspec, ge_lo, gv_lo = filter_backward_lo(
-        one_lo, gm_lo, four_lo, vec, tabs_lo, weights, bias, gspec
-    )
-    gram = after(gram, gspec)
     orth = newton_one(gram, direction)
     back = after(back, orth)
     grad_hi, gv_hi = norm_backward(own, split_hi, packs, back, vec)
-    red_spec, new_vectors, new_adam_first, new_adam_second = update_small(
-        count, gspec, (gv_lo, gv_hi, gv, gc1, ge_lo, ge), vectors, adam_first, adam_second
+    gc1 = gc1.reshape(2, 2 * count, own_width).transpose(1, 0, 2).reshape(4, D)
+    new_vectors, new_adam_first, new_adam_second, new_spectral, new_moment_spec = update_small(
+        count, (gv_lo, gv_hi, gv, gc1, ge_lo, ge), vectors, adam_first, adam_second,
+        red_spec, spectral_w, moment_spec,
     )
     new_moment_in, new_moment_out = own_rows(first, new_moment)
     orth_in, orth_out = own_rows(first, orth)
-    new_moment_spec = momentum * moment_spec + red_spec
-    dir_spec = red_spec + momentum * new_moment_spec
-    rows = moment_spec.shape[0]
-    if rows == BS:
-        orth_spec = newton_small(dir_spec)
-    else:
-        gathered = lax.all_gather(dir_spec, SP, axis=0, tiled=True)
-        orth_spec = lax.dynamic_slice_in_dim(newton_small(gathered), sp * rows, rows, 0)
 
     keep_share = 1.0 - muon_rate * decay
     new_weight_in = weight_in * keep_share - muon_rate * orth_in.T
     new_weight_out = weight_out * keep_share - muon_rate * math.sqrt(max(1.0, FF / D)) * orth_out
-    new_spectral = spectral_w * keep_share - muon_rate * orth_spec
+    rows = moment_spec.shape[0]
+    if rows != BS:
+        gathered = lax.all_gather(new_spectral, SP, axis=0, tiled=True)
+        orth_spec = lax.dynamic_slice_in_dim(newton_small(gathered), sp * rows, rows, 0)
+        new_spectral = spectral_w * keep_share - muon_rate * orth_spec
     return (
         block_hi.reshape(samples_hi.shape),
         block_lo.transpose(1, 0, 2).reshape(samples_lo.shape),

time: 908 us -> 852 us (0.938)
  waiting for transfers between devices: 67.8 us -> 0.18 us
    pallas_call x1, Pallas kernels: 24.8 us -> 107 us  [gather_small(): pl.pallas_call(functools.partial(gather_kernel, count), in_specs=[VM] * 2...]
    ppermute x12, waiting for transfers between devices: 67.7 us -> 0.09 us  [exchange(): moved.append(lax.ppermute(slabs[j], SP, [(i, i ^ j) for i in range(SPLIT)]))]
    pallas_call x5, Pallas kernels: 260 us -> 217 us  [the longest x1 80.2 us: filter_backward(): pl.pallas_call(filter_back_kernel, in_specs=[SM] + [VM] * 14, out_specs=[...]
    pallas_call x1, Pallas kernels: 38.4 us -> 22.8 us  [update_small(): pl.pallas_call(functools.partial(vectors_kernel, count), in_specs=[VM] *...]
    pallas_call x1, Pallas kernels: 26.8 us -> 16.2 us  [filter_forward_lo(): pl.pallas_call(filter_lo_kernel, in_specs=[VM] * 10, out_specs=[VM] * 2,...]
  transfers between devices with their start and end apart: 18 -> 18, of which waited for: 3 -> 1; matrix products, arithmetic and copies ran while one was open for 1% -> 1% of each run, Pallas kernels for 56% -> 66%
where the time goes in v3:
time: 852 us; the launch traced here: 849 us
  Pallas kernels  802 us (94%)
  between operations  15.2 us (2%)
  local copies, waits for them, and re-layouts  11.7 us (1%)
  starting transfers between devices  10.1 us (1%)
  other arithmetic  10 us (1%)
    pallas_call x2, Pallas kernels, feed(): pl.pallas_call(functools.partial(feed_kernel, high), grid=(steps,), in_sp...  245 us
    pallas_call x1, Pallas kernels, gather_small(): pl.pallas_call(functools.partial(gather_kernel, count), in_specs=[VM] * 2...  107 us
    pallas_call x1, Pallas kernels, reduce_feed(): pl.pallas_call(functools.partial(reduce_kernel, bits), in_specs=[ANY, ANY...  93.7 us
    pallas_call x1, Pallas kernels, filter_backward(): pl.pallas_call(filter_back_kernel, in_specs=[SM] + [VM] * 14, out_specs=[...  80.2 us
    pallas_call x1, Pallas kernels, newton_one(): pl.pallas_call(newton_kernel, in_specs=[VM] * 2, out_specs=VM, out_shape=...  70.5 us
    pallas_call x1, Pallas kernels, filter_forward(): pl.pallas_call(filter_kernel, in_specs=[SM] + [VM] * 13, out_specs=[VM] *...  47.1 us
    pallas_call x1, Pallas kernels, scatter_spec(): pl.pallas_call(functools.partial(spec_kernel, count), in_specs=[VM], out_...  46.7 us
    pallas_call x1, Pallas kernels, filter_backward_lo(): pl.pallas_call(filter_back_lo_kernel, in_specs=[VM] * 12, out_specs=[VM]...  30.7 us
  transfers between devices with their start and end apart: 18, of which 1 were waited for; matrix products, arithmetic and copies ran while one was open for 1% of the time, Pallas kernels for 66%

profile of v3, /device:TPU:0, one launch (start us, length us, event | category | flops | bytes accessed | tf_op | source)
XLA Modules:
  0.0 849.4 jit_solution(12557011904505303085)
XLA Ops:
  7.2 1.0 convert_bitcast_fusion
  8.2 1.0 convert_bitcast_fusion.1
  9.2 0.7 pad_maximum_fusion.1
  10.0 12.7 %norm_pack.1 = (bf16[45,48,384]{2,1,0:T(8,128)(2,1)}, bf16[45,48,384]{2,1,0:T(8,128)(2,1)}, bf16[45,48,384]{2,1,0:T(8,128)(2,1)}, bf16[45,48,384]{2,1,0:T(8,128)(2,1)}) custom-call(s32[1]{0:T(128)} %bitcast.own_ref, bf16[2,45,45,768]{3,2,1,0:T(8,128)(2,1)} %bitcast.45), custom_call_target="tpu_custom_call" | custom-call | flops 16000000000 | bytes 16000000 | tf_op jit(solution)/shard_map/norm_pack/pallas_call | solution.py:200
  22.7 0.5 collective-permute-start
  23.2 2.6 collective-permute-start.1
  25.8 0.1 collective-permute-start.2
  25.9 0.2 collective-permute-start.10
  26.1 107.2 %gather_small.1 = (f32[16,768]{1,0:T(8,128)}, f32[4,2,384]{2,1,0:T(2,128)}, f32[4,2,384]{2,1,0:T(2,128)}, bf16[4,192,384]{2,1,0:T(8,128)(2,1)}, bf16[4,192,384]{...) custom-call(f32[13,24]{1,0:T(8,128)} %vec_ref.2, f32[96,96]{1,0:T(8,128)} %spec_ref.2), custom_call_target="tpu_custom_call" | custom-call | flops 70000001024 | bytes 70000000 | tf_op jit(solution)/shard_map/gather_small/pallas_call | solution.py:1139
  133.4 0.8 slice.3
  134.2 0.1 reshape.77
  134.3 0.7 reshape.78.refs_4_.refs_7_
  135.7 0.9 pad_maximum_fusion.moment
  136.6 0.2 collective-permute-start.6
  136.8 0.9 copy-done.7
  137.7 47.1 %filter_forward.1 = (bf16[45,48,384]{2,1,0:T(8,128)(2,1)}, bf16[45,48,384]{2,1,0:T(8,128)(2,1)}, bf16[45,48,384]{2,1,0:T(8,128)(2,1)}, bf16[45,48,384]{2,1,0:T(8,128)(2,1)}, bf16[13,2,672,192]{3,2,1,0:T(8,128)(2,1)}) custom-call(s32[1]{0:T(128)} %bitcast.own_ref, bf16[45,48,384]{2,1,0:T(8,128)(2,1)} %get-tuple-element.101.x0, ...), custom_call_target="tpu_custom_call" | custom-call | flops 95000002560 | bytes 95000000 | tf_op jit(solution)/shard_map/filter_forward/pallas_call | solution.py:430
  184.8 0.2 collective-permute-start.3
  185.0 1.4 collective-permute-start.4
  186.4 0.3 collective-permute-start.5
  186.6 16.2 %filter_forward_lo.1 = (bf16[45,24,768]{2,1,0:T(8,128)(2,1)}, bf16[4,2,576,192]{3,2,1,0:T(8,128)(2,1)}) custom-call(bf16[45,23,768]{2,1,0:T(8,128)(2,1)} %bitcast.52, f32[16,768]{1,0:T(8,128)} %get-tuple-element.96.vec_ref.refs_3_.refs_6_, bf16[24,24]{1,0:T(8,128)(2,1)} %constant.35.clone.tw, bf16[24,24]{1,0:T(8,128)(2,1)} %constant.36.clone.twt, ...), custom_call_target="tpu_custom_call" | custom-call | flops 35000000512 | bytes 35000000 | tf_op jit(solution)/shard_map/filter_forward_lo/pallas_call | solution.py:587
  202.9 55.7 %feed_lo.1 = (bf16[45,23,768]{2,1,0:T(8,128)(2,1)}, bf16[45,24,768]{2,1,0:T(8,128)(2,1)}, f32[2,3072,768]{2,1,0:T(8,128)}, f32[4,768]{1,0:T(4,128)}, f32[8,768]{1,0:T(8,128)}) custom-call(s32[1]{0:T(128)} %bitcast.own_ref, s32[1]{0:T(128)S(6)} %copy.57.live_ref, bf16[45,23,768]{2,1,0:T(8,128)(2,1)} %bitcast.53, bf16[45,23,768]{2,1,0:T(8,128)(2,1)} %bitcast.51, ...), custom_call_target="tpu_custom_call" | custom-call | flops 70000001024 | bytes 70000000 | tf_op jit(solution)/shard_map/feed_lo/pallas_call | solution.py:877
  258.7 1.1 copy-done.10
  259.8 0.5 copy-done.11
  260.3 188.9 %feed_hi.1 = (bf16[2,45,45,768]{3,2,1,0:T(8,128)(2,1)}, bf16[45,48,384]{2,1,0:T(8,128)(2,1)}, bf16[45,48,384]{2,1,0:T(8,128)(2,1)}, bf16[45,48,384]{2,1,0:T(8,12...) custom-call(s32[1]{0:T(128)} %bitcast.own_ref, ...), custom_call_target="tpu_custom_call" | custom-call | flops 210000003072 | bytes 210000000 | tf_op jit(solution)/shard_map/feed_hi/pallas_call | solution.py:877
  449.2 0.5 collective-permute-start.7
  449.7 1.4 collective-permute-start.8
  451.2 93.7 %reduce_feed.1 = (f32[192,768]{1,0:T(8,128)}, f32[192,768]{1,0:T(8,128)}, f32[768,768]{1,0:T(8,128)}) custom-call(f32[2,16,96,768]{3,2,1,0:T(8,128)} %bitcast.56, bf16[2,16,96,768]{3,2,1,0:T(8,128)(2,1)} %bitcast.58, f32[192,768]{1,0:T(8,128)} %pad_maximum_fusion.moment), custom_call_target="tpu_custom_call" | custom-call | flops 80000000000 | bytes 80000000 | tf_op jit(solution)/shard_map/reduce_feed/pallas_call | solution.py:1462
  544.9 1.8 slice_select_fusion.2
  546.8 30.7 %filter_backward_lo.1 = (f32[6210,1,128]{2,1,0:T(1,128)}, f32[32,96,96]{2,1,0:T(8,128)}, f32[4,2,384]{2,1,0:T(2,128)}, f32[2,768]{1,0:T(2,128)}) custom-call(bf16[45,23,768]{2,1,0:T(8,128)(2,1)} %bitcast.54, bf16[45,24,768]{2,1,0:T(8,128)(2,1)} %get-tuple-element.135.gm_ref, bf16[4,2,576,192]{3,2,1,0:T(8,128)(2,1)} %get-tuple-element.136.four, ...), custom_call_target="tpu_custom_call" | custom-call | flops 44999999488 | bytes 45000000 | tf_op jit(solution)/shard_map/filter_backward_lo/pallas_call | solution.py:673
  577.5 80.2 %filter_backward.1 = (bf16[45,48,384]{2,1,0:T(8,128)(2,1)}, bf16[45,48,384]{2,1,0:T(8,128)(2,1)}, bf16[45,48,384]{2,1,0:T(8,128)(2,1)}, bf16[45,48,384]{2,1,0:T(...) custom-call(s32[1]{0:T(128)} %bitcast.own_ref, bf16[45,48,384]{2,1,0:T(8,128)(2,1)} %get-tuple-element.130.x0.m0, ...), custom_call_target="tpu_custom_call" | custom-call | flops 124999999488 | bytes 125000000 | tf_op jit(solution)/shard_map/filter_backward/pallas_call | solution.py:485
  657.7 46.7 %scatter_spec.1.red_spec = f32[96,96]{1,0:T(8,128)} custom-call(f32[8,4,96,96]{3,2,1,0:T(8,128)} %bitcast.61), custom_call_target="tpu_custom_call" | custom-call | flops 24999999488 | bytes 25000000 | tf_op jit(solution)/shard_map/scatter_spec/pallas_call | solution.py:1225
  704.5 0.4 collective-permute-start.11
  704.9 0.4 collective-permute-start.12
  705.2 1.2 collective-permute-start.13
  706.4 70.5 %newton.1 = f32[192,768]{1,0:T(8,128)} custom-call(f32[768,768]{1,0:T(8,128)} %all-reduce.2.cloned.1.call-done.g_ref, f32[192,768]{1,0:T(8,128)} %get-tuple-element.129.x_ref), custom_call_target="tpu_custom_call" | custom-call | flops 60000002048 | bytes 60000000 | tf_op jit(solution)/shard_map/newton/pallas_call | solution.py:985
  776.9 1.2 slice_select_fusion
  778.1 0.7 collective-permute-start.14
  778.9 0.7 reshape.89.gc1
  779.6 1.8 broadcast_select_fusion
  781.4 0.8 select_subtract_fusion
  782.2 0.8 bitcast_subtract_fusion
  783.0 29.8 %norm_backward.1 = (f32[2,12150,1,128]{3,2,1,0:T(1,128)}, f32[2,768]{1,0:T(2,128)}) custom-call(s32[1]{0:T(128)} %bitcast.own_ref, bf16[2,45,45,768]{3,2,1,0:T(8,128)(2,1)} %bitcast.47, bf16[45,48,384]{2,1,0:T(8,128)(2,1)} %get-tuple-element.130.x0.m0, bf16[45,48,384]{2,1,0:T(8,128)(2,1)} %get-tuple-element.123.m1, ...), custom_call_target="tpu_custom_call" | custom-call | flops 30000001024 | bytes 30000000 | tf_op jit(solution)/shard_map/norm_backward/pallas_call | solution.py:1353
  812.8 22.8 %update_small.1 = (f32[13,24]{1,0:T(8,128)}, f32[13,24]{1,0:T(8,128)}, f32[13,24]{1,0:T(8,128)}, f32[96,96]{1,0:T(8,128)}, f32[96,96]{1,0:T(8,128)}) custom-call(f32[2,768]{1,0:T(2,128)} %get-tuple-element.155.gv_lo, f32[2,768]{1,0:T(2,128)} %get-tuple-element.156.gv_hi, f32[8,768]{1,0:T(8,128)} %get-tuple-element.157.gv, f32[4,768]{1,0:T(4,128)} %reshape.89.gc1, ...), custom_call_target="tpu_custom_call" | custom-call | flops 15000000512 | bytes 15000000 | tf_op jit(solution)/shard_map/update_small/pallas_call | solution.py:1308
  835.6 1.4 copy.58
  837.0 1.4 copy.59
  838.4 1.3 copy.60
  839.7 1.3 copy.61
  841.0 1.3 copy.62
  (50 shorter events, 0.5 us)
Async XLA Ops:
  7.2 129.4 %all-gather.3.cloned.1.call-start = ((), (), s32[]{:S(2)}) async-start(), calls=%async_computation.1 | async-start | bytes 5013504 | tf_op jit(solution)/shard_map/all_gather | solution.py:1510
  10.0 694.5 %all-reduce.2.cloned.1.call-start = ((), (), s32[]{:S(2)}) async-start(), calls=%async_computation | async-start | bytes 4718592 | tf_op jit(solution)/shard_map/psum | solution.py:1531
  10.0 15.9 %copy-start.2 = (f32[96,768]{1,0:T(8,128)S(1)}, f32[96,768]{1,0:T(8,128)}, u32[]{:S(2)}) copy-start(f32[96,768]{1,0:T(8,128)} %param.33) | copy-start | bytes 884740
  10.0 15.9 %copy-start.3 = (f32[768,96]{0,1:T(8,128)S(1)}, f32[768,96]{0,1:T(8,128)}, u32[]{:S(2)}) copy-start(f32[768,96]{0,1:T(8,128)} %param.32) | copy-start | bytes 884740
  22.7 113.8 %collective-permute-start = (bf16[45,48,384]{2,1,0:T(8,128)(2,1)}, bf16[45,48,384]{2,1,0:T(8,128)(2,1)S(1)}, u32[]{:S(2)}, u32[]{:S(2)}) collective-permute-start(bf16[45,48,384]{2,1,0:T(8,128)(2,1)} %get-tuple-element.91), channel_id=1, source_target_pairs={{0,1},{1,0},{2,3},{3,2},{4,5},{5,4},{6,7},{7,6},{8,9},{9,8},{10,11... | collective-permute-start | bytes 4976648 | tf_op jit(solution)/shard_map/ppermute | solution.py:216
  23.2 113.3 %collective-permute-start.1 = (bf16[45,48,384]{2,1,0:T(8,128)(2,1)}, bf16[45,48,384]{2,1,0:T(8,128)(2,1)}, u32[]{:S(2)}, u32[]{:S(2)}) collective-permute-start(bf16[45,48,384]{2,1,0:T(8,128)(2,1)} %get-tuple-element.92), channel_id=1, source_target_pairs={{0,2},{1,3},{2,0},{3,1},{4,6},{5,7},{6,4},{7,5},{8,10},{9,11},{10,... | collective-permute-start | bytes 4976648 | tf_op jit(solution)/shard_map/ppermute | solution.py:216
  25.8 110.8 %collective-permute-start.2 = (bf16[45,48,384]{2,1,0:T(8,128)(2,1)}, bf16[45,48,384]{2,1,0:T(8,128)(2,1)}, u32[]{:S(2)}, u32[]{:S(2)}) collective-permute-start(bf16[45,48,384]{2,1,0:T(8,128)(2,1)} %get-tuple-element.93), channel_id=1, source_target_pairs={{0,3},{1,2},{2,1},{3,0},{4,7},{5,6},{6,5},{7,4},{8,11},{9,10},{10,... | collective-permute-start | bytes 4976648 | tf_op jit(solution)/shard_map/ppermute | solution.py:216
  25.9 109.7 %collective-permute-start.10 = (f32[96,768]{1,0:T(8,128)S(1)}, f32[96,768]{1,0:T(8,128)S(1)}, u32[]{:S(2)}, u32[]{:S(2)}) collective-permute-start(f32[96,768]{1,0:T(8,128)S(1)} %bitcast_select_fusion), channel_id=1, source_target_pairs={{0,1},{1,0},{2,3},{3,2},{4,5},{5,4},{6,7},{7,6},{8,9},{9,8},{10,11... | collective-permute-start | bytes 884744 | tf_op jit(solution)/shard_map/ppermute | solution.py:1008
  136.5 1.2 copy-start.7
  136.6 66.3 %collective-permute-start.6 = (bf16[16,2,96,768]{3,2,1,0:T(8,128)(2,1)}, bf16[16,2,96,768]{3,2,1,0:T(8,128)(2,1)}, u32[]{:S(2)}, u32[]{:S(2)}) collective-permute-start(bf16[16,2,96,768]{3,2,1,0:T(8,128)(2,1)} %bitcast.48), channel_id=1, source_target_pairs={{0,1},{1,0},{2,3},{3,2},{4,5},{5,4},{6,7},{7,6},{8,9},{9,8},{10,11... | collective-permute-start | bytes 14155784 | tf_op jit(solution)/shard_map/ppermute | solution.py:1516
  184.8 73.8 %collective-permute-start.3 = (bf16[45,48,384]{2,1,0:T(8,128)(2,1)}, bf16[45,48,384]{2,1,0:T(8,128)(2,1)S(1)}, u32[]{:S(2)}, u32[]{:S(2)}) collective-permute-start(bf16[45,48,384]{2,1,0:T(8,128)(2,1)} %get-tuple-element.111), channel_id=1, source_target_pairs={{0,1},{1,0},{2,3},{3,2},{4,5},{5,4},{6,7},{7,6},{8,9},{9,8},{10,11... | collective-permute-start | bytes 4976648 | tf_op jit(solution)/shard_map/ppermute | solution.py:216
  185.0 73.6 %collective-permute-start.4 = (bf16[45,48,384]{2,1,0:T(8,128)(2,1)}, bf16[45,48,384]{2,1,0:T(8,128)(2,1)S(1)}, u32[]{:S(2)}, u32[]{:S(2)}) collective-permute-start(bf16[45,48,384]{2,1,0:T(8,128)(2,1)} %get-tuple-element.112), channel_id=1, source_target_pairs={{0,2},{1,3},{2,0},{3,1},{4,6},{5,7},{6,4},{7,5},{8,10},{9,11},{10,... | collective-permute-start | bytes 4976648 | tf_op jit(solution)/shard_map/ppermute | solution.py:216
  186.4 72.3 %collective-permute-start.5 = (bf16[45,48,384]{2,1,0:T(8,128)(2,1)}, bf16[45,48,384]{2,1,0:T(8,128)(2,1)}, u32[]{:S(2)}, u32[]{:S(2)}) collective-permute-start(bf16[45,48,384]{2,1,0:T(8,128)(2,1)} %get-tuple-element.113), channel_id=1, source_target_pairs={{0,3},{1,2},{2,1},{3,0},{4,7},{5,6},{6,5},{7,4},{8,11},{9,10},{10,... | collective-permute-start | bytes 4976648 | tf_op jit(solution)/shard_map/ppermute | solution.py:216
  258.6 1.2 copy-start.10
  258.6 1.7 copy-start.11
  449.2 97.6 %collective-permute-start.7 = (bf16[45,48,384]{2,1,0:T(8,128)(2,1)}, bf16[45,48,384]{2,1,0:T(8,128)(2,1)S(1)}, u32[]{:S(2)}, u32[]{:S(2)}) collective-permute-start(bf16[45,48,384]{2,1,0:T(8,128)(2,1)} %get-tuple-element.123.m1), channel_id=1, source_target_pairs={{0,1},{1,0},{2,3},{3,2},{4,5},{5,4},{6,7},{7,6},{8,9},{9,8},{10,11... | collective-permute-start | bytes 4976648 | tf_op jit(solution)/shard_map/ppermute | solution.py:216
  449.7 97.0 %collective-permute-start.8 = (bf16[45,48,384]{2,1,0:T(8,128)(2,1)}, bf16[45,48,384]{2,1,0:T(8,128)(2,1)S(1)}, u32[]{:S(2)}, u32[]{:S(2)}) collective-permute-start(bf16[45,48,384]{2,1,0:T(8,128)(2,1)} %get-tuple-element.124.m2), channel_id=1, source_target_pairs={{0,2},{1,3},{2,0},{3,1},{4,6},{5,7},{6,4},{7,5},{8,10},{9,11},{10,... | collective-permute-start | bytes 4976648 | tf_op jit(solution)/shard_map/ppermute | solution.py:216
  451.1 95.7 %collective-permute-start.9 = (bf16[45,48,384]{2,1,0:T(8,128)(2,1)}, bf16[45,48,384]{2,1,0:T(8,128)(2,1)}, u32[]{:S(2)}, u32[]{:S(2)}) collective-permute-start(bf16[45,48,384]{2,1,0:T(8,128)(2,1)} %get-tuple-element.125.m3), channel_id=1, source_target_pairs={{0,3},{1,2},{2,1},{3,0},{4,7},{5,6},{6,5},{7,4},{8,11},{9,10},{10,... | collective-permute-start | bytes 4976648 | tf_op jit(solution)/shard_map/ppermute | solution.py:216
  546.7 232.9 %collective-permute-start.15 = (f32[96,768]{1,0:T(8,128)}, f32[96,768]{1,0:T(8,128)}, u32[]{:S(2)}, u32[]{:S(2)}) collective-permute-start(f32[96,768]{1,0:T(8,128)} %slice_select_fusion.2), channel_id=1, source_target_pairs={{0,1},{1,0},{2,3},{3,2},{4,5},{5,4},{6,7},{7,6},{8,9},{9,8},{10,11... | collective-permute-start | bytes 884744 | tf_op jit(solution)/shard_map/ppermute | solution.py:1017
  546.7 30.7 %copy-start.8 = (bf16[45,48,384]{2,1,0:T(8,128)(2,1)}, bf16[45,48,384]{2,1,0:T(8,128)(2,1)S(1)}, u32[]{:S(2)}) copy-start(bf16[45,48,384]{2,1,0:T(8,128)(2,1)S(1)} %collective-permute-done.7.x1) | copy-start | bytes 4976644
  546.8 30.7 %copy-start.9 = (bf16[45,48,384]{2,1,0:T(8,128)(2,1)}, bf16[45,48,384]{2,1,0:T(8,128)(2,1)S(1)}, u32[]{:S(2)}) copy-start(bf16[45,48,384]{2,1,0:T(8,128)(2,1)S(1)} %collective-permute-done.8.x2) | copy-start | bytes 4976644
  704.4 74.4 %copy-start.6 = (f32[4,768]{1,0:T(4,128)S(1)}, f32[4,768]{1,0:T(4,128)}, u32[]{:S(2)}) copy-start(f32[4,768]{1,0:T(4,128)} %get-tuple-element.158) | copy-start | bytes 36868
  704.4 75.2 %copy-start.1 = (f32[192,768]{1,0:T(8,128)S(1)}, f32[192,768]{1,0:T(8,128)}, u32[]{:S(2)}) copy-start(f32[192,768]{1,0:T(8,128)} %get-tuple-element.163) | copy-start | bytes 1769476
  704.5 78.6 %collective-permute-start.11 = (bf16[45,48,384]{2,1,0:T(8,128)(2,1)}, bf16[45,48,384]{2,1,0:T(8,128)(2,1)}, u32[]{:S(2)}, u32[]{:S(2)}) collective-permute-start(bf16[45,48,384]{2,1,0:T(8,128)(2,1)} %get-tuple-element.145), channel_id=1, source_target_pairs={{0,1},{1,0},{2,3},{3,2},{4,5},{5,4},{6,7},{7,6},{8,9},{9,8},{10,11... | collective-permute-start | bytes 4976648 | tf_op jit(solution)/shard_map/ppermute | solution.py:216
  704.9 78.1 %collective-permute-start.12 = (bf16[45,48,384]{2,1,0:T(8,128)(2,1)}, bf16[45,48,384]{2,1,0:T(8,128)(2,1)}, u32[]{:S(2)}, u32[]{:S(2)}) collective-permute-start(bf16[45,48,384]{2,1,0:T(8,128)(2,1)} %get-tuple-element.146), channel_id=1, source_target_pairs={{0,2},{1,3},{2,0},{3,1},{4,6},{5,7},{6,4},{7,5},{8,10},{9,11},{10,... | collective-permute-start | bytes 4976648 | tf_op jit(solution)/shard_map/ppermute | solution.py:216
  705.2 77.8 %collective-permute-start.13 = (bf16[45,48,384]{2,1,0:T(8,128)(2,1)}, bf16[45,48,384]{2,1,0:T(8,128)(2,1)}, u32[]{:S(2)}, u32[]{:S(2)}) collective-permute-start(bf16[45,48,384]{2,1,0:T(8,128)(2,1)} %get-tuple-element.147), channel_id=1, source_target_pairs={{0,3},{1,2},{2,1},{3,0},{4,7},{5,6},{6,5},{7,4},{8,11},{9,10},{10,... | collective-permute-start | bytes 4976648 | tf_op jit(solution)/shard_map/ppermute | solution.py:216
  776.9 4.5 copy-start
  776.9 4.5 copy-start.4
  778.1 4.1 copy-start.5
  778.1 3.3 collective-permute-start.14
Sparse Core Ops, SparseCore 0:
  11.4 103.4 all-gather.2
  546.8 154.1 all-reduce.1

commit v4 on v3

--- a/solution.py
+++ b/solution.py
@@ -921,7 +921,7 @@
     return top, middle, (rest - middle.astype(F32)).astype(BF)
 
 
-TILE = 256
+TILE = 384
 
 
 def mul_parts(left, right_ref, parts, full, out, finish=None):

time: 852 us -> 854 us (level)
  no operation moved by 1% of the time
where the time goes in v4:
time: 854 us; the launch traced here: 846 us
  Pallas kernels  799 us (94%)
  between operations  15.4 us (2%)
  local copies, waits for them, and re-layouts  11.7 us (1%)
  starting transfers between devices  10 us (1%)
  other arithmetic  10 us (1%)
    pallas_call x2, Pallas kernels, feed(): pl.pallas_call(functools.partial(feed_kernel, high), grid=(steps,), in_sp...  245 us
    pallas_call x1, Pallas kernels, gather_small(): pl.pallas_call(functools.partial(gather_kernel, count), in_specs=[VM] * 2...  107 us
    pallas_call x1, Pallas kernels, reduce_feed(): pl.pallas_call(functools.partial(reduce_kernel, bits), in_specs=[ANY, ANY...  93.7 us
    pallas_call x1, Pallas kernels, filter_backward(): pl.pallas_call(filter_back_kernel, in_specs=[SM] + [VM] * 14, out_specs=[...  80.2 us
    pallas_call x1, Pallas kernels, newton_one(): pl.pallas_call(newton_kernel, in_specs=[VM] * 2, out_specs=VM, out_shape=...  66.6 us
    pallas_call x1, Pallas kernels, filter_forward(): pl.pallas_call(filter_kernel, in_specs=[SM] + [VM] * 13, out_specs=[VM] *...  47.1 us
    pallas_call x1, Pallas kernels, scatter_spec(): pl.pallas_call(functools.partial(spec_kernel, count), in_specs=[VM], out_...  46.7 us
    pallas_call x1, Pallas kernels, filter_backward_lo(): pl.pallas_call(filter_back_lo_kernel, in_specs=[VM] * 12, out_specs=[VM]...  30.7 us
  transfers between devices with their start and end apart: 18, of which 1 were waited for; matrix products, arithmetic and copies ran while one was open for 1% of the time, Pallas kernels for 66%

profile of v4, /device:TPU:0, one launch (start us, length us, event | category | flops | bytes accessed | tf_op | source)
XLA Modules:
  0.0 846.0 jit_solution(14654063549921403013)
XLA Ops:
  7.2 1.0 convert_bitcast_fusion
  8.2 1.0 convert_bitcast_fusion.1
  9.2 0.7 pad_maximum_fusion.1
  10.0 12.7 %norm_pack.1 = (bf16[45,48,384]{2,1,0:T(8,128)(2,1)}, bf16[45,48,384]{2,1,0:T(8,128)(2,1)}, bf16[45,48,384]{2,1,0:T(8,128)(2,1)}, bf16[45,48,384]{2,1,0:T(8,128)(2,1)}) custom-call(s32[1]{0:T(128)} %bitcast.own_ref, bf16[2,45,45,768]{3,2,1,0:T(8,128)(2,1)} %bitcast.45), custom_call_target="tpu_custom_call" | custom-call | flops 16000000000 | bytes 16000000 | tf_op jit(solution)/shard_map/norm_pack/pallas_call | solution.py:200
  22.7 0.5 collective-permute-start
  23.2 2.6 collective-permute-start.1
  25.8 0.1 collective-permute-start.2
  25.9 0.2 collective-permute-start.10
  26.1 107.2 %gather_small.1 = (f32[16,768]{1,0:T(8,128)}, f32[4,2,384]{2,1,0:T(2,128)}, f32[4,2,384]{2,1,0:T(2,128)}, bf16[4,192,384]{2,1,0:T(8,128)(2,1)}, bf16[4,192,384]{...) custom-call(f32[13,24]{1,0:T(8,128)} %vec_ref.2, f32[96,96]{1,0:T(8,128)} %spec_ref.2), custom_call_target="tpu_custom_call" | custom-call | flops 70000001024 | bytes 70000000 | tf_op jit(solution)/shard_map/gather_small/pallas_call | solution.py:1139
  133.4 0.8 slice.3
  134.2 0.1 reshape.77
  134.3 0.7 reshape.78.refs_4_.refs_7_
  135.7 0.9 pad_maximum_fusion.moment
  136.6 0.2 collective-permute-start.6
  136.8 0.9 copy-done.7
  137.7 47.1 %filter_forward.1 = (bf16[45,48,384]{2,1,0:T(8,128)(2,1)}, bf16[45,48,384]{2,1,0:T(8,128)(2,1)}, bf16[45,48,384]{2,1,0:T(8,128)(2,1)}, bf16[45,48,384]{2,1,0:T(8,128)(2,1)}, bf16[13,2,672,192]{3,2,1,0:T(8,128)(2,1)}) custom-call(s32[1]{0:T(128)} %bitcast.own_ref, bf16[45,48,384]{2,1,0:T(8,128)(2,1)} %get-tuple-element.101.x0, ...), custom_call_target="tpu_custom_call" | custom-call | flops 95000002560 | bytes 95000000 | tf_op jit(solution)/shard_map/filter_forward/pallas_call | solution.py:430
  184.8 0.2 collective-permute-start.3
  185.0 1.4 collective-permute-start.4
  186.4 0.3 collective-permute-start.5
  186.6 16.2 %filter_forward_lo.1 = (bf16[45,24,768]{2,1,0:T(8,128)(2,1)}, bf16[4,2,576,192]{3,2,1,0:T(8,128)(2,1)}) custom-call(bf16[45,23,768]{2,1,0:T(8,128)(2,1)} %bitcast.52, f32[16,768]{1,0:T(8,128)} %get-tuple-element.96.vec_ref.refs_3_.refs_6_, bf16[24,24]{1,0:T(8,128)(2,1)} %constant.35.clone.tw, bf16[24,24]{1,0:T(8,128)(2,1)} %constant.36.clone.twt, ...), custom_call_target="tpu_custom_call" | custom-call | flops 35000000512 | bytes 35000000 | tf_op jit(solution)/shard_map/filter_forward_lo/pallas_call | solution.py:587
  202.9 55.7 %feed_lo.1 = (bf16[45,23,768]{2,1,0:T(8,128)(2,1)}, bf16[45,24,768]{2,1,0:T(8,128)(2,1)}, f32[2,3072,768]{2,1,0:T(8,128)}, f32[4,768]{1,0:T(4,128)}, f32[8,768]{1,0:T(8,128)}) custom-call(s32[1]{0:T(128)} %bitcast.own_ref, s32[1]{0:T(128)S(6)} %copy.57.live_ref, bf16[45,23,768]{2,1,0:T(8,128)(2,1)} %bitcast.53, bf16[45,23,768]{2,1,0:T(8,128)(2,1)} %bitcast.51, ...), custom_call_target="tpu_custom_call" | custom-call | flops 70000001024 | bytes 70000000 | tf_op jit(solution)/shard_map/feed_lo/pallas_call | solution.py:877
  258.7 1.1 copy-done.10
  259.8 0.5 copy-done.11
  260.3 188.9 %feed_hi.1 = (bf16[2,45,45,768]{3,2,1,0:T(8,128)(2,1)}, bf16[45,48,384]{2,1,0:T(8,128)(2,1)}, bf16[45,48,384]{2,1,0:T(8,128)(2,1)}, bf16[45,48,384]{2,1,0:T(8,12...) custom-call(s32[1]{0:T(128)} %bitcast.own_ref, ...), custom_call_target="tpu_custom_call" | custom-call | flops 210000003072 | bytes 210000000 | tf_op jit(solution)/shard_map/feed_hi/pallas_call | solution.py:877
  449.2 0.5 collective-permute-start.7
  449.7 1.4 collective-permute-start.8
  451.2 93.7 %reduce_feed.1 = (f32[192,768]{1,0:T(8,128)}, f32[192,768]{1,0:T(8,128)}, f32[768,768]{1,0:T(8,128)}) custom-call(f32[2,16,96,768]{3,2,1,0:T(8,128)} %bitcast.56, bf16[2,16,96,768]{3,2,1,0:T(8,128)(2,1)} %bitcast.58, f32[192,768]{1,0:T(8,128)} %pad_maximum_fusion.moment), custom_call_target="tpu_custom_call" | custom-call | flops 80000000000 | bytes 80000000 | tf_op jit(solution)/shard_map/reduce_feed/pallas_call | solution.py:1462
  544.9 1.8 slice_select_fusion.2
  546.8 30.7 %filter_backward_lo.1 = (f32[6210,1,128]{2,1,0:T(1,128)}, f32[32,96,96]{2,1,0:T(8,128)}, f32[4,2,384]{2,1,0:T(2,128)}, f32[2,768]{1,0:T(2,128)}) custom-call(bf16[45,23,768]{2,1,0:T(8,128)(2,1)} %bitcast.54, bf16[45,24,768]{2,1,0:T(8,128)(2,1)} %get-tuple-element.135.gm_ref, bf16[4,2,576,192]{3,2,1,0:T(8,128)(2,1)} %get-tuple-element.136.four, ...), custom_call_target="tpu_custom_call" | custom-call | flops 44999999488 | bytes 45000000 | tf_op jit(solution)/shard_map/filter_backward_lo/pallas_call | solution.py:673
  577.5 80.2 %filter_backward.1 = (bf16[45,48,384]{2,1,0:T(8,128)(2,1)}, bf16[45,48,384]{2,1,0:T(8,128)(2,1)}, bf16[45,48,384]{2,1,0:T(8,128)(2,1)}, bf16[45,48,384]{2,1,0:T(...) custom-call(s32[1]{0:T(128)} %bitcast.own_ref, bf16[45,48,384]{2,1,0:T(8,128)(2,1)} %get-tuple-element.130.x0.m0, ...), custom_call_target="tpu_custom_call" | custom-call | flops 124999999488 | bytes 125000000 | tf_op jit(solution)/shard_map/filter_backward/pallas_call | solution.py:485
  657.7 46.7 %scatter_spec.1.red_spec = f32[96,96]{1,0:T(8,128)} custom-call(f32[8,4,96,96]{3,2,1,0:T(8,128)} %bitcast.61), custom_call_target="tpu_custom_call" | custom-call | flops 24999999488 | bytes 25000000 | tf_op jit(solution)/shard_map/scatter_spec/pallas_call | solution.py:1225
  704.5 0.4 collective-permute-start.11
  704.9 0.4 collective-permute-start.12
  705.2 1.2 collective-permute-start.13
  706.4 66.6 %newton.1 = f32[192,768]{1,0:T(8,128)} custom-call(f32[768,768]{1,0:T(8,128)} %all-reduce.2.cloned.1.call-done.g_ref, f32[192,768]{1,0:T(8,128)} %get-tuple-element.129.x_ref), custom_call_target="tpu_custom_call" | custom-call | flops 60000002048 | bytes 60000000 | tf_op jit(solution)/shard_map/newton/pallas_call | solution.py:985
  773.0 1.2 slice_select_fusion
  774.2 0.7 collective-permute-start.14
  775.0 0.7 reshape.89.gc1
  775.7 1.8 broadcast_select_fusion
  777.5 0.8 select_subtract_fusion
  778.3 0.8 bitcast_subtract_fusion
  779.1 30.0 %norm_backward.1 = (f32[2,12150,1,128]{3,2,1,0:T(1,128)}, f32[2,768]{1,0:T(2,128)}) custom-call(s32[1]{0:T(128)} %bitcast.own_ref, bf16[2,45,45,768]{3,2,1,0:T(8,128)(2,1)} %bitcast.47, bf16[45,48,384]{2,1,0:T(8,128)(2,1)} %get-tuple-element.130.x0.m0, bf16[45,48,384]{2,1,0:T(8,128)(2,1)} %get-tuple-element.123.m1, ...), custom_call_target="tpu_custom_call" | custom-call | flops 30000001024 | bytes 30000000 | tf_op jit(solution)/shard_map/norm_backward/pallas_call | solution.py:1353
  809.1 22.8 %update_small.1 = (f32[13,24]{1,0:T(8,128)}, f32[13,24]{1,0:T(8,128)}, f32[13,24]{1,0:T(8,128)}, f32[96,96]{1,0:T(8,128)}, f32[96,96]{1,0:T(8,128)}) custom-call(f32[2,768]{1,0:T(2,128)} %get-tuple-element.155.gv_lo, f32[2,768]{1,0:T(2,128)} %get-tuple-element.156.gv_hi, f32[8,768]{1,0:T(8,128)} %get-tuple-element.157.gv, f32[4,768]{1,0:T(4,128)} %reshape.89.gc1, ...), custom_call_target="tpu_custom_call" | custom-call | flops 15000000512 | bytes 15000000 | tf_op jit(solution)/shard_map/update_small/pallas_call | solution.py:1308
  831.9 1.4 copy.58
  833.4 1.4 copy.59
  834.8 1.3 copy.60
  836.1 1.3 copy.61
  837.4 1.3 copy.62
  (50 shorter events, 0.5 us)
Async XLA Ops:
  7.2 129.4 %all-gather.3.cloned.1.call-start = ((), (), s32[]{:S(2)}) async-start(), calls=%async_computation.1 | async-start | bytes 5013504 | tf_op jit(solution)/shard_map/all_gather | solution.py:1510
  10.0 694.5 %all-reduce.2.cloned.1.call-start = ((), (), s32[]{:S(2)}) async-start(), calls=%async_computation | async-start | bytes 4718592 | tf_op jit(solution)/shard_map/psum | solution.py:1531
  10.0 15.9 %copy-start.2 = (f32[96,768]{1,0:T(8,128)S(1)}, f32[96,768]{1,0:T(8,128)}, u32[]{:S(2)}) copy-start(f32[96,768]{1,0:T(8,128)} %param.33) | copy-start | bytes 884740
  10.0 15.9 %copy-start.3 = (f32[768,96]{0,1:T(8,128)S(1)}, f32[768,96]{0,1:T(8,128)}, u32[]{:S(2)}) copy-start(f32[768,96]{0,1:T(8,128)} %param.32) | copy-start | bytes 884740
  22.7 113.8 %collective-permute-start = (bf16[45,48,384]{2,1,0:T(8,128)(2,1)}, bf16[45,48,384]{2,1,0:T(8,128)(2,1)S(1)}, u32[]{:S(2)}, u32[]{:S(2)}) collective-permute-start(bf16[45,48,384]{2,1,0:T(8,128)(2,1)} %get-tuple-element.91), channel_id=1, source_target_pairs={{0,1},{1,0},{2,3},{3,2},{4,5},{5,4},{6,7},{7,6},{8,9},{9,8},{10,11... | collective-permute-start | bytes 4976648 | tf_op jit(solution)/shard_map/ppermute | solution.py:216
  23.2 113.3 %collective-permute-start.1 = (bf16[45,48,384]{2,1,0:T(8,128)(2,1)}, bf16[45,48,384]{2,1,0:T(8,128)(2,1)}, u32[]{:S(2)}, u32[]{:S(2)}) collective-permute-start(bf16[45,48,384]{2,1,0:T(8,128)(2,1)} %get-tuple-element.92), channel_id=1, source_target_pairs={{0,2},{1,3},{2,0},{3,1},{4,6},{5,7},{6,4},{7,5},{8,10},{9,11},{10,... | collective-permute-start | bytes 4976648 | tf_op jit(solution)/shard_map/ppermute | solution.py:216
  25.8 110.8 %collective-permute-start.2 = (bf16[45,48,384]{2,1,0:T(8,128)(2,1)}, bf16[45,48,384]{2,1,0:T(8,128)(2,1)}, u32[]{:S(2)}, u32[]{:S(2)}) collective-permute-start(bf16[45,48,384]{2,1,0:T(8,128)(2,1)} %get-tuple-element.93), channel_id=1, source_target_pairs={{0,3},{1,2},{2,1},{3,0},{4,7},{5,6},{6,5},{7,4},{8,11},{9,10},{10,... | collective-permute-start | bytes 4976648 | tf_op jit(solution)/shard_map/ppermute | solution.py:216
  25.9 109.7 %collective-permute-start.10 = (f32[96,768]{1,0:T(8,128)S(1)}, f32[96,768]{1,0:T(8,128)S(1)}, u32[]{:S(2)}, u32[]{:S(2)}) collective-permute-start(f32[96,768]{1,0:T(8,128)S(1)} %bitcast_select_fusion), channel_id=1, source_target_pairs={{0,1},{1,0},{2,3},{3,2},{4,5},{5,4},{6,7},{7,6},{8,9},{9,8},{10,11... | collective-permute-start | bytes 884744 | tf_op jit(solution)/shard_map/ppermute | solution.py:1008
  136.5 1.2 copy-start.7
  136.6 66.3 %collective-permute-start.6 = (bf16[16,2,96,768]{3,2,1,0:T(8,128)(2,1)}, bf16[16,2,96,768]{3,2,1,0:T(8,128)(2,1)}, u32[]{:S(2)}, u32[]{:S(2)}) collective-permute-start(bf16[16,2,96,768]{3,2,1,0:T(8,128)(2,1)} %bitcast.48), channel_id=1, source_target_pairs={{0,1},{1,0},{2,3},{3,2},{4,5},{5,4},{6,7},{7,6},{8,9},{9,8},{10,11... | collective-permute-start | bytes 14155784 | tf_op jit(solution)/shard_map/ppermute | solution.py:1516
  184.8 73.8 %collective-permute-start.3 = (bf16[45,48,384]{2,1,0:T(8,128)(2,1)}, bf16[45,48,384]{2,1,0:T(8,128)(2,1)S(1)}, u32[]{:S(2)}, u32[]{:S(2)}) collective-permute-start(bf16[45,48,384]{2,1,0:T(8,128)(2,1)} %get-tuple-element.111), channel_id=1, source_target_pairs={{0,1},{1,0},{2,3},{3,2},{4,5},{5,4},{6,7},{7,6},{8,9},{9,8},{10,11... | collective-permute-start | bytes 4976648 | tf_op jit(solution)/shard_map/ppermute | solution.py:216
  185.0 73.6 %collective-permute-start.4 = (bf16[45,48,384]{2,1,0:T(8,128)(2,1)}, bf16[45,48,384]{2,1,0:T(8,128)(2,1)S(1)}, u32[]{:S(2)}, u32[]{:S(2)}) collective-permute-start(bf16[45,48,384]{2,1,0:T(8,128)(2,1)} %get-tuple-element.112), channel_id=1, source_target_pairs={{0,2},{1,3},{2,0},{3,1},{4,6},{5,7},{6,4},{7,5},{8,10},{9,11},{10,... | collective-permute-start | bytes 4976648 | tf_op jit(solution)/shard_map/ppermute | solution.py:216
  186.4 72.3 %collective-permute-start.5 = (bf16[45,48,384]{2,1,0:T(8,128)(2,1)}, bf16[45,48,384]{2,1,0:T(8,128)(2,1)}, u32[]{:S(2)}, u32[]{:S(2)}) collective-permute-start(bf16[45,48,384]{2,1,0:T(8,128)(2,1)} %get-tuple-element.113), channel_id=1, source_target_pairs={{0,3},{1,2},{2,1},{3,0},{4,7},{5,6},{6,5},{7,4},{8,11},{9,10},{10,... | collective-permute-start | bytes 4976648 | tf_op jit(solution)/shard_map/ppermute | solution.py:216
  258.6 1.2 copy-start.10
  258.6 1.7 copy-start.11
  449.2 97.6 %collective-permute-start.7 = (bf16[45,48,384]{2,1,0:T(8,128)(2,1)}, bf16[45,48,384]{2,1,0:T(8,128)(2,1)S(1)}, u32[]{:S(2)}, u32[]{:S(2)}) collective-permute-start(bf16[45,48,384]{2,1,0:T(8,128)(2,1)} %get-tuple-element.123.m1), channel_id=1, source_target_pairs={{0,1},{1,0},{2,3},{3,2},{4,5},{5,4},{6,7},{7,6},{8,9},{9,8},{10,11... | collective-permute-start | bytes 4976648 | tf_op jit(solution)/shard_map/ppermute | solution.py:216
  449.7 97.0 %collective-permute-start.8 = (bf16[45,48,384]{2,1,0:T(8,128)(2,1)}, bf16[45,48,384]{2,1,0:T(8,128)(2,1)S(1)}, u32[]{:S(2)}, u32[]{:S(2)}) collective-permute-start(bf16[45,48,384]{2,1,0:T(8,128)(2,1)} %get-tuple-element.124.m2), channel_id=1, source_target_pairs={{0,2},{1,3},{2,0},{3,1},{4,6},{5,7},{6,4},{7,5},{8,10},{9,11},{10,... | collective-permute-start | bytes 4976648 | tf_op jit(solution)/shard_map/ppermute | solution.py:216
  451.1 95.7 %collective-permute-start.9 = (bf16[45,48,384]{2,1,0:T(8,128)(2,1)}, bf16[45,48,384]{2,1,0:T(8,128)(2,1)}, u32[]{:S(2)}, u32[]{:S(2)}) collective-permute-start(bf16[45,48,384]{2,1,0:T(8,128)(2,1)} %get-tuple-element.125.m3), channel_id=1, source_target_pairs={{0,3},{1,2},{2,1},{3,0},{4,7},{5,6},{6,5},{7,4},{8,11},{9,10},{10,... | collective-permute-start | bytes 4976648 | tf_op jit(solution)/shard_map/ppermute | solution.py:216
  546.7 229.0 %collective-permute-start.15 = (f32[96,768]{1,0:T(8,128)}, f32[96,768]{1,0:T(8,128)}, u32[]{:S(2)}, u32[]{:S(2)}) collective-permute-start(f32[96,768]{1,0:T(8,128)} %slice_select_fusion.2), channel_id=1, source_target_pairs={{0,1},{1,0},{2,3},{3,2},{4,5},{5,4},{6,7},{7,6},{8,9},{9,8},{10,11... | collective-permute-start | bytes 884744 | tf_op jit(solution)/shard_map/ppermute | solution.py:1017
  546.7 30.7 %copy-start.8 = (bf16[45,48,384]{2,1,0:T(8,128)(2,1)}, bf16[45,48,384]{2,1,0:T(8,128)(2,1)S(1)}, u32[]{:S(2)}) copy-start(bf16[45,48,384]{2,1,0:T(8,128)(2,1)S(1)} %collective-permute-done.7.x1) | copy-start | bytes 4976644
  546.8 30.7 %copy-start.9 = (bf16[45,48,384]{2,1,0:T(8,128)(2,1)}, bf16[45,48,384]{2,1,0:T(8,128)(2,1)S(1)}, u32[]{:S(2)}) copy-start(bf16[45,48,384]{2,1,0:T(8,128)(2,1)S(1)} %collective-permute-done.8.x2) | copy-start | bytes 4976644
  704.4 70.4 %copy-start.6 = (f32[4,768]{1,0:T(4,128)S(1)}, f32[4,768]{1,0:T(4,128)}, u32[]{:S(2)}) copy-start(f32[4,768]{1,0:T(4,128)} %get-tuple-element.158) | copy-start | bytes 36868
  704.4 71.2 %copy-start.1 = (f32[192,768]{1,0:T(8,128)S(1)}, f32[192,768]{1,0:T(8,128)}, u32[]{:S(2)}) copy-start(f32[192,768]{1,0:T(8,128)} %get-tuple-element.163) | copy-start | bytes 1769476
  704.5 74.6 %collective-permute-start.11 = (bf16[45,48,384]{2,1,0:T(8,128)(2,1)}, bf16[45,48,384]{2,1,0:T(8,128)(2,1)}, u32[]{:S(2)}, u32[]{:S(2)}) collective-permute-start(bf16[45,48,384]{2,1,0:T(8,128)(2,1)} %get-tuple-element.145), channel_id=1, source_target_pairs={{0,1},{1,0},{2,3},{3,2},{4,5},{5,4},{6,7},{7,6},{8,9},{9,8},{10,11... | collective-permute-start | bytes 4976648 | tf_op jit(solution)/shard_map/ppermute | solution.py:216
  704.9 74.2 %collective-permute-start.12 = (bf16[45,48,384]{2,1,0:T(8,128)(2,1)}, bf16[45,48,384]{2,1,0:T(8,128)(2,1)}, u32[]{:S(2)}, u32[]{:S(2)}) collective-permute-start(bf16[45,48,384]{2,1,0:T(8,128)(2,1)} %get-tuple-element.146), channel_id=1, source_target_pairs={{0,2},{1,3},{2,0},{3,1},{4,6},{5,7},{6,4},{7,5},{8,10},{9,11},{10,... | collective-permute-start | bytes 4976648 | tf_op jit(solution)/shard_map/ppermute | solution.py:216
  705.2 73.9 %collective-permute-start.13 = (bf16[45,48,384]{2,1,0:T(8,128)(2,1)}, bf16[45,48,384]{2,1,0:T(8,128)(2,1)}, u32[]{:S(2)}, u32[]{:S(2)}) collective-permute-start(bf16[45,48,384]{2,1,0:T(8,128)(2,1)} %get-tuple-element.147), channel_id=1, source_target_pairs={{0,3},{1,2},{2,1},{3,0},{4,7},{5,6},{6,5},{7,4},{8,11},{9,10},{10,... | collective-permute-start | bytes 4976648 | tf_op jit(solution)/shard_map/ppermute | solution.py:216
  773.0 4.5 copy-start
  773.0 4.5 copy-start.4
  774.2 4.1 copy-start.5
  774.2 3.3 collective-permute-start.14
Sparse Core Ops, SparseCore 0:
  11.4 103.4 all-gather.2
  546.8 154.1 all-reduce.1
